TPU v7x, 32 devices: a whole 2x2x4 slice. The times are simulated.
32 devices in a mesh: domain: 8 (over y, x, core), band: 4 (over z).
Axes of the slice: x: 2, y: 2, z: 4, core: 2. Of those that a mesh axis runs over, the one named last changes fastest.
Arguments:
- orbitals: float32 [512, 72, 1152], P('band', 'domain'), may hold values from -6 to 6
- potential: float32 [72, 1152], P('domain'), may hold values from -16 to 4
Outputs:
- filtered: float32 [512, 72, 1152], P('band', 'domain')
- proj_ham: float32 [512, 512], P('domain', 'band')
- proj_intersection: float32 [512, 512], P('domain', 'band')
All inputs are finite; a program needn't handle non-finite values.
Results may differ from a plain program's by a relative error of at most 0.0003.
Values may be sent and summed in bfloat16 or wider, within the bound.
No kernel may reach another device: no remote copies, remote signals or barrier semaphores. Data moves between devices by JAX's collectives and lax.ppermute only.
A program may use at most 128 MiB of HBM per device.

v0:
```python
import functools

import jax
import jax.numpy as jnp
from jax import lax
from jax.experimental import pallas as pl
from jax.experimental.pallas import tpu as pltpu
from jax.sharding import PartitionSpec as P

NZ = 144
GROUP = 64
TILE = 16
PAD = 8
CUT = 72
PART = 80
FIRST_B = NZ - PART
VMEM_LIMIT = 40 << 20

coeffs = (-205.0 / 72.0, 8.0 / 5.0, -1.0 / 5.0, 8.0 / 315.0, -1.0 / 560.0)
kinetic = -0.5 / 0.09
center = 68.0
half_width = 48.0
scaled_coeffs = [kinetic * c / half_width for c in coeffs]
carry = [coeffs[k] / coeffs[k + 1] for k in range(1, 4)]

IN_VMEM = pl.BlockSpec(memory_space=pltpu.VMEM)
ANYWHERE = pl.BlockSpec(memory_space=pl.ANY)
IN_SMEM = pl.BlockSpec(memory_space=pltpu.SMEM)


def rounded_planes(planes):
    sent, error = [], None
    for i, plane in enumerate(planes):
        value = plane if error is None else plane + carry[i - 1] * error
        low = value.astype(jnp.bfloat16)
        error = value - low.astype(jnp.float32)
        sent.append(low)
    return sent


def pack_kernel(chunks, field, *refs):
    outs, errors = refs[: 3 * chunks], refs[3 * chunks :]
    step = pl.program_id(0)
    rows = field[0]
    if rows.shape[0] < 128:
        rows = jnp.concatenate([rows, rows], axis=0)
    flipped = rows.T
    half = flipped.shape[0] // 2
    left = lax.broadcasted_iota(jnp.int32, (NZ, 128), 1) < GROUP
    place = lax.rem(step, 4)
    factor = jnp.where(
        place == 0, 0.0, jnp.where(place == 1, carry[0], jnp.where(place == 2, carry[1], carry[2]))
    ).astype(jnp.float32)

    @pl.when(step == 0)
    def _():
        for error in errors:
            error[...] = jnp.zeros_like(error)

    for y in range(half // NZ):
        near = flipped[y * NZ : (y + 1) * NZ]
        far = flipped[half + y * NZ : half + (y + 1) * NZ]
        for c in range(chunks):
            packed, below, above = outs[3 * c : 3 * c + 3]
            if chunks == 1:
                value = jnp.where(left, near, far)
            elif c == 0:
                value = jnp.where(left, near, pltpu.roll(far, GROUP, 1))
            else:
                value = jnp.where(left, pltpu.roll(near, GROUP, 1), far)
            packed[0, y, 0:PAD, :] = jnp.zeros((PAD, 128), jnp.float32)
            packed[0, y, NZ + PAD : NZ + 2 * PAD, :] = jnp.zeros((PAD, 128), jnp.float32)
            packed[0, y, PAD : NZ + PAD, :] = value
            wide = value + factor * errors[c][y]
            low = wide.astype(jnp.bfloat16)
            errors[c][y] = wide - low.astype(jnp.float32)

            @pl.when(step < 4)
            def _():
                below[step, y] = low

            @pl.when(jnp.logical_and(step >= 4, step < 8))
            def _():
                above[7 - step, y] = low


def pack(field, chunks):
    nx, rows, cells = field.shape
    ny = cells // NZ // 2

    def plane(s):
        return jnp.where(s < 4, s, jnp.where(s < 8, nx + 3 - s, s - 4))

    shapes, specs = [], []
    for _ in range(chunks):
        shapes.append(jax.ShapeDtypeStruct((nx, ny, NZ + 2 * PAD, 128), jnp.float32))
        specs.append(pl.BlockSpec((1, ny, NZ + 2 * PAD, 128), lambda s: (plane(s), 0, 0, 0)))
        for _ in range(2):
            shapes.append(jax.ShapeDtypeStruct((4, ny, NZ, 128), jnp.bfloat16))
            specs.append(pl.BlockSpec((4, ny, NZ, 128), lambda s: (0, 0, 0, 0)))
    return pl.pallas_call(
        functools.partial(pack_kernel, chunks),
        grid=(nx,),
        in_specs=[pl.BlockSpec((1, rows, cells), lambda s: (plane(s), 0, 0))],
        out_specs=specs,
        out_shape=shapes,
        scratch_shapes=[pltpu.VMEM((ny, NZ, 128), jnp.float32)] * chunks,
        compiler_params=pltpu.CompilerParams(vmem_limit_bytes=VMEM_LIMIT),
        name="pack",
    )(field)


def unpack_kernel(rows, count, *refs):
    chunks, out = refs[:count], refs[-1]
    ny = chunks[0].shape[1]
    left = lax.broadcasted_iota(jnp.int32, (NZ, 128), 1) < GROUP
    near, far = [], []
    for y in range(ny):
        parts = [chunk[0, y, PAD : NZ + PAD, :] for chunk in chunks]
        if len(parts) == 1:
            near.append(parts[0])
            far.append(pltpu.roll(parts[0], GROUP, 1))
        else:
            near.append(jnp.where(left, parts[0], pltpu.roll(parts[1], GROUP, 1)))
            far.append(jnp.where(left, pltpu.roll(parts[0], GROUP, 1), parts[1]))
    out[0] = jnp.concatenate(near + far, axis=0).T[:rows]


def unpack(chunks, rows, after=()):
    nx, ny, depth, _ = chunks[0].shape
    cells = 2 * ny * NZ
    return pl.pallas_call(
        functools.partial(unpack_kernel, rows, len(chunks)),
        grid=(nx,),
        in_specs=[pl.BlockSpec((1, ny, depth, 128), lambda s: (s, 0, 0, 0))] * len(chunks)
        + [ANYWHERE] * len(after),
        out_specs=pl.BlockSpec((1, rows, cells), lambda s: (s, 0, 0)),
        out_shape=jax.ShapeDtypeStruct((nx, rows, cells), jnp.float32),
        compiler_params=pltpu.CompilerParams(vmem_limit_bytes=VMEM_LIMIT),
        name="unpack",
    )(*chunks, *after)


def apply_kernel(mode, *refs):
    refs = list(refs)
    lower = refs.pop(0) if mode == "image" else None
    cur = refs.pop(0)
    prev = refs.pop(0) if mode in ("middle", "last") else None
    below, above, pot = refs.pop(0), refs.pop(0), refs.pop(0)
    nx, ny = cur.shape[:2]
    left = lax.broadcasted_iota(jnp.int32, (TILE, 128), 1) < GROUP
    if mode == "image":
        part_a, part_b, part_w = refs
    else:
        new, out_below, out_above = refs[:3]
        zero = jnp.zeros((PAD, 128), jnp.float32)
        for x in range(nx):
            for y in range(ny):
                new[x, y, 0:PAD, :] = zero
                new[x, y, NZ + PAD : NZ + 2 * PAD, :] = zero

    def body(t, in_a, in_b):
        z = pl.multiple_of(t * TILE, TILE)
        in_cut = lax.broadcasted_iota(jnp.int32, (TILE, 128), 0) + FIRST_B >= CUT

        def plane(x, y):
            if x < 0:
                return below[4 + x, y, pl.ds(z, TILE), :].astype(jnp.float32)
            if x >= nx:
                return above[x - nx, y, pl.ds(z, TILE), :].astype(jnp.float32)
            return cur[x, y, pl.ds(z + PAD, TILE), :]

        results = []
        for x in range(nx):
            mine = [plane(x, y) for y in range(ny)]
            other = [pltpu.roll(a, GROUP, 1) for a in mine]
            after = [jnp.where(left, a, 0.0) for a in other]
            before = [jnp.where(left, 0.0, a) for a in other]
            row = []
            for y in range(ny):
                total = pot[x, y, pl.ds(z, TILE), :] * mine[y]
                both = in_a and in_b and mode == "image"
                strip = jnp.zeros_like(total) if both else None
                for k in range(1, 5):
                    pairs = plane(x - k, y) + plane(x + k, y)
                    if k == ny:
                        pairs = pairs + other[y]
                    else:
                        up = mine[y + k] if y + k < ny else after[y + k - ny]
                        down = mine[y - k] if y >= k else before[y - k + ny]
                        pairs = pairs + (up + down)
                    forth = cur[x, y, pl.ds(z + PAD + k, TILE), :]
                    back = cur[x, y, pl.ds(z + PAD - k, TILE), :]
                    if both:
                        depth = lax.broadcasted_iota(jnp.int32, (TILE, 128), 0) + FIRST_B
                        cut = jnp.where(in_cut, pairs, 0.0) + jnp.where(depth + k >= CUT, forth, 0.0)
                        cut = cut + jnp.where(depth - k >= CUT, back, 0.0)
                        strip = strip + scaled_coeffs[k] * cut
                        if k == 1:
                            strip = strip + jnp.where(in_cut, total, 0.0)
                    pairs = pairs + (forth + back)
                    total = total + scaled_coeffs[k] * pairs
                if mode == "image":
                    low = mine[y].astype(jnp.bfloat16)
                    image = total.astype(jnp.bfloat16)
                    if both:
                        none = jnp.zeros_like(low)
                        keep_b = in_cut.astype(jnp.float32).astype(jnp.bfloat16)
                        keep_a = 1.0 - keep_b
                        part_a[x, y, pl.ds(z, TILE), 0:128] = image * keep_a
                        part_a[x, y, pl.ds(z, TILE), 128:256] = low * keep_a
                        part_b[x, y, 0:TILE, 0:128] = image * keep_b
                        part_b[x, y, 0:TILE, 128:256] = low * keep_b
                        whole = jnp.where(in_cut, total, 0.0)
                        chosen = jnp.where(lower[0] > 0, strip, whole).astype(jnp.bfloat16)
                        part_w[x, y, 0:TILE, 0:128] = chosen
                        part_w[x, y, 0:TILE, 128:256] = low * keep_b
                    elif in_a:
                        part_a[x, y, pl.ds(z, TILE), 0:128] = image
                        part_a[x, y, pl.ds(z, TILE), 128:256] = low
                    else:
                        for part in (part_b, part_w):
                            part[x, y, pl.ds(z - FIRST_B, TILE), 0:128] = image
                            part[x, y, pl.ds(z - FIRST_B, TILE), 128:256] = low
                    continue
                if prev is not None:
                    total = (total + total) - prev[x, y, pl.ds(z + PAD, TILE), :]
                new[x, y, pl.ds(z + PAD, TILE), :] = total
                if mode == "last":
                    low = total.astype(jnp.bfloat16)
                    if in_a:
                        refs[3][x, y, pl.ds(z, TILE), :] = low
                    if in_b:
                        refs[4][x, y, pl.ds(z - FIRST_B, TILE), :] = low
                row.append(total)
            results.append(row)
        if mode == "image":
            return
        for y in range(ny):
            for i, low in enumerate(rounded_planes([results[i][y] for i in range(4)])):
                out_below[i, y, pl.ds(z, TILE), :] = low
            for i, low in enumerate(rounded_planes([results[nx - 1 - i][y] for i in range(4)])):
                out_above[3 - i, y, pl.ds(z, TILE), :] = low

    def loop(start, stop, in_a, in_b):
        def step(t, _):
            body(t, in_a, in_b)
            return 0

        lax.fori_loop(start, stop, step, 0)

    if mode in ("first", "middle"):
        loop(0, NZ // TILE, False, False)
    else:
        loop(0, FIRST_B // TILE, True, False)
        loop(FIRST_B // TILE, PART // TILE, True, True)
        loop(PART // TILE, NZ // TILE, False, True)


def apply_op(mode, cur, prev, below, above, pot, lower=None):
    nx, ny = cur.shape[:2]
    edge = jax.ShapeDtypeStruct((4, ny, NZ, 128), jnp.bfloat16)
    part = jax.ShapeDtypeStruct((nx, ny, PART, 128), jnp.bfloat16)
    wide = jax.ShapeDtypeStruct((nx, ny, PART, 256), jnp.bfloat16)
    shapes = [jax.ShapeDtypeStruct(cur.shape, cur.dtype), edge, edge]
    if mode == "last":
        shapes = shapes + [part, part]
    if mode == "image":
        shapes = [wide, wide, wide]
    args = [cur] + ([prev] if prev is not None else []) + [below, above, pot]
    specs = [IN_VMEM] * len(args)
    if mode == "image":
        args, specs = [lower] + args, [IN_SMEM] + specs
    return pl.pallas_call(
        functools.partial(apply_kernel, mode),
        in_specs=specs,
        out_specs=[IN_VMEM] * len(shapes),
        out_shape=shapes,
        compiler_params=pltpu.CompilerParams(vmem_limit_bytes=VMEM_LIMIT),
        cost_estimate=pl.CostEstimate(
            flops=30 * cur.size, bytes_accessed=4 * cur.size, transcendentals=0
        ),
        name="apply_" + mode,
    )(*args)


def exchange(below, above):
    count = lax.axis_size("domain")
    up = [(i, i + 1) for i in range(count - 1)]
    down = [(i + 1, i) for i in range(count - 1)]
    return lax.ppermute(above, "domain", up), lax.ppermute(below, "domain", down)


def gram_kernel(kinds, chunks, has_sums, *refs):
    plan, refs = refs[0], refs[1:]
    blocks, refs = refs[: len(kinds)], refs[len(kinds) :]
    rights, refs = refs[: 3 * chunks], refs[3 * chunks :]
    sums = refs[0] if has_sums else None
    out, full = refs[-2], refs[-1]
    left = lax.broadcasted_iota(jnp.int32, (GROUP, 128), 1) < GROUP
    out[...] = sums[...] if has_sums else jnp.zeros_like(out)
    depth = blocks[0].shape[0]
    part = depth // 3

    def one(block, kind, slot):
        full[...] = jnp.zeros_like(full)

        def step(i, _):
            rows = pl.ds(pl.multiple_of(i * part, 16), part)
            for c in range(chunks):
                full[c] += lax.dot_general(
                    block[rows, :],
                    rights[3 * c + kind][rows, :],
                    (((0,), (0,)), ((), ())),
                    preferred_element_type=jnp.float32,
                )
            return 0

        lax.fori_loop(0, 3, step, 0)
        for m in range(2):
            lanes = slice(128 * m, 128 * (m + 1))
            value = full[0, 0:GROUP, lanes] + pltpu.roll(full[0, GROUP:128, lanes], GROUP, 1)
            if chunks == 2:
                second = pltpu.roll(full[1, 0:GROUP, lanes], GROUP, 1) + full[1, GROUP:128, lanes]
                value = jnp.where(left, value, second)
            out[m, slot] += value

    for i, choices in enumerate(kinds):
        for kind in choices:

            @pl.when(plan[2 * i] == kind)
            def _():
                one(blocks[i], kind, plan[2 * i + 1])


def gram(blocks, kinds, plan, rights, sums, bands, after=()):
    chunks = len(rights)
    flat = [block.reshape(-1, 128) for block in blocks]
    flat = flat + [part.reshape(-1, 256) for three in rights for part in three]
    if sums is not None:
        flat.append(sums)
    shape = (2, bands, GROUP, 128)
    kernel = functools.partial(gram_kernel, kinds, chunks, sums is not None)
    return pl.pallas_call(
        lambda plan, *refs: kernel(plan, *refs[: len(flat)], *refs[len(flat) + len(after) :]),
        in_specs=[IN_SMEM] + [IN_VMEM] * len(flat) + [ANYWHERE] * len(after),
        out_specs=IN_VMEM,
        out_shape=jax.ShapeDtypeStruct(shape, jnp.float32),
        scratch_shapes=[pltpu.VMEM((chunks, 128, 256), jnp.float32)],
        compiler_params=pltpu.CompilerParams(vmem_limit_bytes=VMEM_LIMIT),
        name="gram",
    )(plan, *flat, *after)


def hops(low_a, low_b):
    bands = lax.axis_size("band")
    band = lax.axis_index("band")
    mid = bands // 2
    up, down = low_a, low_b
    ups, downs = [], []
    for hop in range(1, bands):
        pairs = [b for b in range(hop, bands) if b - hop < mid]
        if hop >= mid:
            pairs = pairs + list(range(hop - mid + 1, mid))
        if hop == mid and mid > 1:
            up = jnp.where(band < mid - 1, low_b, up)
            down = jnp.where(band > bands - mid, low_a, down)
        up = lax.ppermute(up, "band", [(b - 1, b) for b in pairs])
        down = lax.ppermute(down, "band", [(bands - b, bands - 1 - b) for b in pairs])
        ups.append(up)
        downs.append(down)
    return ups, downs


def hop_plan(hop, bands, band):
    mid = bands // 2
    late = hop - mid + 1
    skip = 3

    def one(place, main, other, sign):
        is_main = jnp.logical_and(place >= hop, place - hop < mid)
        is_late = jnp.logical_and(hop >= mid, jnp.logical_and(place >= late, place < mid))
        kind = jnp.where(is_main, main, jnp.where(is_late, other, skip))
        slot = band - sign * jnp.where(is_main, hop, jnp.where(is_late, late, 0))
        return [kind, slot]

    return one(band, 0, 1, 1) + one(bands - 1 - band, 2, 0, -1)


def summed_over_domain(table):
    count = lax.axis_size("domain")
    me = lax.axis_index("domain")
    bit = 1
    table = table.reshape(2, count, table.shape[1] // count, table.shape[2])
    while bit < count:
        groups = table.reshape((2, table.shape[1] // 2, 2) + table.shape[2:])
        mine = lax.rem(me // bit, 2)
        keep = lax.dynamic_index_in_dim(groups, mine, axis=2, keepdims=False)
        send = lax.dynamic_index_in_dim(groups, 1 - mine, axis=2, keepdims=False)
        table = keep + lax.ppermute(send, "domain", [(i, i ^ bit) for i in range(count)])
        bit *= 2
    return table[:, 0]


def other_triangle(table):
    bands, count = lax.axis_size("band"), lax.axis_size("domain")
    d, b = lax.axis_index("domain"), lax.axis_index("band")
    ratio = count // bands
    rows = table.shape[1]
    place = lax.rem(d, ratio)
    pieces = []
    for shift in range(ratio):
        to = lax.rem(place + shift, ratio)
        block = lax.dynamic_slice_in_dim(table, to * rows, rows, axis=2)
        pairs = []
        for i in range(count):
            for j in range(bands):
                target = ratio * j + (i % ratio + shift) % ratio
                pairs.append((i * bands + j, target * bands + i // ratio))
        pieces.append(lax.ppermute(block, ("domain", "band"), pairs).transpose(0, 2, 1))
    ordered = [
        lax.dynamic_index_in_dim(
            jnp.stack(pieces), lax.rem(place - t + ratio, ratio), axis=0, keepdims=False
        )
        for t in range(ratio)
    ]
    out = jnp.concatenate(ordered, axis=2)
    return jnp.where(d // ratio == b, 0.0, out)


def pot_kernel(diagonal, out):
    row = diagonal[0]
    half = row.shape[1] // 2
    wide = -(-half // 128) * 128
    first = lax.broadcasted_iota(jnp.int32, (128, wide), 0) < GROUP
    near = jnp.broadcast_to(row[:, :wide], (128, wide))
    far = jnp.broadcast_to(pltpu.roll(row, half, 1)[:, :wide], (128, wide))
    flipped = jnp.where(first, near, far).T
    for y in range(out.shape[1]):
        out[0, y] = flipped[y * NZ : (y + 1) * NZ]


def spread(diagonal):
    nx, cells = diagonal.shape
    ny = cells // NZ // 2
    return pl.pallas_call(
        pot_kernel,
        grid=(nx,),
        in_specs=[pl.BlockSpec((1, 1, cells), lambda s: (s, 0, 0))],
        out_specs=pl.BlockSpec((1, ny, NZ, 128), lambda s: (s, 0, 0, 0)),
        out_shape=jax.ShapeDtypeStruct((nx, ny, NZ, 128), jnp.float32),
        name="spread",
    )(diagonal.reshape(nx, 1, cells))


def shards(orbitals, potential):
    own, nx, cells = orbitals.shape
    chunks = own // GROUP
    bands = lax.axis_size("band")
    total_cells = lax.axis_size("domain") * potential.size

    pot = spread((3.0 * kinetic * coeffs[0] + potential - center) / half_width)

    packed = pack(orbitals.transpose(1, 0, 2), chunks)
    cur = [packed[3 * c] for c in range(chunks)]
    edges = [(packed[3 * c + 1], packed[3 * c + 2]) for c in range(chunks)]
    prev = [None] * chunks
    lows = [None] * chunks
    for step in range(4):
        mode = "first" if step == 0 else ("last" if step == 3 else "middle")
        for c in range(chunks):
            below, above = exchange(*edges[c])
            out = apply_op(mode, cur[c], prev[c], below, above, pot)
            prev[c], cur[c], edges[c] = cur[c], out[0], (out[1], out[2])
            lows[c] = out[3:]
    band = lax.axis_index("band")
    lower = (band < bands // 2).astype(jnp.int32).reshape(1)
    moved = [hops(*lows[c]) for c in range(chunks)]
    rights = []
    for c in range(chunks):
        below, above = exchange(*edges[c])
        rights.append(apply_op("image", cur[c], None, below, above, pot, lower))
    filtered = unpack(cur, own, after=[rights[-1][0]])

    own_plan = [jnp.int32(0), band, jnp.int32(1), band]
    plans = [hop_plan(hop, bands, band) for hop in range(1, bands)]
    kinds = [((0,), (2,)) if hop < bands // 2 else ((0, 1), (2, 0)) for hop in range(1, bands)]
    tables = []
    for c in range(chunks):
        ups, downs = moved[c]
        blocks = list(lows[c])
        plan, choice = list(own_plan), [(0,), (1,)]
        sums = None
        for i in range(bands - 1):
            blocks += [ups[i], downs[i]]
            plan += plans[i]
            choice += kinds[i]
            if i == bands - 2 or (c == chunks - 1 and i == bands - 3):
                rows = jnp.stack(plan).astype(jnp.int32)
                sums = gram(blocks, tuple(choice), rows, rights, sums, bands)
                blocks, plan, choice = [], [], []
        tables.append(sums)
    table = jnp.stack(tables, axis=2).reshape(2, bands * own, 128)[:, :, :own]
    table = summed_over_domain(table)
    table = (table + other_triangle(table)) / total_cells
    return (filtered.transpose(1, 0, 2), table[0], table[1])


def solution(mesh):
    placed = (P("band", "domain", None), P("domain", None))
    return jax.shard_map(
        shards,
        mesh=mesh,
        in_specs=placed,
        out_specs=(P("band", "domain", None), P("domain", "band"), P("domain", "band")),
        check_vma=False,
    )
```

profile of v0, /device:TPU:3, one launch (start us, length us, event | category | flops | bytes accessed | tf_op | source)
XLA Modules:
  0.0 271.4 jit_solution(15740904321593854467)
XLA Ops:
  0.6 2.5 copy-done.23
  3.1 10.3 %pack.1 = (f32[9,4,160,128]{3,2,1,0:T(8,128)S(1)}, bf16[4,4,144,128]{3,2,1,0:T(8,128)(2,1)}, bf16[4,4,144,128]{3,2,1,0:T(8,128)(2,1)}, f32[9,4,160,128]{3,2,1,0:...) custom-call(f32[9,128,1152]{2,1,0:T(8,128)S(1)} %bitcast.87), custom_call_target="tpu_custom_call" | custom-call | tf_op jit(solution)/shard_map/pack/pallas_call | solution.py:101
  13.4 1.6 copy-done.7
  15.0 3.7 %collective-permute-start.8 = (bf16[4,4,144,128]{3,2,1,0:T(8,128)(2,1)}, bf16[4,4,144,128]{3,2,1,0:T(8,128)(2,1)}, u32[]{:S(2)}, u32[]{:S(2)}) collective-permute-start(bf16[4,4,144,128]{3,2,1,0:T(8,128)(2,1)} %get-tuple-element.57), channel_id=1, source_target_pairs={{0,4},{4,8},{8,12},{12,16},{16,20},{20,24},{24,28},{1,5},{5,9},{9,... | collective-permute-start | bytes 1769480 | tf_op jit(solution)/shard_map/ppermute | solution.py:291
  18.7 1.9 collective-permute-start.9
  20.6 4.5 %collective-permute-start = (bf16[4,4,144,128]{3,2,1,0:T(8,128)(2,1)}, bf16[4,4,144,128]{3,2,1,0:T(8,128)(2,1)S(1)}, u32[]{:S(2)}, u32[]{:S(2)}) collective-permute-start(bf16[4,4,144,128]{3,2,1,0:T(8,128)(2,1)} %get-tuple-element.44), channel_id=1, source_target_pairs={{0,4},{4,8},{8,12},{12,16},{16,20},{20,24},{24,28},{1,5},{5,9},{9,... | collective-permute-start | bytes 1769480 | tf_op jit(solution)/shard_map/ppermute | solution.py:291
  25.2 1.9 collective-permute-start.1
  27.8 5.8 %spread.1.refs_3_.refs_4_ = f32[9,4,144,128]{3,2,1,0:T(8,128)} custom-call(f32[9,1,1152]{2,1,0:T(1,128)} %reshape.102.diagonal), custom_call_target="tpu_custom_call" | custom-call | tf_op jit(solution)/shard_map/spread/pallas_call | solution.py:446
  33.6 3.9 %collective-permute-done.9.refs_2_ = bf16[4,4,144,128]{3,2,1,0:T(8,128)(2,1)} collective-permute-done((bf16[4,4,144,128]{3,2,1,0:T(8,128)(2,1)}, bf16[4,4,144,128]{3,2,1,0:T(8,128)(2,1)}, u32[]{:S(2)}, u32[]{:S(2)}) %collective-permute-start.9) | collective-permute-done | bytes 589856 | tf_op jit(solution)/shard_map/ppermute | solution.py:291
  37.5 1.7 copy-done
  39.3 1.8 copy-done.8
  41.1 5.5 %apply_first.3 = (f32[9,4,160,128]{3,2,1,0:T(8,128)S(1)}, bf16[4,4,144,128]{3,2,1,0:T(8,128)(2,1)S(1)}, bf16[4,4,144,128]{3,2,1,0:T(8,128)(2,1)S(1)}) custom-call(f32[9,4,160,128]{3,2,1,0:T(8,128)S(1)} %copy-done.8, bf16[4,4,144,128]{3,2,1,0:T(8,128)(2,1)} %collective-permute-done.8.refs_1_, bf16[4,4,144,128]{3,2,1,0:T(8,128)(2,1)} %collective-permute-done.9.refs_2_, ...), custom_call_target="tpu_custom_call" | custom-call | flops 22118400 | bytes 2949120 | tf_op jit(solution)/shard_map/apply_first/pallas_call | solution.py:274
  46.6 1.9 collective-permute-start.10
  48.5 2.4 collective-permute-start.11
  51.0 5.3 %apply_first.2 = (f32[9,4,160,128]{3,2,1,0:T(8,128)S(1)}, bf16[4,4,144,128]{3,2,1,0:T(8,128)(2,1)S(1)}, bf16[4,4,144,128]{3,2,1,0:T(8,128)(2,1)S(1)}) custom-call(f32[9,4,160,128]{3,2,1,0:T(8,128)S(1)} %get-tuple-element.43.refs_0_.refs_1_, bf16[4,4,144,128]{3,2,1,0:T(8,128)(2,1)S(1)} %collective-permute-done.refs_1_, ...), custom_call_target="tpu_custom_call" | custom-call | flops 22118400 | bytes 2949120 | tf_op jit(solution)/shard_map/apply_first/pallas_call | solution.py:274
  56.3 1.6 copy-done.18
  57.9 4.0 %collective-permute-start.2 = (bf16[4,4,144,128]{3,2,1,0:T(8,128)(2,1)S(1)}, bf16[4,4,144,128]{3,2,1,0:T(8,128)(2,1)S(1)}, u32[]{:S(2)}, u32[]{:S(2)}) collective-permute-start(bf16[4,4,144,128]{3,2,1,0:T(8,128)(2,1)S(1)} %get-tuple-element.47), channel_id=1, source_target_pairs={{0,4},{4,8},{8,12},{12,16},{16,20},{20,24},{24,28},{1,5},{5,9},{9,... | collective-permute-start | bytes 1769480 | tf_op jit(solution)/shard_map/ppermute | solution.py:291
  61.9 1.9 collective-permute-start.3
  63.9 4.3 %apply_middle.6 = (f32[9,4,160,128]{3,2,1,0:T(8,128)S(1)}, bf16[4,4,144,128]{3,2,1,0:T(8,128)(2,1)S(1)}, bf16[4,4,144,128]{3,2,1,0:T(8,128)(2,1)S(1)}) custom-call(f32[9,4,160,128]{3,2,1,0:T(8,128)S(1)} %get-tuple-element.59.refs_0_.refs_1_, f32[9,4,160,128]{3,2,1,0:T(8,128)S(1)} %copy-done.8, bf16[4,4,144,128]{3,2,1,0:T(8,128)(2,1)S(1)} %collective-permute-done.10.refs_2_, ...), custom_call_target="tpu_custom_call" | custom-call | flops 22118400 | bytes 2949120 | tf_op jit(solution)/shard_map/apply_middle/pallas_call | solution.py:274
  68.2 4.5 %collective-permute-start.12 = (bf16[4,4,144,128]{3,2,1,0:T(8,128)(2,1)S(1)}, bf16[4,4,144,128]{3,2,1,0:T(8,128)(2,1)S(1)}, u32[]{:S(2)}, u32[]{:S(2)}) collective-permute-start(bf16[4,4,144,128]{3,2,1,0:T(8,128)(2,1)S(1)} %get-tuple-element.63), channel_id=1, source_target_pairs={{0,4},{4,8},{8,12},{12,16},{16,20},{20,24},{24,28},{1,5},{5,9},{9,... | collective-permute-start | bytes 1769480 | tf_op jit(solution)/shard_map/ppermute | solution.py:291
  72.8 1.9 collective-permute-start.13
  74.7 2.1 collective-permute-done.3.refs_3_
  76.8 1.8 copy-done.19
  78.7 4.3 %apply_middle.4 = (f32[9,4,160,128]{3,2,1,0:T(8,128)S(1)}, bf16[4,4,144,128]{3,2,1,0:T(8,128)(2,1)S(1)}, bf16[4,4,144,128]{3,2,1,0:T(8,128)(2,1)S(1)}) custom-call(f32[9,4,160,128]{3,2,1,0:T(8,128)S(1)} %copy-done.19, f32[9,4,160,128]{3,2,1,0:T(8,128)S(1)} %copy-done.6, bf16[4,4,144,128]{3,2,1,0:T(8,128)(2,1)S(1)} %collective-permute-done.2.refs_2_, ...), custom_call_target="tpu_custom_call" | custom-call | flops 22118400 | bytes 2949120 | tf_op jit(solution)/shard_map/apply_middle/pallas_call | solution.py:274
  83.0 2.5 collective-permute-start.4
  85.4 1.9 collective-permute-start.5
  87.4 2.0 collective-permute-done.13.refs_3_
  89.4 1.8 copy-done.17
  91.3 1.8 copy-done.22
  93.1 4.3 %apply_middle.7 = (f32[9,4,160,128]{3,2,1,0:T(8,128)S(1)}, bf16[4,4,144,128]{3,2,1,0:T(8,128)(2,1)S(1)}, bf16[4,4,144,128]{3,2,1,0:T(8,128)(2,1)S(1)}) custom-call(f32[9,4,160,128]{3,2,1,0:T(8,128)S(1)} %copy-done.17, f32[9,4,160,128]{3,2,1,0:T(8,128)S(1)} %copy-done.22, bf16[4,4,144,128]{3,2,1,0:T(8,128)(2,1)S(1)} %collective-permute-done.12.refs_2_, ...), custom_call_target="tpu_custom_call" | custom-call | flops 22118400 | bytes 2949120 | tf_op jit(solution)/shard_map/apply_middle/pallas_call | solution.py:274
  97.4 1.6 copy-done.26
  99.0 2.5 collective-permute-start.14
  101.5 1.9 collective-permute-start.15
  103.5 4.3 %apply_middle.5 = (f32[9,4,160,128]{3,2,1,0:T(8,128)S(1)}, bf16[4,4,144,128]{3,2,1,0:T(8,128)(2,1)S(1)}, bf16[4,4,144,128]{3,2,1,0:T(8,128)(2,1)S(1)}) custom-call(f32[9,4,160,128]{3,2,1,0:T(8,128)S(1)} %get-tuple-element.49.refs_0_.refs_1_, f32[9,4,160,128]{3,2,1,0:T(8,128)S(1)} %copy-done.20, bf16[4,4,144,128]{3,2,1,0:T(8,128)(2,1)S(1)} %collective-permute-done.4.refs_2_, ...), custom_call_target="tpu_custom_call" | custom-call | flops 22118400 | bytes 2949120 | tf_op jit(solution)/shard_map/apply_middle/pallas_call | solution.py:274
  107.8 1.6 copy-done.24
  109.4 4.5 %collective-permute-start.6 = (bf16[4,4,144,128]{3,2,1,0:T(8,128)(2,1)S(1)}, bf16[4,4,144,128]{3,2,1,0:T(8,128)(2,1)S(1)}, u32[]{:S(2)}, u32[]{:S(2)}) collective-permute-start(bf16[4,4,144,128]{3,2,1,0:T(8,128)(2,1)S(1)} %get-tuple-element.53), channel_id=1, source_target_pairs={{0,4},{4,8},{8,12},{12,16},{16,20},{20,24},{24,28},{1,5},{5,9},{9,... | collective-permute-start | bytes 1769480 | tf_op jit(solution)/shard_map/ppermute | solution.py:291
  113.9 1.9 collective-permute-start.7
  115.9 7.5 %apply_last.3 = (f32[9,4,160,128]{3,2,1,0:T(8,128)S(1)}, bf16[4,4,144,128]{3,2,1,0:T(8,128)(2,1)}, bf16[4,4,144,128]{3,2,1,0:T(8,128)(2,1)S(1)}, bf16[9,4,80,128...) custom-call(f32[9,4,160,128]{3,2,1,0:T(8,128)S(1)} %copy-done.27, f32[9,4,160,128]{3,2,1,0:T(8,128)} %copy-done.16, ...), custom_call_target="tpu_custom_call" | custom-call | flops 22118400 | bytes 2949120 | tf_op jit(solution)/shard_map/apply_last/pallas_call | solution.py:274
  123.4 1.6 copy-done.9
  126.5 3.8 %collective-permute-start.26 = (bf16[9,4,80,128]{3,2,1,0:T(8,128)(2,1)S(1)}, bf16[9,4,80,128]{3,2,1,0:T(8,128)(2,1)}, u32[]{:S(2)}, u32[]{:S(2)}) collective-permute-start(bf16[9,4,80,128]{3,2,1,0:T(8,128)(2,1)S(1)} %get-tuple-element.82), channel_id=1, source_target_pairs={{0,1},{1,2},{4,5},{5,6},{8,9},{9,10},{12,13},{13,14},{16,17},{17,1... | collective-permute-start | bytes 2211848 | tf_op jit(solution)/shard_map/ppermute | solution.py:368
  130.4 7.1 %apply_last.2 = (f32[9,4,160,128]{3,2,1,0:T(8,128)S(1)}, bf16[4,4,144,128]{3,2,1,0:T(8,128)(2,1)S(1)}, bf16[4,4,144,128]{3,2,1,0:T(8,128)(2,1)S(1)}, bf16[9,4,80...) custom-call(f32[9,4,160,128]{3,2,1,0:T(8,128)S(1)} %copy-done.25, f32[9,4,160,128]{3,2,1,0:T(8,128)} %copy-done.15, ...), custom_call_target="tpu_custom_call" | custom-call | flops 22118400 | bytes 2949120 | tf_op jit(solution)/shard_map/apply_last/pallas_call | solution.py:274
  137.4 1.6 copy-done.12
  141.6 4.1 %collective-permute-start.18 = (bf16[9,4,80,128]{3,2,1,0:T(8,128)(2,1)}, bf16[9,4,80,128]{3,2,1,0:T(8,128)(2,1)}, u32[]{:S(2)}, u32[]{:S(2)}) collective-permute-start(bf16[9,4,80,128]{3,2,1,0:T(8,128)(2,1)} %get-tuple-element.72), channel_id=1, source_target_pairs={{0,1},{1,2},{4,5},{5,6},{8,9},{9,10},{12,13},{13,14},{16,17},{17,1... | collective-permute-start | bytes 2211848 | tf_op jit(solution)/shard_map/ppermute | solution.py:368
  145.7 5.5 %collective-permute-start.24 = (bf16[4,4,144,128]{3,2,1,0:T(8,128)(2,1)}, bf16[4,4,144,128]{3,2,1,0:T(8,128)(2,1)S(1)}, u32[]{:S(2)}, u32[]{:S(2)}) collective-permute-start(bf16[4,4,144,128]{3,2,1,0:T(8,128)(2,1)} %copy-done.42), channel_id=1, source_target_pairs={{0,4},{4,8},{8,12},{12,16},{16,20},{20,24},{24,28},{1,5},{5,9},{9,... | collective-permute-start | bytes 1769480 | tf_op jit(solution)/shard_map/ppermute | solution.py:291
  151.3 1.9 collective-permute-start.25
  157.8 2.3 collective-permute-done.18
  160.1 5.0 %collective-permute-start.27 = (bf16[9,4,80,128]{3,2,1,0:T(8,128)(2,1)S(1)}, bf16[9,4,80,128]{3,2,1,0:T(8,128)(2,1)}, u32[]{:S(2)}, u32[]{:S(2)}) collective-permute-start(bf16[9,4,80,128]{3,2,1,0:T(8,128)(2,1)S(1)} %broadcast_select_fusion.2), channel_id=1, source_target_pairs={{1,2},{2,3},{0,1},{5,6},{6,7},{4,5},{9,10},{10,11},{8,9},{13,14},{... | collective-permute-start | bytes 2211848 | tf_op jit(solution)/shard_map/ppermute | solution.py:368
  165.2 10.0 %collective-permute-start.20 = (bf16[9,4,80,128]{3,2,1,0:T(8,128)(2,1)S(1)}, bf16[9,4,80,128]{3,2,1,0:T(8,128)(2,1)}, u32[]{:S(2)}, u32[]{:S(2)}) collective-permute-start(bf16[9,4,80,128]{3,2,1,0:T(8,128)(2,1)S(1)} %broadcast_select_fusion.3), channel_id=1, source_target_pairs={{1,2},{2,3},{0,1},{5,6},{6,7},{4,5},{9,10},{10,11},{8,9},{13,14},{... | collective-permute-start | bytes 2211848 | tf_op jit(solution)/shard_map/ppermute | solution.py:368
  179.1 5.9 %collective-permute-start.16 = (bf16[4,4,144,128]{3,2,1,0:T(8,128)(2,1)S(1)}, bf16[4,4,144,128]{3,2,1,0:T(8,128)(2,1)S(1)}, u32[]{:S(2)}, u32[]{:S(2)}) collective-permute-start(bf16[4,4,144,128]{3,2,1,0:T(8,128)(2,1)S(1)} %copy-done.40), channel_id=1, source_target_pairs={{0,4},{4,8},{8,12},{12,16},{16,20},{20,24},{24,28},{1,5},{5,9},{9,... | collective-permute-start | bytes 1769480 | tf_op jit(solution)/shard_map/ppermute | solution.py:291
  187.9 5.8 %collective-permute-done.20 = bf16[9,4,80,128]{3,2,1,0:T(8,128)(2,1)} collective-permute-done((bf16[9,4,80,128]{3,2,1,0:T(8,128)(2,1)S(1)}, bf16[9,4,80,128]{3,2,1,0:T(8,128)(2,1)}, u32[]{:S(2)}, u32[]{:S(2)}) %collective-permute-start.20) | collective-permute-done | bytes 737312 | tf_op jit(solution)/shard_map/ppermute | solution.py:368
  197.9 5.9 %collective-permute-start.17 = (bf16[4,4,144,128]{3,2,1,0:T(8,128)(2,1)}, bf16[4,4,144,128]{3,2,1,0:T(8,128)(2,1)}, u32[]{:S(2)}, u32[]{:S(2)}) collective-permute-start(bf16[4,4,144,128]{3,2,1,0:T(8,128)(2,1)} %get-tuple-element.70), channel_id=1, source_target_pairs={{4,0},{8,4},{12,8},{16,12},{20,16},{24,20},{28,24},{5,1},{9,5},{13... | collective-permute-start | bytes 1769480 | tf_op jit(solution)/shard_map/ppermute | solution.py:291
  204.2 1.8 copy-done.13
  208.2 4.2 %apply_image.3 = (bf16[9,4,80,256]{3,2,1,0:T(8,128)(2,1)S(1)}, bf16[9,4,80,256]{3,2,1,0:T(8,128)(2,1)S(1)}, bf16[9,4,80,256]{3,2,1,0:T(8,128)(2,1)S(1)}) custom-call(s32[1]{0:T(128)} %bitcast.1.refs_0_, f32[9,4,160,128]{3,2,1,0:T(8,128)S(1)} %copy-done.13, bf16[4,4,144,128]{3,2,1,0:T(8,128)(2,1)S(1)} %copy-done.34, bf16[4,4,144,128]{3,2,1,0:T(8,128)(2,1)S(1)} %copy-done.36, ...), custom_call_target="tpu_custom_call" | custom-call | flops 22118400 | bytes 2949120 | tf_op jit(solution)/shard_map/apply_image/pallas_call | solution.py:274
  213.4 5.6 %apply_image.2 = (bf16[9,4,80,256]{3,2,1,0:T(8,128)(2,1)S(1)}, bf16[9,4,80,256]{3,2,1,0:T(8,128)(2,1)S(1)}, bf16[9,4,80,256]{3,2,1,0:T(8,128)(2,1)S(1)}) custom-call(s32[1]{0:T(128)} %bitcast.1.refs_0_, f32[9,4,160,128]{3,2,1,0:T(8,128)S(1)} %copy-done.10, bf16[4,4,144,128]{3,2,1,0:T(8,128)(2,1)S(1)} %copy-done.38, ...), custom_call_target="tpu_custom_call" | custom-call | flops 22118400 | bytes 2949120 | tf_op jit(solution)/shard_map/apply_image/pallas_call | solution.py:274
  219.0 6.7 %gram.4.refs_8_ = f32[2,4,64,128]{3,2,1,0:T(8,128)S(1)} custom-call(s32[12]{0:T(128)S(1)} %stack.100.plan, bf16[2880,128]{1,0:T(8,128)(2,1)S(1)} %bitcast.88, bf16[2880,128]{1,0:T(8,128)(2,1)} %bitcast.34.refs_1_, bf16[2880,128]{1,0:T(8,128)(2,1)} %bitcast.35.refs_2_, bf16[2880,128]{1,0:T(8,128)(2,1)} %bitcast.36.refs_3_, ...), custom_call_target="tpu_custom_call" | custom-call | tf_op jit(solution)/shard_map/gram/pallas_call | solution.py:344
  225.7 2.7 gram.5
  228.5 7.5 %gram.3 = f32[2,4,64,128]{3,2,1,0:T(8,128)S(1)} custom-call(s32[16]{0:T(128)S(1)} %stack.97.plan, bf16[2880,128]{1,0:T(8,128)(2,1)} %bitcast.16.refs_0_, bf16[2880,128]{1,0:T(8,128)(2,1)S(1)} %bitcast.89, bf16[2880,128]{1,0:T(8,128)(2,1)} %bitcast.18.refs_2_, bf16[2880,128]{1,0:T(8,128)(2,1)S(1)} %bitcast.90, bf16[2880,128]{1,0:T(8,128)(2,1)} %bitcast.20.refs_4_, ...), custom_call_target="tpu_custom_call" | custom-call | tf_op jit(solution)/shard_map/gram/pallas_call | solution.py:344
  238.5 4.7 %collective-permute-done.33 = f32[2,2,64,128]{3,2,1,0:T(8,128)S(1)} collective-permute-done((f32[2,2,64,128]{3,2,1,0:T(8,128)S(1)}, f32[2,2,64,128]{3,2,1,0:T(8,128)S(1)}, u32[]{:S(2)}, u32[]{:S(2)}) %collective-permute-start.33) | collective-permute-done | bytes 131104 | tf_op jit(solution)/shard_map/ppermute | solution.py:400
  243.3 3.1 %collective-permute-done.34 = f32[2,1,64,128]{3,2,1,0:T(8,128)S(1)} collective-permute-done((f32[2,1,64,128]{3,2,1,0:T(8,128)S(1)}, f32[2,1,64,128]{3,2,1,0:T(8,128)S(1)}, u32[]{:S(2)}, u32[]{:S(2)}) %collective-permute-start.34) | collective-permute-done | bytes 65568 | tf_op jit(solution)/shard_map/ppermute | solution.py:400
  246.5 12.4 %collective-permute-start.35 = (f32[2,64,64]{2,1,0:T(8,128)S(1)}, f32[2,64,64]{2,1,0:T(8,128)S(1)}, u32[]{:S(2)}, u32[]{:S(2)}) collective-permute-start(f32[2,64,64]{2,1,0:T(8,128)S(1)} %get-tuple-element.88), channel_id=1, source_target_pairs={{0,0},{1,8},{2,16},{3,24},{4,4},{5,12},{6,20},{7,28},{8,1},{9,9},{... | collective-permute-start | bytes 98312 | tf_op jit(solution)/shard_map/ppermute | solution.py:420
  258.9 1.8 collective-permute-start.36
  260.8 1.8 copy-done.11
  262.6 1.8 copy-done.14
  264.4 6.1 %unpack.1 = f32[9,128,1152]{2,1,0:T(8,128)} custom-call(f32[9,4,160,128]{3,2,1,0:T(8,128)S(1)} %copy-done.14, f32[9,4,160,128]{3,2,1,0:T(8,128)S(1)} %copy-done.11, bf16[9,4,80,256]{3,2,1,0:T(8,128)(2,1)S(1)} %copy-done.3), custom_call_target="tpu_custom_call" | custom-call | tf_op jit(solution)/shard_map/unpack/pallas_call | solution.py:132
  (135 shorter events, 27.3 us)
Async XLA Ops:
  0.6 2.5 copy-start.23
  3.1 24.0 %copy-start.43 = (f32[9,1152]{1,0:T(8,128)S(1)}, f32[9,1152]{1,0:T(8,128)}, u32[]{:S(2)}) copy-start(f32[9,1152]{1,0:T(8,128)} %param.3) | copy-start | bytes 124420
  15.0 35.9 %copy-start.5 = (f32[9,4,160,128]{3,2,1,0:T(8,128)}, f32[9,4,160,128]{3,2,1,0:T(8,128)S(1)}, u32[]{:S(2)}) copy-start(f32[9,4,160,128]{3,2,1,0:T(8,128)S(1)} %get-tuple-element.43.refs_0_.refs_1_) | copy-start | bytes 8847364
  15.0 18.6 %collective-permute-start.8 = (bf16[4,4,144,128]{3,2,1,0:T(8,128)(2,1)}, bf16[4,4,144,128]{3,2,1,0:T(8,128)(2,1)}, u32[]{:S(2)}, u32[]{:S(2)}) collective-permute-start(bf16[4,4,144,128]{3,2,1,0:T(8,128)(2,1)} %get-tuple-element.57), channel_id=1, source_target_pairs={{0,4},{4,8},{8,12},{12,16},{16,20},{20,24},{24,28},{1,5},{5,9},{9,... | collective-permute-start | bytes 1769480 | tf_op jit(solution)/shard_map/ppermute | solution.py:291
  18.7 18.8 %collective-permute-start.9 = (bf16[4,4,144,128]{3,2,1,0:T(8,128)(2,1)}, bf16[4,4,144,128]{3,2,1,0:T(8,128)(2,1)}, u32[]{:S(2)}, u32[]{:S(2)}) collective-permute-start(bf16[4,4,144,128]{3,2,1,0:T(8,128)(2,1)} %get-tuple-element.58), channel_id=1, source_target_pairs={{4,0},{8,4},{12,8},{16,12},{20,16},{24,20},{28,24},{5,1},{9,5},{13... | collective-permute-start | bytes 1769480 | tf_op jit(solution)/shard_map/ppermute | solution.py:291
  20.6 30.3 %collective-permute-start = (bf16[4,4,144,128]{3,2,1,0:T(8,128)(2,1)}, bf16[4,4,144,128]{3,2,1,0:T(8,128)(2,1)S(1)}, u32[]{:S(2)}, u32[]{:S(2)}) collective-permute-start(bf16[4,4,144,128]{3,2,1,0:T(8,128)(2,1)} %get-tuple-element.44), channel_id=1, source_target_pairs={{0,4},{4,8},{8,12},{12,16},{16,20},{20,24},{24,28},{1,5},{5,9},{9,... | collective-permute-start | bytes 1769480 | tf_op jit(solution)/shard_map/ppermute | solution.py:291
  25.2 25.8 %collective-permute-start.1 = (bf16[4,4,144,128]{3,2,1,0:T(8,128)(2,1)}, bf16[4,4,144,128]{3,2,1,0:T(8,128)(2,1)}, u32[]{:S(2)}, u32[]{:S(2)}) collective-permute-start(bf16[4,4,144,128]{3,2,1,0:T(8,128)(2,1)} %get-tuple-element.45), channel_id=1, source_target_pairs={{4,0},{8,4},{12,8},{16,12},{20,16},{24,20},{28,24},{5,1},{9,5},{13... | collective-permute-start | bytes 1769480 | tf_op jit(solution)/shard_map/ppermute | solution.py:291
  39.3 1.8 copy-start.8
  46.6 17.3 %copy-start.21 = (f32[9,4,160,128]{3,2,1,0:T(8,128)}, f32[9,4,160,128]{3,2,1,0:T(8,128)S(1)}, u32[]{:S(2)}) copy-start(f32[9,4,160,128]{3,2,1,0:T(8,128)S(1)} %get-tuple-element.59.refs_0_.refs_1_) | copy-start | bytes 8847364
  46.6 17.3 %collective-permute-start.10 = (bf16[4,4,144,128]{3,2,1,0:T(8,128)(2,1)S(1)}, bf16[4,4,144,128]{3,2,1,0:T(8,128)(2,1)S(1)}, u32[]{:S(2)}, u32[]{:S(2)}) collective-permute-start(bf16[4,4,144,128]{3,2,1,0:T(8,128)(2,1)S(1)} %get-tuple-element.60), channel_id=1, source_target_pairs={{0,4},{4,8},{8,12},{12,16},{16,20},{20,24},{24,28},{1,5},{5,9},{9,... | collective-permute-start | bytes 1769480 | tf_op jit(solution)/shard_map/ppermute | solution.py:291
  48.5 15.4 %collective-permute-start.11 = (bf16[4,4,144,128]{3,2,1,0:T(8,128)(2,1)S(1)}, bf16[4,4,144,128]{3,2,1,0:T(8,128)(2,1)S(1)}, u32[]{:S(2)}, u32[]{:S(2)}) collective-permute-start(bf16[4,4,144,128]{3,2,1,0:T(8,128)(2,1)S(1)} %get-tuple-element.61), channel_id=1, source_target_pairs={{4,0},{8,4},{12,8},{16,12},{20,16},{24,20},{28,24},{5,1},{9,5},{13... | collective-permute-start | bytes 1769480 | tf_op jit(solution)/shard_map/ppermute | solution.py:291
  57.9 16.8 %collective-permute-start.2 = (bf16[4,4,144,128]{3,2,1,0:T(8,128)(2,1)S(1)}, bf16[4,4,144,128]{3,2,1,0:T(8,128)(2,1)S(1)}, u32[]{:S(2)}, u32[]{:S(2)}) collective-permute-start(bf16[4,4,144,128]{3,2,1,0:T(8,128)(2,1)S(1)} %get-tuple-element.47), channel_id=1, source_target_pairs={{0,4},{4,8},{8,12},{12,16},{16,20},{20,24},{24,28},{1,5},{5,9},{9,... | collective-permute-start | bytes 1769480 | tf_op jit(solution)/shard_map/ppermute | solution.py:291
  61.9 14.9 %collective-permute-start.3 = (bf16[4,4,144,128]{3,2,1,0:T(8,128)(2,1)S(1)}, bf16[4,4,144,128]{3,2,1,0:T(8,128)(2,1)S(1)}, u32[]{:S(2)}, u32[]{:S(2)}) collective-permute-start(bf16[4,4,144,128]{3,2,1,0:T(8,128)(2,1)S(1)} %get-tuple-element.48), channel_id=1, source_target_pairs={{4,0},{8,4},{12,8},{16,12},{20,16},{24,20},{28,24},{5,1},{9,5},{13... | collective-permute-start | bytes 1769480 | tf_op jit(solution)/shard_map/ppermute | solution.py:291
  63.9 12.9 %copy-start.6 = (f32[9,4,160,128]{3,2,1,0:T(8,128)S(1)}, f32[9,4,160,128]{3,2,1,0:T(8,128)}, u32[]{:S(2)}) copy-start(f32[9,4,160,128]{3,2,1,0:T(8,128)} %copy-done.5) | copy-start | bytes 8847364
  68.2 14.7 %copy-start.16 = (f32[9,4,160,128]{3,2,1,0:T(8,128)}, f32[9,4,160,128]{3,2,1,0:T(8,128)S(1)}, u32[]{:S(2)}) copy-start(f32[9,4,160,128]{3,2,1,0:T(8,128)S(1)} %get-tuple-element.62.refs_0_.refs_1_) | copy-start | bytes 8847364
  68.2 19.2 %collective-permute-start.12 = (bf16[4,4,144,128]{3,2,1,0:T(8,128)(2,1)S(1)}, bf16[4,4,144,128]{3,2,1,0:T(8,128)(2,1)S(1)}, u32[]{:S(2)}, u32[]{:S(2)}) collective-permute-start(bf16[4,4,144,128]{3,2,1,0:T(8,128)(2,1)S(1)} %get-tuple-element.63), channel_id=1, source_target_pairs={{0,4},{4,8},{8,12},{12,16},{16,20},{20,24},{24,28},{1,5},{5,9},{9,... | collective-permute-start | bytes 1769480 | tf_op jit(solution)/shard_map/ppermute | solution.py:291
  72.8 16.6 %collective-permute-start.13 = (bf16[4,4,144,128]{3,2,1,0:T(8,128)(2,1)S(1)}, bf16[4,4,144,128]{3,2,1,0:T(8,128)(2,1)S(1)}, u32[]{:S(2)}, u32[]{:S(2)}) collective-permute-start(bf16[4,4,144,128]{3,2,1,0:T(8,128)(2,1)S(1)} %get-tuple-element.64), channel_id=1, source_target_pairs={{4,0},{8,4},{12,8},{16,12},{20,16},{24,20},{28,24},{5,1},{9,5},{13... | collective-permute-start | bytes 1769480 | tf_op jit(solution)/shard_map/ppermute | solution.py:291
  76.8 1.8 copy-start.19
  78.7 10.8 %copy-start.1 = (f32[9,4,144,128]{3,2,1,0:T(8,128)S(1)}, f32[9,4,144,128]{3,2,1,0:T(8,128)}, u32[]{:S(2)}) copy-start(f32[9,4,144,128]{3,2,1,0:T(8,128)} %spread.1.refs_3_.refs_4_) | copy-start | bytes 7962628
  83.0 20.5 %copy-start.15 = (f32[9,4,160,128]{3,2,1,0:T(8,128)}, f32[9,4,160,128]{3,2,1,0:T(8,128)S(1)}, u32[]{:S(2)}) copy-start(f32[9,4,160,128]{3,2,1,0:T(8,128)S(1)} %get-tuple-element.49.refs_0_.refs_1_) | copy-start | bytes 8847364
  83.0 20.5 %collective-permute-start.4 = (bf16[4,4,144,128]{3,2,1,0:T(8,128)(2,1)S(1)}, bf16[4,4,144,128]{3,2,1,0:T(8,128)(2,1)S(1)}, u32[]{:S(2)}, u32[]{:S(2)}) collective-permute-start(bf16[4,4,144,128]{3,2,1,0:T(8,128)(2,1)S(1)} %get-tuple-element.50), channel_id=1, source_target_pairs={{0,4},{4,8},{8,12},{12,16},{16,20},{20,24},{24,28},{1,5},{5,9},{9,... | collective-permute-start | bytes 1769480 | tf_op jit(solution)/shard_map/ppermute | solution.py:291
  85.4 18.0 %collective-permute-start.5 = (bf16[4,4,144,128]{3,2,1,0:T(8,128)(2,1)S(1)}, bf16[4,4,144,128]{3,2,1,0:T(8,128)(2,1)S(1)}, u32[]{:S(2)}, u32[]{:S(2)}) collective-permute-start(bf16[4,4,144,128]{3,2,1,0:T(8,128)(2,1)S(1)} %get-tuple-element.51), channel_id=1, source_target_pairs={{4,0},{8,4},{12,8},{16,12},{20,16},{24,20},{28,24},{5,1},{9,5},{13... | collective-permute-start | bytes 1769480 | tf_op jit(solution)/shard_map/ppermute | solution.py:291
  89.4 1.8 copy-start.17
  91.3 1.8 copy-start.22
  93.1 10.4 %copy-start.20 = (f32[9,4,160,128]{3,2,1,0:T(8,128)S(1)}, f32[9,4,160,128]{3,2,1,0:T(8,128)}, u32[]{:S(2)}) copy-start(f32[9,4,160,128]{3,2,1,0:T(8,128)} %copy-done.18) | copy-start | bytes 8847364
  99.0 16.9 %collective-permute-start.14 = (bf16[4,4,144,128]{3,2,1,0:T(8,128)(2,1)S(1)}, bf16[4,4,144,128]{3,2,1,0:T(8,128)(2,1)S(1)}, u32[]{:S(2)}, u32[]{:S(2)}) collective-permute-start(bf16[4,4,144,128]{3,2,1,0:T(8,128)(2,1)S(1)} %get-tuple-element.66), channel_id=1, source_target_pairs={{0,4},{4,8},{8,12},{12,16},{16,20},{20,24},{24,28},{1,5},{5,9},{9,... | collective-permute-start | bytes 1769480 | tf_op jit(solution)/shard_map/ppermute | solution.py:291
  101.5 14.4 %collective-permute-start.15 = (bf16[4,4,144,128]{3,2,1,0:T(8,128)(2,1)S(1)}, bf16[4,4,144,128]{3,2,1,0:T(8,128)(2,1)S(1)}, u32[]{:S(2)}, u32[]{:S(2)}) collective-permute-start(bf16[4,4,144,128]{3,2,1,0:T(8,128)(2,1)S(1)} %get-tuple-element.67), channel_id=1, source_target_pairs={{4,0},{8,4},{12,8},{16,12},{20,16},{24,20},{28,24},{5,1},{9,5},{13... | collective-permute-start | bytes 1769480 | tf_op jit(solution)/shard_map/ppermute | solution.py:291
  103.5 12.4 %copy-start.27 = (f32[9,4,160,128]{3,2,1,0:T(8,128)S(1)}, f32[9,4,160,128]{3,2,1,0:T(8,128)}, u32[]{:S(2)}) copy-start(f32[9,4,160,128]{3,2,1,0:T(8,128)} %copy-done.26) | copy-start | bytes 8847364
  109.4 20.9 %collective-permute-start.6 = (bf16[4,4,144,128]{3,2,1,0:T(8,128)(2,1)S(1)}, bf16[4,4,144,128]{3,2,1,0:T(8,128)(2,1)S(1)}, u32[]{:S(2)}, u32[]{:S(2)}) collective-permute-start(bf16[4,4,144,128]{3,2,1,0:T(8,128)(2,1)S(1)} %get-tuple-element.53), channel_id=1, source_target_pairs={{0,4},{4,8},{8,12},{12,16},{16,20},{20,24},{24,28},{1,5},{5,9},{9,... | collective-permute-start | bytes 1769480 | tf_op jit(solution)/shard_map/ppermute | solution.py:291
  113.9 16.4 %collective-permute-start.7 = (bf16[4,4,144,128]{3,2,1,0:T(8,128)(2,1)S(1)}, bf16[4,4,144,128]{3,2,1,0:T(8,128)(2,1)S(1)}, u32[]{:S(2)}, u32[]{:S(2)}) collective-permute-start(bf16[4,4,144,128]{3,2,1,0:T(8,128)(2,1)S(1)} %get-tuple-element.54), channel_id=1, source_target_pairs={{4,0},{8,4},{12,8},{16,12},{20,16},{24,20},{28,24},{5,1},{9,5},{13... | collective-permute-start | bytes 1769480 | tf_op jit(solution)/shard_map/ppermute | solution.py:291
  115.9 14.4 %copy-start.25 = (f32[9,4,160,128]{3,2,1,0:T(8,128)S(1)}, f32[9,4,160,128]{3,2,1,0:T(8,128)}, u32[]{:S(2)}) copy-start(f32[9,4,160,128]{3,2,1,0:T(8,128)} %copy-done.24) | copy-start | bytes 8847364
  125.0 12.5 %copy-start.39 = (bf16[4,4,144,128]{3,2,1,0:T(8,128)(2,1)}, bf16[4,4,144,128]{3,2,1,0:T(8,128)(2,1)S(1)}, u32[]{:S(2)}) copy-start(bf16[4,4,144,128]{3,2,1,0:T(8,128)(2,1)S(1)} %get-tuple-element.69) | copy-start | bytes 1769476
  125.0 28.2 %collective-permute-start.29 = (bf16[9,4,80,128]{3,2,1,0:T(8,128)(2,1)}, bf16[9,4,80,128]{3,2,1,0:T(8,128)(2,1)}, u32[]{:S(2)}, u32[]{:S(2)}) collective-permute-start(bf16[9,4,80,128]{3,2,1,0:T(8,128)(2,1)} %get-tuple-element.81), channel_id=1, source_target_pairs={{3,2},{2,1},{7,6},{6,5},{11,10},{10,9},{15,14},{14,13},{19,18},{18... | collective-permute-start | bytes 2211848 | tf_op jit(solution)/shard_map/ppermute | solution.py:369
  126.5 28.6 %collective-permute-start.26 = (bf16[9,4,80,128]{3,2,1,0:T(8,128)(2,1)S(1)}, bf16[9,4,80,128]{3,2,1,0:T(8,128)(2,1)}, u32[]{:S(2)}, u32[]{:S(2)}) collective-permute-start(bf16[9,4,80,128]{3,2,1,0:T(8,128)(2,1)S(1)} %get-tuple-element.82), channel_id=1, source_target_pairs={{0,1},{1,2},{4,5},{5,6},{8,9},{9,10},{12,13},{13,14},{16,17},{17,1... | collective-permute-start | bytes 2211848 | tf_op jit(solution)/shard_map/ppermute | solution.py:368
  141.6 18.5 %collective-permute-start.18 = (bf16[9,4,80,128]{3,2,1,0:T(8,128)(2,1)}, bf16[9,4,80,128]{3,2,1,0:T(8,128)(2,1)}, u32[]{:S(2)}, u32[]{:S(2)}) collective-permute-start(bf16[9,4,80,128]{3,2,1,0:T(8,128)(2,1)} %get-tuple-element.72), channel_id=1, source_target_pairs={{0,1},{1,2},{4,5},{5,6},{8,9},{9,10},{12,13},{13,14},{16,17},{17,1... | collective-permute-start | bytes 2211848 | tf_op jit(solution)/shard_map/ppermute | solution.py:368
  145.7 19.3 %copy-start.29 = (bf16[9,4,80,128]{3,2,1,0:T(8,128)(2,1)S(1)}, bf16[9,4,80,128]{3,2,1,0:T(8,128)(2,1)}, u32[]{:S(2)}) copy-start(bf16[9,4,80,128]{3,2,1,0:T(8,128)(2,1)} %copy-done.28) | copy-start | bytes 2211844
  145.7 30.4 %collective-permute-start.24 = (bf16[4,4,144,128]{3,2,1,0:T(8,128)(2,1)}, bf16[4,4,144,128]{3,2,1,0:T(8,128)(2,1)S(1)}, u32[]{:S(2)}, u32[]{:S(2)}) collective-permute-start(bf16[4,4,144,128]{3,2,1,0:T(8,128)(2,1)} %copy-done.42), channel_id=1, source_target_pairs={{0,4},{4,8},{8,12},{12,16},{16,20},{20,24},{24,28},{1,5},{5,9},{9,... | collective-permute-start | bytes 1769480 | tf_op jit(solution)/shard_map/ppermute | solution.py:291
  151.3 27.0 %collective-permute-start.25 = (bf16[4,4,144,128]{3,2,1,0:T(8,128)(2,1)}, bf16[4,4,144,128]{3,2,1,0:T(8,128)(2,1)S(1)}, u32[]{:S(2)}, u32[]{:S(2)}) collective-permute-start(bf16[4,4,144,128]{3,2,1,0:T(8,128)(2,1)} %copy-done.41), channel_id=1, source_target_pairs={{4,0},{8,4},{12,8},{16,12},{20,16},{24,20},{28,24},{5,1},{9,5},{13... | collective-permute-start | bytes 1769480 | tf_op jit(solution)/shard_map/ppermute | solution.py:291
  153.2 11.9 %collective-permute-start.19 = (bf16[9,4,80,128]{3,2,1,0:T(8,128)(2,1)}, bf16[9,4,80,128]{3,2,1,0:T(8,128)(2,1)S(1)}, u32[]{:S(2)}, u32[]{:S(2)}) collective-permute-start(bf16[9,4,80,128]{3,2,1,0:T(8,128)(2,1)} %copy-done.28), channel_id=1, source_target_pairs={{3,2},{2,1},{7,6},{6,5},{11,10},{10,9},{15,14},{14,13},{19,18},{18... | collective-permute-start | bytes 2211848 | tf_op jit(solution)/shard_map/ppermute | solution.py:369
  155.1 24.0 %copy-start.40 = (bf16[4,4,144,128]{3,2,1,0:T(8,128)(2,1)S(1)}, bf16[4,4,144,128]{3,2,1,0:T(8,128)(2,1)}, u32[]{:S(2)}) copy-start(bf16[4,4,144,128]{3,2,1,0:T(8,128)(2,1)} %copy-done.39) | copy-start | bytes 1769476
  155.1 29.9 %collective-permute-start.30 = (bf16[9,4,80,128]{3,2,1,0:T(8,128)(2,1)S(1)}, bf16[9,4,80,128]{3,2,1,0:T(8,128)(2,1)}, u32[]{:S(2)}, u32[]{:S(2)}) collective-permute-start(bf16[9,4,80,128]{3,2,1,0:T(8,128)(2,1)S(1)} %broadcast_select_fusion), channel_id=1, source_target_pairs={{2,1},{1,0},{3,2},{6,5},{5,4},{7,6},{10,9},{9,8},{11,10},{14,13},{... | collective-permute-start | bytes 2211848 | tf_op jit(solution)/shard_map/ppermute | solution.py:369
  160.1 26.3 %collective-permute-start.27 = (bf16[9,4,80,128]{3,2,1,0:T(8,128)(2,1)S(1)}, bf16[9,4,80,128]{3,2,1,0:T(8,128)(2,1)}, u32[]{:S(2)}, u32[]{:S(2)}) collective-permute-start(bf16[9,4,80,128]{3,2,1,0:T(8,128)(2,1)S(1)} %broadcast_select_fusion.2), channel_id=1, source_target_pairs={{1,2},{2,3},{0,1},{5,6},{6,7},{4,5},{9,10},{10,11},{8,9},{13,14},{... | collective-permute-start | bytes 2211848 | tf_op jit(solution)/shard_map/ppermute | solution.py:368
  165.2 28.6 %collective-permute-start.20 = (bf16[9,4,80,128]{3,2,1,0:T(8,128)(2,1)S(1)}, bf16[9,4,80,128]{3,2,1,0:T(8,128)(2,1)}, u32[]{:S(2)}, u32[]{:S(2)}) collective-permute-start(bf16[9,4,80,128]{3,2,1,0:T(8,128)(2,1)S(1)} %broadcast_select_fusion.3), channel_id=1, source_target_pairs={{1,2},{2,3},{0,1},{5,6},{6,7},{4,5},{9,10},{10,11},{8,9},{13,14},{... | collective-permute-start | bytes 2211848 | tf_op jit(solution)/shard_map/ppermute | solution.py:368
  177.0 18.8 %collective-permute-start.21 = (bf16[9,4,80,128]{3,2,1,0:T(8,128)(2,1)S(1)}, bf16[9,4,80,128]{3,2,1,0:T(8,128)(2,1)}, u32[]{:S(2)}, u32[]{:S(2)}) collective-permute-start(bf16[9,4,80,128]{3,2,1,0:T(8,128)(2,1)S(1)} %broadcast_select_fusion.1), channel_id=1, source_target_pairs={{2,1},{1,0},{3,2},{6,5},{5,4},{7,6},{10,9},{9,8},{11,10},{14,13},{... | collective-permute-start | bytes 2211848 | tf_op jit(solution)/shard_map/ppermute | solution.py:369
  179.1 17.9 %collective-permute-start.16 = (bf16[4,4,144,128]{3,2,1,0:T(8,128)(2,1)S(1)}, bf16[4,4,144,128]{3,2,1,0:T(8,128)(2,1)S(1)}, u32[]{:S(2)}, u32[]{:S(2)}) collective-permute-start(bf16[4,4,144,128]{3,2,1,0:T(8,128)(2,1)S(1)} %copy-done.40), channel_id=1, source_target_pairs={{0,4},{4,8},{8,12},{12,16},{16,20},{20,24},{24,28},{1,5},{5,9},{9,... | collective-permute-start | bytes 1769480 | tf_op jit(solution)/shard_map/ppermute | solution.py:291
  185.1 40.6 %collective-permute-start.31 = (bf16[9,4,80,128]{3,2,1,0:T(8,128)(2,1)}, bf16[9,4,80,128]{3,2,1,0:T(8,128)(2,1)}, u32[]{:S(2)}, u32[]{:S(2)}) collective-permute-start(bf16[9,4,80,128]{3,2,1,0:T(8,128)(2,1)} %collective-permute-done.30), channel_id=1, source_target_pairs={{1,0},{5,4},{9,8},{13,12},{17,16},{21,20},{25,24},{29,28}} | collective-permute-start | bytes 2211848 | tf_op jit(solution)/shard_map/ppermute | solution.py:369
  186.4 39.3 %collective-permute-start.28 = (bf16[9,4,80,128]{3,2,1,0:T(8,128)(2,1)}, bf16[9,4,80,128]{3,2,1,0:T(8,128)(2,1)}, u32[]{:S(2)}, u32[]{:S(2)}) collective-permute-start(bf16[9,4,80,128]{3,2,1,0:T(8,128)(2,1)} %collective-permute-done.27), channel_id=1, source_target_pairs={{2,3},{6,7},{10,11},{14,15},{18,19},{22,23},{26,27},{30,31}} | collective-permute-start | bytes 2211848 | tf_op jit(solution)/shard_map/ppermute | solution.py:368
  193.8 34.7 %collective-permute-start.22 = (bf16[9,4,80,128]{3,2,1,0:T(8,128)(2,1)}, bf16[9,4,80,128]{3,2,1,0:T(8,128)(2,1)}, u32[]{:S(2)}, u32[]{:S(2)}) collective-permute-start(bf16[9,4,80,128]{3,2,1,0:T(8,128)(2,1)} %collective-permute-done.20), channel_id=1, source_target_pairs={{2,3},{6,7},{10,11},{14,15},{18,19},{22,23},{26,27},{30,31}} | collective-permute-start | bytes 2211848 | tf_op jit(solution)/shard_map/ppermute | solution.py:368
  195.8 32.7 %collective-permute-start.23 = (bf16[9,4,80,128]{3,2,1,0:T(8,128)(2,1)}, bf16[9,4,80,128]{3,2,1,0:T(8,128)(2,1)}, u32[]{:S(2)}, u32[]{:S(2)}) collective-permute-start(bf16[9,4,80,128]{3,2,1,0:T(8,128)(2,1)} %collective-permute-done.21), channel_id=1, source_target_pairs={{1,0},{5,4},{9,8},{13,12},{17,16},{21,20},{25,24},{29,28}} | collective-permute-start | bytes 2211848 | tf_op jit(solution)/shard_map/ppermute | solution.py:369
  197.9 15.5 %collective-permute-start.17 = (bf16[4,4,144,128]{3,2,1,0:T(8,128)(2,1)}, bf16[4,4,144,128]{3,2,1,0:T(8,128)(2,1)}, u32[]{:S(2)}, u32[]{:S(2)}) collective-permute-start(bf16[4,4,144,128]{3,2,1,0:T(8,128)(2,1)} %get-tuple-element.70), channel_id=1, source_target_pairs={{4,0},{8,4},{12,8},{16,12},{20,16},{24,20},{28,24},{5,1},{9,5},{13... | collective-permute-start | bytes 1769480 | tf_op jit(solution)/shard_map/ppermute | solution.py:291
  204.2 1.8 copy-start.13
  208.2 5.2 %copy-start.10 = (f32[9,4,160,128]{3,2,1,0:T(8,128)S(1)}, f32[9,4,160,128]{3,2,1,0:T(8,128)}, u32[]{:S(2)}) copy-start(f32[9,4,160,128]{3,2,1,0:T(8,128)} %copy-done.9) | copy-start | bytes 8847364
  208.2 5.2 %copy-start.38 = (bf16[4,4,144,128]{3,2,1,0:T(8,128)(2,1)S(1)}, bf16[4,4,144,128]{3,2,1,0:T(8,128)(2,1)}, u32[]{:S(2)}) copy-start(bf16[4,4,144,128]{3,2,1,0:T(8,128)(2,1)} %copy-done.37) | copy-start | bytes 1769476
  219.0 6.7 %copy-start.4 = (bf16[9,4,80,256]{3,2,1,0:T(8,128)(2,1)}, bf16[9,4,80,256]{3,2,1,0:T(8,128)(2,1)S(1)}, u32[]{:S(2)}) copy-start(bf16[9,4,80,256]{3,2,1,0:T(8,128)(2,1)S(1)} %get-tuple-element.80) | copy-start | bytes 4423684
  219.0 9.5 %copy-start.2 = (bf16[9,4,80,256]{3,2,1,0:T(8,128)(2,1)}, bf16[9,4,80,256]{3,2,1,0:T(8,128)(2,1)S(1)}, u32[]{:S(2)}) copy-start(bf16[9,4,80,256]{3,2,1,0:T(8,128)(2,1)S(1)} %get-tuple-element.71.refs_2_) | copy-start | bytes 4423684
  225.7 2.8 %copy-start.30 = (bf16[9,4,80,128]{3,2,1,0:T(8,128)(2,1)S(1)}, bf16[9,4,80,128]{3,2,1,0:T(8,128)(2,1)}, u32[]{:S(2)}) copy-start(bf16[9,4,80,128]{3,2,1,0:T(8,128)(2,1)} %copy-done.28) | copy-start | bytes 2211844
  225.7 2.8 %copy-start.32 = (bf16[9,4,80,128]{3,2,1,0:T(8,128)(2,1)S(1)}, bf16[9,4,80,128]{3,2,1,0:T(8,128)(2,1)}, u32[]{:S(2)}) copy-start(bf16[9,4,80,128]{3,2,1,0:T(8,128)(2,1)} %copy-done.31) | copy-start | bytes 2211844
  236.0 24.8 %copy-start.3 = (bf16[9,4,80,256]{3,2,1,0:T(8,128)(2,1)S(1)}, bf16[9,4,80,256]{3,2,1,0:T(8,128)(2,1)}, u32[]{:S(2)}) copy-start(bf16[9,4,80,256]{3,2,1,0:T(8,128)(2,1)} %copy-done.2) | copy-start | bytes 4423684
  236.1 2.2 collective-permute-start.32
  238.4 4.8 %collective-permute-start.33 = (f32[2,2,64,128]{3,2,1,0:T(8,128)S(1)}, f32[2,2,64,128]{3,2,1,0:T(8,128)S(1)}, u32[]{:S(2)}, u32[]{:S(2)}) collective-permute-start(f32[2,2,64,128]{3,2,1,0:T(8,128)S(1)} %dynamic-slice_bitcast_fusion), channel_id=1, source_target_pairs={{0,8},{4,12},{8,0},{12,4},{16,24},{20,28},{24,16},{28,20},{1,9},{5... | collective-permute-start | bytes 393224 | tf_op jit(solution)/shard_map/ppermute | solution.py:400
  243.2 3.2 %collective-permute-start.34 = (f32[2,1,64,128]{3,2,1,0:T(8,128)S(1)}, f32[2,1,64,128]{3,2,1,0:T(8,128)S(1)}, u32[]{:S(2)}, u32[]{:S(2)}) collective-permute-start(f32[2,1,64,128]{3,2,1,0:T(8,128)S(1)} %constant_dynamic-slice_fusion), channel_id=1, source_target_pairs={{0,16},{4,20},{8,24},{12,28},{16,0},{20,4},{24,8},{28,12},{1,17},{... | collective-permute-start | bytes 196616 | tf_op jit(solution)/shard_map/ppermute | solution.py:400
  246.5 24.0 %collective-permute-start.35 = (f32[2,64,64]{2,1,0:T(8,128)S(1)}, f32[2,64,64]{2,1,0:T(8,128)S(1)}, u32[]{:S(2)}, u32[]{:S(2)}) collective-permute-start(f32[2,64,64]{2,1,0:T(8,128)S(1)} %get-tuple-element.88), channel_id=1, source_target_pairs={{0,0},{1,8},{2,16},{3,24},{4,4},{5,12},{6,20},{7,28},{8,1},{9,9},{... | collective-permute-start | bytes 98312 | tf_op jit(solution)/shard_map/ppermute | solution.py:420
  258.9 11.6 %collective-permute-start.36 = (f32[2,64,64]{2,1,0:T(8,128)S(1)}, f32[2,64,64]{2,1,0:T(8,128)S(1)}, u32[]{:S(2)}, u32[]{:S(2)}) collective-permute-start(f32[2,64,64]{2,1,0:T(8,128)S(1)} %get-tuple-element.87), channel_id=1, source_target_pairs={{0,4},{1,12},{2,20},{3,28},{4,0},{5,8},{6,16},{7,24},{8,5},{9,13},... | collective-permute-start | bytes 98312 | tf_op jit(solution)/shard_map/ppermute | solution.py:420
  260.8 1.8 copy-start.11
  (17 other events, 21.2 us)
where the time goes:
time: 275 us; the launch traced here: 271 us
  starting transfers between devices  112 us (41%)
  Pallas kernels  91.4 us (33%)
  local copies, waits for them, and re-layouts  36.5 us (13%)
  waiting for transfers between devices  26.5 us (10%)
  other arithmetic  2.93 us (1%)
    pallas_call x10, Pallas kernels, apply_op(): pl.pallas_call(functools.partial(apply_kernel, mode), in_specs=specs, out...  52.4 us
    ppermute x10, starting transfers between devices, exchange(): lax.ppermute(above, 'domain', up)  39.7 us
    unnamed x88, local copies, waits for them, and re-layouts  34.8 us
    ppermute x6, starting transfers between devices, hops(): up = lax.ppermute(up, 'band', [(b - 1, b) for b in pairs])  26 us
    ppermute x10, starting transfers between devices, exchange(): lax.ppermute(below, 'domain', down)  23.7 us
    pallas_call x3, Pallas kernels, gram(): pl.pallas_call(lambda plan, *refs: kernel(plan, *refs[:len(flat)], *refs[...  16.9 us
    ppermute x2, starting transfers between devices, other_triangle(): lax.ppermute(block, ('domain', 'band'), pairs).transpose(0, 2, 1)  14.2 us
    pallas_call x1, Pallas kernels, pack(): pl.pallas_call(functools.partial(pack_kernel, chunks), grid=(nx,), in_spe...  10.3 us
  transfers between devices with their start and end apart: 37, of which 10 were waited for; matrix products, arithmetic and copies ran while one was open for 1% of the time, Pallas kernels for 27%

commit v1 on v0

--- a/solution.py
+++ b/solution.py
@@ -14,7 +14,8 @@
 CUT = 72
 PART = 80
 FIRST_B = NZ - PART
-VMEM_LIMIT = 40 << 20
+SMALL_LIMIT = 6 << 20
+GRAM_LIMIT = 10 << 20
 
 coeffs = (-205.0 / 72.0, 8.0 / 5.0, -1.0 / 5.0, 8.0 / 315.0, -1.0 / 560.0)
 kinetic = -0.5 / 0.09
@@ -23,9 +24,15 @@
 scaled_coeffs = [kinetic * c / half_width for c in coeffs]
 carry = [coeffs[k] / coeffs[k + 1] for k in range(1, 4)]
 
+limits = {"first": 12 << 20, "middle": 15 << 20, "last": 19 << 20, "image": 14 << 20}
+
 IN_VMEM = pl.BlockSpec(memory_space=pltpu.VMEM)
 ANYWHERE = pl.BlockSpec(memory_space=pl.ANY)
 IN_SMEM = pl.BlockSpec(memory_space=pltpu.SMEM)
+
+
+def cost(moved):
+    return pl.CostEstimate(flops=0, bytes_accessed=moved, transcendentals=0)
 
 
 def rounded_planes(planes):
@@ -38,15 +45,16 @@
     return sent
 
 
-def pack_kernel(chunks, field, *refs):
-    outs, errors = refs[: 3 * chunks], refs[3 * chunks :]
+def halves(rows):
+    half = rows.shape[1] // 2
+    wide = -(-half // 128) * 128
+    far = pltpu.roll(rows, half, 1)
+    return jnp.concatenate([rows[:, :wide], far[:, :wide]], axis=0).T
+
+
+def pack_kernel(field, packed, below, above, error):
     step = pl.program_id(0)
-    rows = field[0]
-    if rows.shape[0] < 128:
-        rows = jnp.concatenate([rows, rows], axis=0)
-    flipped = rows.T
-    half = flipped.shape[0] // 2
-    left = lax.broadcasted_iota(jnp.int32, (NZ, 128), 1) < GROUP
+    flipped = halves(field[0])
     place = lax.rem(step, 4)
     factor = jnp.where(
         place == 0, 0.0, jnp.where(place == 1, carry[0], jnp.where(place == 2, carry[1], carry[2]))
@@ -54,58 +62,51 @@
 
     @pl.when(step == 0)
     def _():
-        for error in errors:
-            error[...] = jnp.zeros_like(error)
-
-    for y in range(half // NZ):
-        near = flipped[y * NZ : (y + 1) * NZ]
-        far = flipped[half + y * NZ : half + (y + 1) * NZ]
-        for c in range(chunks):
-            packed, below, above = outs[3 * c : 3 * c + 3]
-            if chunks == 1:
-                value = jnp.where(left, near, far)
-            elif c == 0:
-                value = jnp.where(left, near, pltpu.roll(far, GROUP, 1))
-            else:
-                value = jnp.where(left, pltpu.roll(near, GROUP, 1), far)
-            packed[0, y, 0:PAD, :] = jnp.zeros((PAD, 128), jnp.float32)
-            packed[0, y, NZ + PAD : NZ + 2 * PAD, :] = jnp.zeros((PAD, 128), jnp.float32)
-            packed[0, y, PAD : NZ + PAD, :] = value
-            wide = value + factor * errors[c][y]
+        error[...] = jnp.zeros_like(error)
+
+    for y in range(packed.shape[1]):
+        value = flipped[y * NZ : (y + 1) * NZ]
+        packed[0, y, 0:PAD, :] = jnp.zeros((PAD, 128), jnp.float32)
+        packed[0, y, NZ + PAD : NZ + 2 * PAD, :] = jnp.zeros((PAD, 128), jnp.float32)
+        packed[0, y, PAD : NZ + PAD, :] = value
+
+        @pl.when(step < 8)
+        def _():
+            wide = value + factor * error[y]
             low = wide.astype(jnp.bfloat16)
-            errors[c][y] = wide - low.astype(jnp.float32)
+            error[y] = wide - low.astype(jnp.float32)
 
             @pl.when(step < 4)
             def _():
                 below[step, y] = low
 
-            @pl.when(jnp.logical_and(step >= 4, step < 8))
+            @pl.when(step >= 4)
             def _():
                 above[7 - step, y] = low
 
 
-def pack(field, chunks):
-    nx, rows, cells = field.shape
+def pack(field, chunk):
+    nx, _, cells = field.shape
     ny = cells // NZ // 2
 
     def plane(s):
         return jnp.where(s < 4, s, jnp.where(s < 8, nx + 3 - s, s - 4))
 
-    shapes, specs = [], []
-    for _ in range(chunks):
-        shapes.append(jax.ShapeDtypeStruct((nx, ny, NZ + 2 * PAD, 128), jnp.float32))
-        specs.append(pl.BlockSpec((1, ny, NZ + 2 * PAD, 128), lambda s: (plane(s), 0, 0, 0)))
-        for _ in range(2):
-            shapes.append(jax.ShapeDtypeStruct((4, ny, NZ, 128), jnp.bfloat16))
-            specs.append(pl.BlockSpec((4, ny, NZ, 128), lambda s: (0, 0, 0, 0)))
+    edge = jax.ShapeDtypeStruct((4, ny, NZ, 128), jnp.bfloat16)
+    edge_spec = pl.BlockSpec((4, ny, NZ, 128), lambda s: (0, 0, 0, 0))
     return pl.pallas_call(
-        functools.partial(pack_kernel, chunks),
+        pack_kernel,
         grid=(nx,),
-        in_specs=[pl.BlockSpec((1, rows, cells), lambda s: (plane(s), 0, 0))],
-        out_specs=specs,
-        out_shape=shapes,
-        scratch_shapes=[pltpu.VMEM((ny, NZ, 128), jnp.float32)] * chunks,
-        compiler_params=pltpu.CompilerParams(vmem_limit_bytes=VMEM_LIMIT),
+        in_specs=[pl.BlockSpec((1, GROUP, cells), lambda s: (plane(s), chunk, 0))],
+        out_specs=[
+            pl.BlockSpec((1, ny, NZ + 2 * PAD, 128), lambda s: (plane(s), 0, 0, 0)),
+            edge_spec,
+            edge_spec,
+        ],
+        out_shape=[jax.ShapeDtypeStruct((nx, ny, NZ + 2 * PAD, 128), jnp.float32), edge, edge],
+        scratch_shapes=[pltpu.VMEM((ny, NZ, 128), jnp.float32)],
+        compiler_params=pltpu.CompilerParams(vmem_limit_bytes=SMALL_LIMIT),
+        cost_estimate=cost(2 * GROUP * nx * cells * 8),
         name="pack",
     )(field)
 
@@ -136,17 +137,30 @@
         + [ANYWHERE] * len(after),
         out_specs=pl.BlockSpec((1, rows, cells), lambda s: (s, 0, 0)),
         out_shape=jax.ShapeDtypeStruct((nx, rows, cells), jnp.float32),
-        compiler_params=pltpu.CompilerParams(vmem_limit_bytes=VMEM_LIMIT),
+        compiler_params=pltpu.CompilerParams(vmem_limit_bytes=SMALL_LIMIT),
+        cost_estimate=cost(rows * nx * cells * 16),
         name="unpack",
     )(*chunks, *after)
 
 
-def apply_kernel(mode, *refs):
+def apply_kernel(mode, waits, earlier, chunk, *refs):
     refs = list(refs)
+    copies = []
+    if earlier:
+        sems = refs.pop()
     lower = refs.pop(0) if mode == "image" else None
     cur = refs.pop(0)
     prev = refs.pop(0) if mode in ("middle", "last") else None
     below, above, pot = refs.pop(0), refs.pop(0), refs.pop(0)
+    if chunk is not None:
+        below, above = below.at[chunk], above.at[chunk]
+    refs = refs[waits:]
+    if earlier:
+        copies = [pltpu.make_async_copy(refs[i], refs[3 + i].at[0], sems.at[i]) for i in range(2)]
+        refs = refs[2:]
+        refs[1:3] = [refs[1].at[1], refs[2].at[1]]
+    for copy in copies:
+        copy.start()
     nx, ny = cur.shape[:2]
     left = lax.broadcasted_iota(jnp.int32, (TILE, 128), 1) < GROUP
     if mode == "image":
@@ -255,11 +269,13 @@
         loop(0, FIRST_B // TILE, True, False)
         loop(FIRST_B // TILE, PART // TILE, True, True)
         loop(PART // TILE, NZ // TILE, False, True)
-
-
-def apply_op(mode, cur, prev, below, above, pot, lower=None):
+    for copy in copies:
+        copy.wait()
+
+
+def apply_op(mode, cur, prev, below, above, pot, lower=None, after=(), earlier=(), chunk=None):
     nx, ny = cur.shape[:2]
-    edge = jax.ShapeDtypeStruct((4, ny, NZ, 128), jnp.bfloat16)
+    edge = jax.ShapeDtypeStruct(((2,) if earlier else ()) + (4, ny, NZ, 128), jnp.bfloat16)
     part = jax.ShapeDtypeStruct((nx, ny, PART, 128), jnp.bfloat16)
     wide = jax.ShapeDtypeStruct((nx, ny, PART, 256), jnp.bfloat16)
     shapes = [jax.ShapeDtypeStruct(cur.shape, cur.dtype), edge, edge]
@@ -271,15 +287,16 @@
     specs = [IN_VMEM] * len(args)
     if mode == "image":
         args, specs = [lower] + args, [IN_SMEM] + specs
+    args = args + list(after) + list(earlier)
+    specs = specs + [ANYWHERE] * (len(after) + len(earlier))
     return pl.pallas_call(
-        functools.partial(apply_kernel, mode),
+        functools.partial(apply_kernel, mode, len(after), bool(earlier), chunk),
         in_specs=specs,
         out_specs=[IN_VMEM] * len(shapes),
         out_shape=shapes,
-        compiler_params=pltpu.CompilerParams(vmem_limit_bytes=VMEM_LIMIT),
-        cost_estimate=pl.CostEstimate(
-            flops=30 * cur.size, bytes_accessed=4 * cur.size, transcendentals=0
-        ),
+        scratch_shapes=[pltpu.SemaphoreType.DMA((2,))] if earlier else [],
+        compiler_params=pltpu.CompilerParams(vmem_limit_bytes=limits[mode]),
+        cost_estimate=cost(22 * cur.size),
         name="apply_" + mode,
     )(*args)
 
@@ -291,85 +308,109 @@
     return lax.ppermute(above, "domain", up), lax.ppermute(below, "domain", down)
 
 
-def gram_kernel(kinds, chunks, has_sums, *refs):
-    plan, refs = refs[0], refs[1:]
-    blocks, refs = refs[: len(kinds)], refs[len(kinds) :]
-    rights, refs = refs[: 3 * chunks], refs[3 * chunks :]
-    sums = refs[0] if has_sums else None
-    out, full = refs[-2], refs[-1]
+def gram_kernel(kinds, used, chunks, plan, *refs):
+    count = len(kinds)
+    blocks, refs = refs[: count * chunks], refs[count * chunks :]
+    rights, refs = refs[: len(used) * chunks], refs[len(used) * chunks :]
+    sums, out, full = refs[0], refs[-2], refs[-1]
     left = lax.broadcasted_iota(jnp.int32, (GROUP, 128), 1) < GROUP
-    out[...] = sums[...] if has_sums else jnp.zeros_like(out)
-    depth = blocks[0].shape[0]
-    part = depth // 3
-
-    def one(block, kind, slot):
-        full[...] = jnp.zeros_like(full)
-
-        def step(i, _):
-            rows = pl.ds(pl.multiple_of(i * part, 16), part)
-            for c in range(chunks):
-                full[c] += lax.dot_general(
-                    block[rows, :],
-                    rights[3 * c + kind][rows, :],
-                    (((0,), (0,)), ((), ())),
-                    preferred_element_type=jnp.float32,
-                )
-            return 0
-
-        lax.fori_loop(0, 3, step, 0)
-        for m in range(2):
-            lanes = slice(128 * m, 128 * (m + 1))
-            value = full[0, 0:GROUP, lanes] + pltpu.roll(full[0, GROUP:128, lanes], GROUP, 1)
-            if chunks == 2:
-                second = pltpu.roll(full[1, 0:GROUP, lanes], GROUP, 1) + full[1, GROUP:128, lanes]
-                value = jnp.where(left, value, second)
-            out[m, slot] += value
+    step = pl.program_id(0)
 
     for i, choices in enumerate(kinds):
         for kind in choices:
 
             @pl.when(plan[2 * i] == kind)
             def _():
-                one(blocks[i], kind, plan[2 * i + 1])
-
-
-def gram(blocks, kinds, plan, rights, sums, bands, after=()):
+                mine = blocks[chunks * i : chunks * (i + 1)]
+                turned = jnp.concatenate([block[...].T for block in mine], axis=0)
+                ours = [rights[len(used) * c + used.index(kind)][...] for c in range(chunks)]
+                value = jnp.dot(
+                    turned, jnp.concatenate(ours, axis=1), preferred_element_type=jnp.float32
+                )
+
+                @pl.when(step == 0)
+                def _():
+                    full[i] = value
+
+                @pl.when(step > 0)
+                def _():
+                    full[i] += value
+
+    @pl.when(step == pl.num_programs(0) - 1)
+    def _():
+        out[...] = sums[...]
+        for i in range(count):
+
+            @pl.when(plan[2 * i] < 3)
+            def _():
+                for other in range(chunks):
+                    top = slice(128 * other, 128 * other + GROUP)
+                    low = slice(128 * other + GROUP, 128 * (other + 1))
+                    for m in range(2):
+                        lanes = slice(128 * m, 128 * (m + 1))
+                        value = full[i, top, lanes] + pltpu.roll(full[i, low, lanes], GROUP, 1)
+                        if chunks == 2:
+                            lanes = slice(256 + 128 * m, 256 + 128 * (m + 1))
+                            second = pltpu.roll(full[i, top, lanes], GROUP, 1)
+                            value = jnp.where(left, value, second + full[i, low, lanes])
+                        out[m, plan[2 * i + 1], other] += value
+
+
+def gram(blocks, kinds, plan, rights, sums, after=()):
     chunks = len(rights)
+    steps = 6
     flat = [block.reshape(-1, 128) for block in blocks]
-    flat = flat + [part.reshape(-1, 256) for three in rights for part in three]
-    if sums is not None:
-        flat.append(sums)
-    shape = (2, bands, GROUP, 128)
-    kernel = functools.partial(gram_kernel, kinds, chunks, sums is not None)
+    used = sorted({kind for choices in kinds for kind in choices})
+    right = [three[kind].reshape(-1, 256) for three in rights for kind in used]
+    part = flat[0].shape[0] // steps
+    whole = pl.BlockSpec(sums.shape, lambda s: (0,) * sums.ndim)
     return pl.pallas_call(
-        lambda plan, *refs: kernel(plan, *refs[: len(flat)], *refs[len(flat) + len(after) :]),
-        in_specs=[IN_SMEM] + [IN_VMEM] * len(flat) + [ANYWHERE] * len(after),
-        out_specs=IN_VMEM,
-        out_shape=jax.ShapeDtypeStruct(shape, jnp.float32),
-        scratch_shapes=[pltpu.VMEM((chunks, 128, 256), jnp.float32)],
-        compiler_params=pltpu.CompilerParams(vmem_limit_bytes=VMEM_LIMIT),
+        functools.partial(gram_kernel, kinds, used, chunks),
+        grid=(steps,),
+        in_specs=[IN_SMEM]
+        + [pl.BlockSpec((part, 128), lambda s: (s, 0))] * len(flat)
+        + [pl.BlockSpec((part, 256), lambda s: (s, 0))] * len(right)
+        + [whole]
+        + [ANYWHERE] * len(after),
+        out_specs=whole,
+        out_shape=jax.ShapeDtypeStruct(sums.shape, jnp.float32),
+        scratch_shapes=[pltpu.VMEM((len(kinds), 128 * chunks, 256 * chunks), jnp.float32)],
+        compiler_params=pltpu.CompilerParams(vmem_limit_bytes=GRAM_LIMIT),
+        cost_estimate=cost(len(flat) * flat[0].size * 8),
         name="gram",
-    )(plan, *flat, *after)
-
-
-def hops(low_a, low_b):
+    )(plan, *flat, *right, sums, *after)
+
+
+def hop_operands(hop, up, down, low_a, low_b):
     bands = lax.axis_size("band")
     band = lax.axis_index("band")
     mid = bands // 2
-    up, down = low_a, low_b
-    ups, downs = [], []
-    for hop in range(1, bands):
-        pairs = [b for b in range(hop, bands) if b - hop < mid]
-        if hop >= mid:
-            pairs = pairs + list(range(hop - mid + 1, mid))
-        if hop == mid and mid > 1:
-            up = jnp.where(band < mid - 1, low_b, up)
-            down = jnp.where(band > bands - mid, low_a, down)
-        up = lax.ppermute(up, "band", [(b - 1, b) for b in pairs])
-        down = lax.ppermute(down, "band", [(bands - b, bands - 1 - b) for b in pairs])
-        ups.append(up)
-        downs.append(down)
-    return ups, downs
+    if hop == mid and mid > 1:
+        up = jnp.where(band < mid - 1, low_b, up)
+        down = jnp.where(band > bands - mid, low_a, down)
+    return up, down
+
+
+def behind(arrays, after):
+    return pl.pallas_call(
+        lambda *refs: None,
+        in_specs=[ANYWHERE] * (len(arrays) + len(after)),
+        out_specs=[ANYWHERE] * len(arrays),
+        out_shape=[jax.ShapeDtypeStruct(x.shape, x.dtype) for x in arrays],
+        input_output_aliases={i: i for i in range(len(arrays))},
+        name="behind",
+    )(*arrays, *after)
+
+
+def hop_move(hop, up, down):
+    bands = lax.axis_size("band")
+    mid = bands // 2
+    pairs = [b for b in range(hop, bands) if b - hop < mid]
+    if hop >= mid:
+        pairs = pairs + list(range(hop - mid + 1, mid))
+    up = lax.ppermute(up, "band", [(b - 1, b) for b in pairs])
+    down = lax.ppermute(down, "band", [(bands - b, bands - 1 - b) for b in pairs])
+    return up, down
 
 
 def hop_plan(hop, bands, band):
@@ -429,13 +470,7 @@
 
 
 def pot_kernel(diagonal, out):
-    row = diagonal[0]
-    half = row.shape[1] // 2
-    wide = -(-half // 128) * 128
-    first = lax.broadcasted_iota(jnp.int32, (128, wide), 0) < GROUP
-    near = jnp.broadcast_to(row[:, :wide], (128, wide))
-    far = jnp.broadcast_to(pltpu.roll(row, half, 1)[:, :wide], (128, wide))
-    flipped = jnp.where(first, near, far).T
+    flipped = halves(jnp.broadcast_to(diagonal[0], (GROUP, diagonal.shape[2])))
     for y in range(out.shape[1]):
         out[0, y] = flipped[y * NZ : (y + 1) * NZ]
 
@@ -449,6 +484,8 @@
         in_specs=[pl.BlockSpec((1, 1, cells), lambda s: (s, 0, 0))],
         out_specs=pl.BlockSpec((1, ny, NZ, 128), lambda s: (s, 0, 0, 0)),
         out_shape=jax.ShapeDtypeStruct((nx, ny, NZ, 128), jnp.float32),
+        compiler_params=pltpu.CompilerParams(vmem_limit_bytes=SMALL_LIMIT),
+        cost_estimate=cost(128 * nx * cells * 5),
         name="spread",
     )(diagonal.reshape(nx, 1, cells))
 
@@ -461,46 +498,79 @@
 
     pot = spread((3.0 * kinetic * coeffs[0] + potential - center) / half_width)
 
-    packed = pack(orbitals.transpose(1, 0, 2), chunks)
-    cur = [packed[3 * c] for c in range(chunks)]
-    edges = [(packed[3 * c + 1], packed[3 * c + 2]) for c in range(chunks)]
+    field = orbitals.transpose(1, 0, 2)
+    packed = [pack(field, c) for c in range(chunks)]
+    cur = [packed[c][0] for c in range(chunks)]
+    edges = [(packed[c][1], packed[c][2]) for c in range(chunks)]
+    token = packed[-1][0]
     prev = [None] * chunks
     lows = [None] * chunks
     for step in range(4):
         mode = "first" if step == 0 else ("last" if step == 3 else "middle")
         for c in range(chunks):
             below, above = exchange(*edges[c])
-            out = apply_op(mode, cur[c], prev[c], below, above, pot)
+            after = [token]
+            earlier = edges[0] if step == 3 and c > 0 else ()
+            out = apply_op(mode, cur[c], prev[c], below, above, pot, after=after, earlier=earlier)
             prev[c], cur[c], edges[c] = cur[c], out[0], (out[1], out[2])
-            lows[c] = out[3:]
+            lows[c] = out[3:5]
+            token = out[0]
     band = lax.axis_index("band")
     lower = (band < bands // 2).astype(jnp.int32).reshape(1)
-    moved = [hops(*lows[c]) for c in range(chunks)]
-    rights = []
+    ups, downs = [[] for _ in range(chunks)], [[] for _ in range(chunks)]
+    sending, rights = [], []
+
+    def move(c, hop):
+        up, down = hop_move(hop, *sending[c])
+        ups[c].append(up)
+        downs[c].append(down)
+
     for c in range(chunks):
-        below, above = exchange(*edges[c])
-        rights.append(apply_op("image", cur[c], None, below, above, pot, lower))
-    filtered = unpack(cur, own, after=[rights[-1][0]])
-
-    own_plan = [jnp.int32(0), band, jnp.int32(1), band]
+        sending.append(tuple(lows[c]))
+        move(c, 1)
+    halo = exchange(*edges[-1])
+    for c in range(chunks):
+        if bands > 2:
+            sending[c] = hop_operands(2, ups[c][0], downs[c][0], *lows[c])
+            move(c, 2)
+        after = [token] if c > 0 else [token, ups[0][-1], downs[0][-1]]
+        chunk = c if chunks > 1 else None
+        rights.append(apply_op("image", cur[c], None, *halo, pot, lower, after, chunk=chunk))
+        token = rights[-1][0]
+    zeros = jnp.zeros((2, bands, chunks, GROUP, 128), jnp.float32)
+    for hop in range(3, bands):
+        for c in range(chunks):
+            sending[c] = hop_operands(hop, ups[c][-1], downs[c][-1], *lows[c])
+            if hop == 3 and c == chunks - 1:
+                ups[c][-1], downs[c][-1], zeros = behind([*sending[c], zeros], [token])
+                sending[c] = (ups[c][-1], downs[c][-1])
+            move(c, hop)
+
     plans = [hop_plan(hop, bands, band) for hop in range(1, bands)]
-    kinds = [((0,), (2,)) if hop < bands // 2 else ((0, 1), (2, 0)) for hop in range(1, bands)]
-    tables = []
-    for c in range(chunks):
-        ups, downs = moved[c]
-        blocks = list(lows[c])
-        plan, choice = list(own_plan), [(0,), (1,)]
-        sums = None
-        for i in range(bands - 1):
-            blocks += [ups[i], downs[i]]
-            plan += plans[i]
+    late = [0 <= hop - bands // 2 < bands // 2 - 1 for hop in range(1, bands)]
+    kinds = [((0, 1), (2, 0)) if behind else ((0,), (2,)) for behind in late]
+
+    def add_products(sums, first, last, after=()):
+        blocks, plan, choice = [], [], []
+        if first == 0:
+            blocks = [lows[c][part] for part in range(2) for c in range(chunks)]
+            choice = [(0,), (1,)]
+            plan = [jnp.int32(0), band, jnp.int32(1), band]
+        for i in range(max(first, 1) - 1, last):
+            blocks += [ups[c][i] for c in range(chunks)] + [downs[c][i] for c in range(chunks)]
+            plan = plan + plans[i]
             choice += kinds[i]
-            if i == bands - 2 or (c == chunks - 1 and i == bands - 3):
-                rows = jnp.stack(plan).astype(jnp.int32)
-                sums = gram(blocks, tuple(choice), rows, rights, sums, bands)
-                blocks, plan, choice = [], [], []
-        tables.append(sums)
-    table = jnp.stack(tables, axis=2).reshape(2, bands * own, 128)[:, :, :own]
+        rows = jnp.stack(plan).astype(jnp.int32)
+        return gram(blocks, tuple(choice), rows, rights, sums, after=after)
+
+    done = max(bands - 2, 1)
+    table = zeros
+    for last in range(1, done + 1):
+        table = add_products(table, 0 if last == 1 else last, last)
+    filtered = unpack(cur, own, after=[table])
+    if bands > done + 1:
+        table = add_products(table, bands - 1, bands - 1, [filtered])
+    table = table.reshape(2, bands * own, 128)[:, :, :own]
     table = summed_over_domain(table)
     table = (table + other_triangle(table)) / total_cells
     return (filtered.transpose(1, 0, 2), table[0], table[1])

time: 275 us -> 264 us (0.960)
  waiting for transfers between devices: 26.5 us -> 53.2 us
  starting transfers between devices: 112 us -> 86.3 us
  Pallas kernels: 91.4 us -> 81 us
  other arithmetic: 2.93 us -> 8.67 us
  local copies, waits for them, and re-layouts: 36.5 us -> 30.8 us
    ppermute x10 -> x9, waiting for transfers between devices: 8.95 us -> 29.3 us  [exchange(): lax.ppermute(below, 'domain', down)]
    ppermute x10 -> x9, starting transfers between devices: 39.7 us -> 21.9 us  [exchange(): lax.ppermute(above, 'domain', up)]
    pallas_call x14 -> x16, Pallas kernels: 79.6 us -> 73 us  [the longest x10 49.3 us: apply_op(): pl.pallas_call(functools.partial(apply_kernel, mode, len(after), bool(ear...]
    ppermute x2, waiting for transfers between devices: 0.01 us -> 6.04 us  [other_triangle(): lax.ppermute(block, ('domain', 'band'), pairs).transpose(0, 2, 1)]
    unnamed x88 -> x74, local copies, waits for them, and re-layouts: 34.8 us -> 28.8 us
    select_n x4, other arithmetic: 2.57 us -> 8.33 us  [the longest x2 4.18 us: hop_operands(): up = jnp.where(band < mid - 1, low_b, up)]
    pallas_call x1, Pallas kernels: 5.82 us -> 1.87 us  [spread(): pl.pallas_call(pot_kernel, grid=(nx,), in_specs=[pl.BlockSpec((1, 1, cell...]
    ppermute x2, starting transfers between devices: 14.2 us -> 10.4 us  [other_triangle(): lax.ppermute(block, ('domain', 'band'), pairs).transpose(0, 2, 1)]
  transfers between devices with their start and end apart: 37 -> 35, of which waited for: 10 -> 15; matrix products, arithmetic and copies ran while one was open for 1% -> 3% of each run, Pallas kernels for 27% -> 28%
where the time goes in v1:
time: 264 us; the launch traced here: 261 us
  starting transfers between devices  86.3 us (33%)
  Pallas kernels  81 us (31%)
  waiting for transfers between devices  53.2 us (20%)
  local copies, waits for them, and re-layouts  30.8 us (12%)
  other arithmetic  8.67 us (3%)
    pallas_call x10, Pallas kernels, apply_op(): pl.pallas_call(functools.partial(apply_kernel, mode, len(after), bool(ear...  49.3 us
    ppermute x9, waiting for transfers between devices, exchange(): lax.ppermute(below, 'domain', down)  29.3 us
    unnamed x74, local copies, waits for them, and re-layouts  28.8 us
    ppermute x6, starting transfers between devices, hop_move(): up = lax.ppermute(up, 'band', [(b - 1, b) for b in pairs])  22.5 us
    ppermute x9, starting transfers between devices, exchange(): lax.ppermute(above, 'domain', up)  21.9 us
    ppermute x9, starting transfers between devices, exchange(): lax.ppermute(below, 'domain', down)  20.7 us
    pallas_call x3, Pallas kernels, gram(): pl.pallas_call(functools.partial(gram_kernel, kinds, used, chunks), grid=...  18.2 us
    ppermute x2, starting transfers between devices, other_triangle(): lax.ppermute(block, ('domain', 'band'), pairs).transpose(0, 2, 1)  10.4 us
  transfers between devices with their start and end apart: 35, of which 15 were waited for; matrix products, arithmetic and copies ran while one was open for 3% of the time, Pallas kernels for 28%

profile of v1, /device:TPU:3, one launch (start us, length us, event | category | flops | bytes accessed | tf_op | source)
XLA Modules:
  0.0 261.3 jit_solution(5272590997249699692)
XLA Ops:
  0.6 2.5 copy-done.11
  3.1 2.8 %pack.2 = (f32[9,4,160,128]{3,2,1,0:T(8,128)S(1)}, bf16[4,4,144,128]{3,2,1,0:T(8,128)(2,1)S(1)}, bf16[4,4,144,128]{3,2,1,0:T(8,128)(2,1)S(1)}) custom-call(f32[9,128,1152]{2,1,0:T(8,128)S(1)} %bitcast.71), custom_call_target="tpu_custom_call" | custom-call | bytes 10616832 | tf_op jit(solution)/shard_map/pack/pallas_call | solution.py:97
  5.9 3.8 %collective-permute-start = (bf16[4,4,144,128]{3,2,1,0:T(8,128)(2,1)S(1)}, bf16[4,4,144,128]{3,2,1,0:T(8,128)(2,1)S(1)}, u32[]{:S(2)}, u32[]{:S(2)}) collective-permute-start(bf16[4,4,144,128]{3,2,1,0:T(8,128)(2,1)S(1)} %get-tuple-element.47), channel_id=1, source_target_pairs={{0,4},{4,8},{8,12},{12,16},{16,20},{20,24},{24,28},{1,5},{5,9},{9,... | collective-permute-start | bytes 1769480 | tf_op jit(solution)/shard_map/ppermute | solution.py:308
  9.8 1.9 collective-permute-start.1
  11.7 2.8 %pack.3 = (f32[9,4,160,128]{3,2,1,0:T(8,128)S(1)}, bf16[4,4,144,128]{3,2,1,0:T(8,128)(2,1)S(1)}, bf16[4,4,144,128]{3,2,1,0:T(8,128)(2,1)S(1)}) custom-call(f32[9,128,1152]{2,1,0:T(8,128)S(1)} %bitcast.72), custom_call_target="tpu_custom_call" | custom-call | bytes 10616832 | tf_op jit(solution)/shard_map/pack/pallas_call | solution.py:97
  14.5 4.5 %collective-permute-start.4 = (bf16[4,4,144,128]{3,2,1,0:T(8,128)(2,1)S(1)}, bf16[4,4,144,128]{3,2,1,0:T(8,128)(2,1)S(1)}, u32[]{:S(2)}, u32[]{:S(2)}) collective-permute-start(bf16[4,4,144,128]{3,2,1,0:T(8,128)(2,1)S(1)} %get-tuple-element.53), channel_id=1, source_target_pairs={{0,4},{4,8},{8,12},{12,16},{16,20},{20,24},{24,28},{1,5},{5,9},{9,... | collective-permute-start | bytes 1769480 | tf_op jit(solution)/shard_map/ppermute | solution.py:308
  19.1 1.9 collective-permute-start.5
  21.1 1.9 spread.1.refs_3_.refs_4_
  22.9 5.3 %collective-permute-done.1.refs_2_ = bf16[4,4,144,128]{3,2,1,0:T(8,128)(2,1)S(1)} collective-permute-done((bf16[4,4,144,128]{3,2,1,0:T(8,128)(2,1)S(1)}, bf16[4,4,144,128]{3,2,1,0:T(8,128)(2,1)S(1)}, u32[]{:S(2)}, u32[]{:S(2)}) %collective-permute-start.1) | collective-permute-done | bytes 589856 | tf_op jit(solution)/shard_map/ppermute | solution.py:308
  28.2 4.2 %apply_first.2 = (f32[9,4,160,128]{3,2,1,0:T(8,128)S(1)}, bf16[4,4,144,128]{3,2,1,0:T(8,128)(2,1)S(1)}, bf16[4,4,144,128]{3,2,1,0:T(8,128)(2,1)S(1)}) custom-call(f32[9,4,160,128]{3,2,1,0:T(8,128)S(1)} %get-tuple-element.46.refs_0_.refs_1_, bf16[4,4,144,128]{3,2,1,0:T(8,128)(2,1)S(1)} %collective-permute-done.refs_1_, ...), custom_call_target="tpu_custom_call" | custom-call | bytes 16220160 | tf_op jit(solution)/shard_map/apply_first/pallas_call | solution.py:292
  32.5 1.9 collective-permute-start.2
  34.4 2.4 collective-permute-start.3
  36.8 4.0 %collective-permute-done.5.refs_2_ = bf16[4,4,144,128]{3,2,1,0:T(8,128)(2,1)S(1)} collective-permute-done((bf16[4,4,144,128]{3,2,1,0:T(8,128)(2,1)S(1)}, bf16[4,4,144,128]{3,2,1,0:T(8,128)(2,1)S(1)}, u32[]{:S(2)}, u32[]{:S(2)}) %collective-permute-start.5) | collective-permute-done | bytes 589856 | tf_op jit(solution)/shard_map/ppermute | solution.py:308
  40.9 4.2 %apply_first.3 = (f32[9,4,160,128]{3,2,1,0:T(8,128)S(1)}, bf16[4,4,144,128]{3,2,1,0:T(8,128)(2,1)S(1)}, bf16[4,4,144,128]{3,2,1,0:T(8,128)(2,1)S(1)}) custom-call(f32[9,4,160,128]{3,2,1,0:T(8,128)S(1)} %get-tuple-element.49.refs_4_.refs_0_.refs_1_, bf16[4,4,144,128]{3,2,1,0:T(8,128)(2,1)S(1)} %collective-permute-done.4.refs_1_, ...), custom_call_target="tpu_custom_call" | custom-call | bytes 16220160 | tf_op jit(solution)/shard_map/apply_first/pallas_call | solution.py:292
  45.1 1.9 collective-permute-start.8
  47.1 2.4 collective-permute-start.9
  49.5 4.0 %collective-permute-done.3.refs_3_ = bf16[4,4,144,128]{3,2,1,0:T(8,128)(2,1)S(1)} collective-permute-done((bf16[4,4,144,128]{3,2,1,0:T(8,128)(2,1)S(1)}, bf16[4,4,144,128]{3,2,1,0:T(8,128)(2,1)S(1)}, u32[]{:S(2)}, u32[]{:S(2)}) %collective-permute-start.3) | collective-permute-done | bytes 589856 | tf_op jit(solution)/shard_map/ppermute | solution.py:308
  53.5 4.3 %apply_middle.4 = (f32[9,4,160,128]{3,2,1,0:T(8,128)S(1)}, bf16[4,4,144,128]{3,2,1,0:T(8,128)(2,1)S(1)}, bf16[4,4,144,128]{3,2,1,0:T(8,128)(2,1)S(1)}) custom-call(f32[9,4,160,128]{3,2,1,0:T(8,128)S(1)} %get-tuple-element.50.refs_4_.refs_0_.refs_1_, f32[9,4,160,128]{3,2,1,0:T(8,128)S(1)} %get-tuple-element.46.refs_0_.refs_1_, ...), custom_call_target="tpu_custom_call" | custom-call | bytes 16220160 | tf_op jit(solution)/shard_map/apply_middle/pallas_call | solution.py:292
  57.8 1.9 collective-permute-start.6
  59.8 2.4 collective-permute-start.7
  62.2 4.0 %collective-permute-done.9.refs_3_ = bf16[4,4,144,128]{3,2,1,0:T(8,128)(2,1)S(1)} collective-permute-done((bf16[4,4,144,128]{3,2,1,0:T(8,128)(2,1)S(1)}, bf16[4,4,144,128]{3,2,1,0:T(8,128)(2,1)S(1)}, u32[]{:S(2)}, u32[]{:S(2)}) %collective-permute-start.9) | collective-permute-done | bytes 589856 | tf_op jit(solution)/shard_map/ppermute | solution.py:308
  66.2 4.3 %apply_middle.5 = (f32[9,4,160,128]{3,2,1,0:T(8,128)S(1)}, bf16[4,4,144,128]{3,2,1,0:T(8,128)(2,1)S(1)}, bf16[4,4,144,128]{3,2,1,0:T(8,128)(2,1)S(1)}) custom-call(f32[9,4,160,128]{3,2,1,0:T(8,128)S(1)} %get-tuple-element.55.refs_5_.refs_0_.refs_1_, f32[9,4,160,128]{3,2,1,0:T(8,128)S(1)} %get-tuple-element.49.refs_4_.refs_0_.refs_1_, ...), custom_call_target="tpu_custom_call" | custom-call | bytes 16220160 | tf_op jit(solution)/shard_map/apply_middle/pallas_call | solution.py:292
  70.5 1.9 collective-permute-start.12
  72.4 2.4 collective-permute-start.13
  74.8 4.0 %collective-permute-done.7.refs_3_ = bf16[4,4,144,128]{3,2,1,0:T(8,128)(2,1)S(1)} collective-permute-done((bf16[4,4,144,128]{3,2,1,0:T(8,128)(2,1)S(1)}, bf16[4,4,144,128]{3,2,1,0:T(8,128)(2,1)S(1)}, u32[]{:S(2)}, u32[]{:S(2)}) %collective-permute-start.7) | collective-permute-done | bytes 589856 | tf_op jit(solution)/shard_map/ppermute | solution.py:308
  78.8 4.3 %apply_middle.6 = (f32[9,4,160,128]{3,2,1,0:T(8,128)S(1)}, bf16[4,4,144,128]{3,2,1,0:T(8,128)(2,1)S(1)}, bf16[4,4,144,128]{3,2,1,0:T(8,128)(2,1)S(1)}) custom-call(f32[9,4,160,128]{3,2,1,0:T(8,128)S(1)} %get-tuple-element.56.refs_5_.refs_0_.refs_1_, f32[9,4,160,128]{3,2,1,0:T(8,128)S(1)} %get-tuple-element.50.refs_4_.refs_0_.refs_1_, ...), custom_call_target="tpu_custom_call" | custom-call | bytes 16220160 | tf_op jit(solution)/shard_map/apply_middle/pallas_call | solution.py:292
  83.1 1.9 collective-permute-start.10
  85.0 2.4 collective-permute-start.11
  87.5 4.0 %collective-permute-done.13.refs_3_ = bf16[4,4,144,128]{3,2,1,0:T(8,128)(2,1)S(1)} collective-permute-done((bf16[4,4,144,128]{3,2,1,0:T(8,128)(2,1)S(1)}, bf16[4,4,144,128]{3,2,1,0:T(8,128)(2,1)S(1)}, u32[]{:S(2)}, u32[]{:S(2)}) %collective-permute-start.13) | collective-permute-done | bytes 589856 | tf_op jit(solution)/shard_map/ppermute | solution.py:308
  91.4 4.3 %apply_middle.7 = (f32[9,4,160,128]{3,2,1,0:T(8,128)S(1)}, bf16[4,4,144,128]{3,2,1,0:T(8,128)(2,1)S(1)}, bf16[4,4,144,128]{3,2,1,0:T(8,128)(2,1)S(1)}) custom-call(f32[9,4,160,128]{3,2,1,0:T(8,128)S(1)} %get-tuple-element.61.refs_5_.refs_0_.refs_1_, f32[9,4,160,128]{3,2,1,0:T(8,128)S(1)} %get-tuple-element.55.refs_5_.refs_0_.refs_1_, ...), custom_call_target="tpu_custom_call" | custom-call | bytes 16220160 | tf_op jit(solution)/shard_map/apply_middle/pallas_call | solution.py:292
  95.8 1.9 collective-permute-start.14
  97.7 2.4 collective-permute-start.15
  100.1 4.0 %collective-permute-done.11.refs_3_ = bf16[4,4,144,128]{3,2,1,0:T(8,128)(2,1)S(1)} collective-permute-done((bf16[4,4,144,128]{3,2,1,0:T(8,128)(2,1)S(1)}, bf16[4,4,144,128]{3,2,1,0:T(8,128)(2,1)S(1)}, u32[]{:S(2)}, u32[]{:S(2)}) %collective-permute-start.11) | collective-permute-done | bytes 589856 | tf_op jit(solution)/shard_map/ppermute | solution.py:308
  104.1 5.3 %apply_last.2 = (f32[9,4,160,128]{3,2,1,0:T(8,128)S(1)}, bf16[4,4,144,128]{3,2,1,0:T(8,128)(2,1)S(1)}, bf16[4,4,144,128]{3,2,1,0:T(8,128)(2,1)S(1)}, bf16[9,4,80...) custom-call(f32[9,4,160,128]{3,2,1,0:T(8,128)S(1)} %get-tuple-element.62.refs_5_.refs_0_, ...), custom_call_target="tpu_custom_call" | custom-call | bytes 16220160 | tf_op jit(solution)/shard_map/apply_last/pallas_call | solution.py:292
  109.4 2.0 collective-permute-start.24
  111.4 3.3 %collective-permute-start.16 = (bf16[9,4,80,128]{3,2,1,0:T(8,128)(2,1)S(1)}, bf16[9,4,80,128]{3,2,1,0:T(8,128)(2,1)}, u32[]{:S(2)}, u32[]{:S(2)}) collective-permute-start(bf16[9,4,80,128]{3,2,1,0:T(8,128)(2,1)S(1)} %get-tuple-element.75), channel_id=1, source_target_pairs={{0,1},{1,2},{4,5},{5,6},{8,9},{9,10},{12,13},{13,14},{16,17},{17,1... | collective-permute-start | bytes 2211848 | tf_op jit(solution)/shard_map/ppermute | solution.py:411
  114.8 5.9 %apply_last.3 = (f32[9,4,160,128]{3,2,1,0:T(8,128)S(1)}, bf16[2,4,4,144,128]{4,3,2,1,0:T(8,128)(2,1)S(1)}, bf16[2,4,4,144,128]{4,3,2,1,0:T(8,128)(2,1)}, bf16[9,...) custom-call(f32[9,4,160,128]{3,2,1,0:T(8,128)S(1)} %get-tuple-element.67.refs_5_.refs_0_, ...), custom_call_target="tpu_custom_call" | custom-call | bytes 16220160 | tf_op jit(solution)/shard_map/apply_last/pallas_call | solution.py:292
  125.7 2.0 collective-permute-start.22
  127.8 2.4 collective-permute-start.23
  130.2 3.0 %collective-permute-start.18 = (bf16[9,4,80,128]{3,2,1,0:T(8,128)(2,1)}, bf16[9,4,80,128]{3,2,1,0:T(8,128)(2,1)S(1)}, u32[]{:S(2)}, u32[]{:S(2)}) collective-permute-start(bf16[9,4,80,128]{3,2,1,0:T(8,128)(2,1)} %copy-done.28), channel_id=1, source_target_pairs={{0,1},{1,2},{4,5},{5,6},{8,9},{9,10},{12,13},{13,14},{16,17},{17,1... | collective-permute-start | bytes 2211848 | tf_op jit(solution)/shard_map/ppermute | solution.py:411
  133.2 2.1 broadcast_select_fusion
  136.6 2.1 broadcast_select_fusion.3
  138.7 8.3 %collective-permute-start.17 = (bf16[9,4,80,128]{3,2,1,0:T(8,128)(2,1)}, bf16[9,4,80,128]{3,2,1,0:T(8,128)(2,1)}, u32[]{:S(2)}, u32[]{:S(2)}) collective-permute-start(bf16[9,4,80,128]{3,2,1,0:T(8,128)(2,1)} %broadcast_select_fusion.3), channel_id=1, source_target_pairs={{1,2},{2,3},{0,1},{5,6},{6,7},{4,5},{9,10},{10,11},{8,9},{13,14},{... | collective-permute-start | bytes 2211848 | tf_op jit(solution)/shard_map/ppermute | solution.py:411
  147.0 2.1 broadcast_select_fusion.1
  150.6 2.1 broadcast_select_fusion.2
  153.6 4.7 %collective-permute-start.19 = (bf16[9,4,80,128]{3,2,1,0:T(8,128)(2,1)}, bf16[9,4,80,128]{3,2,1,0:T(8,128)(2,1)}, u32[]{:S(2)}, u32[]{:S(2)}) collective-permute-start(bf16[9,4,80,128]{3,2,1,0:T(8,128)(2,1)} %broadcast_select_fusion.2), channel_id=1, source_target_pairs={{1,2},{2,3},{0,1},{5,6},{6,7},{4,5},{9,10},{10,11},{8,9},{13,14},{... | collective-permute-start | bytes 2211848 | tf_op jit(solution)/shard_map/ppermute | solution.py:411
  158.3 6.9 %collective-permute-done.17.refs_6_ = bf16[9,4,80,128]{3,2,1,0:T(8,128)(2,1)} collective-permute-done((bf16[9,4,80,128]{3,2,1,0:T(8,128)(2,1)}, bf16[9,4,80,128]{3,2,1,0:T(8,128)(2,1)}, u32[]{:S(2)}, u32[]{:S(2)}) %collective-permute-start.17) | collective-permute-done | bytes 737312 | tf_op jit(solution)/shard_map/ppermute | solution.py:411
  165.2 1.8 copy-done.1
  167.0 1.8 copy-done.4
  168.8 6.0 %apply_image.2 = (bf16[9,4,80,256]{3,2,1,0:T(8,128)(2,1)S(1)}, bf16[9,4,80,256]{3,2,1,0:T(8,128)(2,1)S(1)}, bf16[9,4,80,256]{3,2,1,0:T(8,128)(2,1)S(1)}) custom-call(s32[1]{0:T(128)} %bitcast.6.refs_0_, f32[9,4,160,128]{3,2,1,0:T(8,128)S(1)} %copy-done.1, bf16[2,4,4,144,128]{4,3,2,1,0:T(8,128)(2,1)} %collective-permute-done.22.refs_2_, ...), custom_call_target="tpu_custom_call" | custom-call | bytes 16220160 | tf_op jit(solution)/shard_map/apply_image/pallas_call | solution.py:292
  177.2 6.4 %apply_image.3 = (bf16[9,4,80,256]{3,2,1,0:T(8,128)(2,1)S(1)}, bf16[9,4,80,256]{3,2,1,0:T(8,128)(2,1)S(1)}, bf16[9,4,80,256]{3,2,1,0:T(8,128)(2,1)S(1)}) custom-call(s32[1]{0:T(128)} %bitcast.6.refs_0_, f32[9,4,160,128]{3,2,1,0:T(8,128)S(1)} %copy-done.5, bf16[2,4,4,144,128]{4,3,2,1,0:T(8,128)(2,1)} %collective-permute-done.22.refs_2_, ...), custom_call_target="tpu_custom_call" | custom-call | bytes 16220160 | tf_op jit(solution)/shard_map/apply_image/pallas_call | solution.py:292
  204.0 7.4 %gram.3.refs_10_ = f32[2,4,2,64,128]{4,3,2,1,0:T(8,128)S(1)} custom-call(s32[8]{0:T(128)S(1)} %stack.71.plan, bf16[2880,128]{1,0:T(8,128)(2,1)S(1)} %bitcast.84, bf16[2880,128]{1,0:T(8,128)(2,1)S(1)} %bitcast.85, bf16[2880,128]{1,0:T(8,128)(2,1)} %bitcast.23.refs_2_, bf16[2880,128]{1,0:T(8,128)(2,1)} %bitcast.24.refs_3_, bf16[2880,128]{1,0:T(8,128)(2,1)} %bitcast.25.refs_4_, ...), custom_call_target="tpu_custom_call" | custom-call | bytes 23592960 | tf_op jit(solution)/shard_map/gram/pallas_call | solution.py:367
  211.5 5.6 %gram.4.refs_2_.refs_8_ = f32[2,4,2,64,128]{4,3,2,1,0:T(8,128)S(1)} custom-call(s32[4]{0:T(128)S(1)} %pad_add_fusion.plan, bf16[2880,128]{1,0:T(8,128)(2,1)} %bitcast.5.refs_0_, bf16[2880,128]{1,0:T(8,128)(2,1)} %bitcast.7.refs_1_, bf16[2880,128]{1,0:T(8,128)(2,1)S(1)} %bitcast.87, bf16[2880,128]{1,0:T(8,128)(2,1)} %bitcast.9.refs_3_, ...), custom_call_target="tpu_custom_call" | custom-call | bytes 11796480 | tf_op jit(solution)/shard_map/gram/pallas_call | solution.py:367
  217.2 6.1 %unpack.1.refs_9_ = f32[9,128,1152]{2,1,0:T(8,128)} custom-call(f32[9,4,160,128]{3,2,1,0:T(8,128)S(1)} %copy-done.2, f32[9,4,160,128]{3,2,1,0:T(8,128)S(1)} %copy-done.6, f32[2,4,2,64,128]{4,3,2,1,0:T(8,128)S(1)} %gram.4.refs_2_.refs_8_), custom_call_target="tpu_custom_call" | custom-call | bytes 21233664 | tf_op jit(solution)/shard_map/unpack/pallas_call | solution.py:133
  223.3 1.8 collective-permute-done.28
  225.1 2.5 copy-done.12
  227.6 5.1 %gram.5 = f32[2,4,2,64,128]{4,3,2,1,0:T(8,128)S(1)} custom-call(s32[4]{0:T(128)S(1)} %pad_add_fusion.1.plan, bf16[2880,128]{1,0:T(8,128)(2,1)} %bitcast.34.refs_0_, bf16[2880,128]{1,0:T(8,128)(2,1)} %bitcast.35.refs_1_, bf16[2880,128]{1,0:T(8,128)(2,1)} %bitcast.36.refs_2_, bf16[2880,128]{1,0:T(8,128)(2,1)} %bitcast.37.refs_3_, ...), custom_call_target="tpu_custom_call" | custom-call | bytes 11796480 | tf_op jit(solution)/shard_map/gram/pallas_call | solution.py:367
  232.7 1.9 collective-permute-start.30
  236.1 4.5 %collective-permute-done.31 = f32[2,2,64,128]{3,2,1,0:T(8,128)S(1)} collective-permute-done((f32[2,2,64,128]{3,2,1,0:T(8,128)S(1)}, f32[2,2,64,128]{3,2,1,0:T(8,128)S(1)}, u32[]{:S(2)}, u32[]{:S(2)}) %collective-permute-start.31) | collective-permute-done | bytes 131104 | tf_op jit(solution)/shard_map/ppermute | solution.py:441
  240.8 3.1 %collective-permute-done.32 = f32[2,1,64,128]{3,2,1,0:T(8,128)S(1)} collective-permute-done((f32[2,1,64,128]{3,2,1,0:T(8,128)S(1)}, f32[2,1,64,128]{3,2,1,0:T(8,128)S(1)}, u32[]{:S(2)}, u32[]{:S(2)}) %collective-permute-start.32) | collective-permute-done | bytes 65568 | tf_op jit(solution)/shard_map/ppermute | solution.py:441
  243.9 8.3 %collective-permute-start.33 = (f32[2,64,64]{2,1,0:T(8,128)S(1)}, f32[2,64,64]{2,1,0:T(8,128)S(1)}, u32[]{:S(2)}, u32[]{:S(2)}) collective-permute-start(f32[2,64,64]{2,1,0:T(8,128)S(1)} %get-tuple-element.94), channel_id=1, source_target_pairs={{0,0},{1,8},{2,16},{3,24},{4,4},{5,12},{6,20},{7,28},{8,1},{9,9},{... | collective-permute-start | bytes 98312 | tf_op jit(solution)/shard_map/ppermute | solution.py:461
  252.3 2.0 collective-permute-start.34
  254.3 2.8 %collective-permute-done.33 = f32[2,64,64]{2,1,0:T(8,128)S(1)} collective-permute-done((f32[2,64,64]{2,1,0:T(8,128)S(1)}, f32[2,64,64]{2,1,0:T(8,128)S(1)}, u32[]{:S(2)}, u32[]{:S(2)}) %collective-permute-start.33) | collective-permute-done | bytes 32800 | tf_op jit(solution)/shard_map/ppermute | solution.py:461
  257.1 3.3 %collective-permute-done.34 = f32[2,64,64]{2,1,0:T(8,128)S(1)} collective-permute-done((f32[2,64,64]{2,1,0:T(8,128)S(1)}, f32[2,64,64]{2,1,0:T(8,128)S(1)}, u32[]{:S(2)}, u32[]{:S(2)}) %collective-permute-start.34) | collective-permute-done | bytes 32800 | tf_op jit(solution)/shard_map/ppermute | solution.py:461
  (120 shorter events, 34.2 us)
Async XLA Ops:
  0.6 2.5 copy-start.11
  5.9 15.1 %copy-start.36 = (f32[9,1152]{1,0:T(8,128)S(1)}, f32[9,1152]{1,0:T(8,128)}, u32[]{:S(2)}) copy-start(f32[9,1152]{1,0:T(8,128)} %param.3) | copy-start | bytes 124420
  5.9 17.0 %collective-permute-start = (bf16[4,4,144,128]{3,2,1,0:T(8,128)(2,1)S(1)}, bf16[4,4,144,128]{3,2,1,0:T(8,128)(2,1)S(1)}, u32[]{:S(2)}, u32[]{:S(2)}) collective-permute-start(bf16[4,4,144,128]{3,2,1,0:T(8,128)(2,1)S(1)} %get-tuple-element.47), channel_id=1, source_target_pairs={{0,4},{4,8},{8,12},{12,16},{16,20},{20,24},{24,28},{1,5},{5,9},{9,... | collective-permute-start | bytes 1769480 | tf_op jit(solution)/shard_map/ppermute | solution.py:308
  9.8 18.5 %collective-permute-start.1 = (bf16[4,4,144,128]{3,2,1,0:T(8,128)(2,1)S(1)}, bf16[4,4,144,128]{3,2,1,0:T(8,128)(2,1)S(1)}, u32[]{:S(2)}, u32[]{:S(2)}) collective-permute-start(bf16[4,4,144,128]{3,2,1,0:T(8,128)(2,1)S(1)} %get-tuple-element.48), channel_id=1, source_target_pairs={{4,0},{8,4},{12,8},{16,12},{20,16},{24,20},{28,24},{5,1},{9,5},{13... | collective-permute-start | bytes 1769480 | tf_op jit(solution)/shard_map/ppermute | solution.py:308
  14.5 22.3 %collective-permute-start.4 = (bf16[4,4,144,128]{3,2,1,0:T(8,128)(2,1)S(1)}, bf16[4,4,144,128]{3,2,1,0:T(8,128)(2,1)S(1)}, u32[]{:S(2)}, u32[]{:S(2)}) collective-permute-start(bf16[4,4,144,128]{3,2,1,0:T(8,128)(2,1)S(1)} %get-tuple-element.53), channel_id=1, source_target_pairs={{0,4},{4,8},{8,12},{12,16},{16,20},{20,24},{24,28},{1,5},{5,9},{9,... | collective-permute-start | bytes 1769480 | tf_op jit(solution)/shard_map/ppermute | solution.py:308
  19.1 21.8 %collective-permute-start.5 = (bf16[4,4,144,128]{3,2,1,0:T(8,128)(2,1)S(1)}, bf16[4,4,144,128]{3,2,1,0:T(8,128)(2,1)S(1)}, u32[]{:S(2)}, u32[]{:S(2)}) collective-permute-start(bf16[4,4,144,128]{3,2,1,0:T(8,128)(2,1)S(1)} %get-tuple-element.54), channel_id=1, source_target_pairs={{4,0},{8,4},{12,8},{16,12},{20,16},{24,20},{28,24},{5,1},{9,5},{13... | collective-permute-start | bytes 1769480 | tf_op jit(solution)/shard_map/ppermute | solution.py:308
  32.5 17.0 %collective-permute-start.2 = (bf16[4,4,144,128]{3,2,1,0:T(8,128)(2,1)S(1)}, bf16[4,4,144,128]{3,2,1,0:T(8,128)(2,1)S(1)}, u32[]{:S(2)}, u32[]{:S(2)}) collective-permute-start(bf16[4,4,144,128]{3,2,1,0:T(8,128)(2,1)S(1)} %get-tuple-element.51), channel_id=1, source_target_pairs={{0,4},{4,8},{8,12},{12,16},{16,20},{20,24},{24,28},{1,5},{5,9},{9,... | collective-permute-start | bytes 1769480 | tf_op jit(solution)/shard_map/ppermute | solution.py:308
  34.4 19.1 %collective-permute-start.3 = (bf16[4,4,144,128]{3,2,1,0:T(8,128)(2,1)S(1)}, bf16[4,4,144,128]{3,2,1,0:T(8,128)(2,1)S(1)}, u32[]{:S(2)}, u32[]{:S(2)}) collective-permute-start(bf16[4,4,144,128]{3,2,1,0:T(8,128)(2,1)S(1)} %get-tuple-element.52), channel_id=1, source_target_pairs={{4,0},{8,4},{12,8},{16,12},{20,16},{24,20},{28,24},{5,1},{9,5},{13... | collective-permute-start | bytes 1769480 | tf_op jit(solution)/shard_map/ppermute | solution.py:308
  45.1 17.0 %collective-permute-start.8 = (bf16[4,4,144,128]{3,2,1,0:T(8,128)(2,1)S(1)}, bf16[4,4,144,128]{3,2,1,0:T(8,128)(2,1)S(1)}, u32[]{:S(2)}, u32[]{:S(2)}) collective-permute-start(bf16[4,4,144,128]{3,2,1,0:T(8,128)(2,1)S(1)} %get-tuple-element.59), channel_id=1, source_target_pairs={{0,4},{4,8},{8,12},{12,16},{16,20},{20,24},{24,28},{1,5},{5,9},{9,... | collective-permute-start | bytes 1769480 | tf_op jit(solution)/shard_map/ppermute | solution.py:308
  47.1 19.1 %collective-permute-start.9 = (bf16[4,4,144,128]{3,2,1,0:T(8,128)(2,1)S(1)}, bf16[4,4,144,128]{3,2,1,0:T(8,128)(2,1)S(1)}, u32[]{:S(2)}, u32[]{:S(2)}) collective-permute-start(bf16[4,4,144,128]{3,2,1,0:T(8,128)(2,1)S(1)} %get-tuple-element.60), channel_id=1, source_target_pairs={{4,0},{8,4},{12,8},{16,12},{20,16},{24,20},{28,24},{5,1},{9,5},{13... | collective-permute-start | bytes 1769480 | tf_op jit(solution)/shard_map/ppermute | solution.py:308
  57.8 17.0 %collective-permute-start.6 = (bf16[4,4,144,128]{3,2,1,0:T(8,128)(2,1)S(1)}, bf16[4,4,144,128]{3,2,1,0:T(8,128)(2,1)S(1)}, u32[]{:S(2)}, u32[]{:S(2)}) collective-permute-start(bf16[4,4,144,128]{3,2,1,0:T(8,128)(2,1)S(1)} %get-tuple-element.57), channel_id=1, source_target_pairs={{0,4},{4,8},{8,12},{12,16},{16,20},{20,24},{24,28},{1,5},{5,9},{9,... | collective-permute-start | bytes 1769480 | tf_op jit(solution)/shard_map/ppermute | solution.py:308
  59.8 19.0 %collective-permute-start.7 = (bf16[4,4,144,128]{3,2,1,0:T(8,128)(2,1)S(1)}, bf16[4,4,144,128]{3,2,1,0:T(8,128)(2,1)S(1)}, u32[]{:S(2)}, u32[]{:S(2)}) collective-permute-start(bf16[4,4,144,128]{3,2,1,0:T(8,128)(2,1)S(1)} %get-tuple-element.58), channel_id=1, source_target_pairs={{4,0},{8,4},{12,8},{16,12},{20,16},{24,20},{28,24},{5,1},{9,5},{13... | collective-permute-start | bytes 1769480 | tf_op jit(solution)/shard_map/ppermute | solution.py:308
  70.5 17.0 %collective-permute-start.12 = (bf16[4,4,144,128]{3,2,1,0:T(8,128)(2,1)S(1)}, bf16[4,4,144,128]{3,2,1,0:T(8,128)(2,1)S(1)}, u32[]{:S(2)}, u32[]{:S(2)}) collective-permute-start(bf16[4,4,144,128]{3,2,1,0:T(8,128)(2,1)S(1)} %get-tuple-element.65), channel_id=1, source_target_pairs={{0,4},{4,8},{8,12},{12,16},{16,20},{20,24},{24,28},{1,5},{5,9},{9,... | collective-permute-start | bytes 1769480 | tf_op jit(solution)/shard_map/ppermute | solution.py:308
  72.4 19.0 %collective-permute-start.13 = (bf16[4,4,144,128]{3,2,1,0:T(8,128)(2,1)S(1)}, bf16[4,4,144,128]{3,2,1,0:T(8,128)(2,1)S(1)}, u32[]{:S(2)}, u32[]{:S(2)}) collective-permute-start(bf16[4,4,144,128]{3,2,1,0:T(8,128)(2,1)S(1)} %get-tuple-element.66), channel_id=1, source_target_pairs={{4,0},{8,4},{12,8},{16,12},{20,16},{24,20},{28,24},{5,1},{9,5},{13... | collective-permute-start | bytes 1769480 | tf_op jit(solution)/shard_map/ppermute | solution.py:308
  83.1 17.0 %collective-permute-start.10 = (bf16[4,4,144,128]{3,2,1,0:T(8,128)(2,1)S(1)}, bf16[4,4,144,128]{3,2,1,0:T(8,128)(2,1)S(1)}, u32[]{:S(2)}, u32[]{:S(2)}) collective-permute-start(bf16[4,4,144,128]{3,2,1,0:T(8,128)(2,1)S(1)} %get-tuple-element.63), channel_id=1, source_target_pairs={{0,4},{4,8},{8,12},{12,16},{16,20},{20,24},{24,28},{1,5},{5,9},{9,... | collective-permute-start | bytes 1769480 | tf_op jit(solution)/shard_map/ppermute | solution.py:308
  85.0 19.0 %collective-permute-start.11 = (bf16[4,4,144,128]{3,2,1,0:T(8,128)(2,1)S(1)}, bf16[4,4,144,128]{3,2,1,0:T(8,128)(2,1)S(1)}, u32[]{:S(2)}, u32[]{:S(2)}) collective-permute-start(bf16[4,4,144,128]{3,2,1,0:T(8,128)(2,1)S(1)} %get-tuple-element.64), channel_id=1, source_target_pairs={{4,0},{8,4},{12,8},{16,12},{20,16},{24,20},{28,24},{5,1},{9,5},{13... | collective-permute-start | bytes 1769480 | tf_op jit(solution)/shard_map/ppermute | solution.py:308
  95.8 19.0 %collective-permute-start.14 = (bf16[4,4,144,128]{3,2,1,0:T(8,128)(2,1)S(1)}, bf16[4,4,144,128]{3,2,1,0:T(8,128)(2,1)S(1)}, u32[]{:S(2)}, u32[]{:S(2)}) collective-permute-start(bf16[4,4,144,128]{3,2,1,0:T(8,128)(2,1)S(1)} %get-tuple-element.69), channel_id=1, source_target_pairs={{0,4},{4,8},{8,12},{12,16},{16,20},{20,24},{24,28},{1,5},{5,9},{9,... | collective-permute-start | bytes 1769480 | tf_op jit(solution)/shard_map/ppermute | solution.py:308
  97.7 17.1 %collective-permute-start.15 = (bf16[4,4,144,128]{3,2,1,0:T(8,128)(2,1)S(1)}, bf16[4,4,144,128]{3,2,1,0:T(8,128)(2,1)S(1)}, u32[]{:S(2)}, u32[]{:S(2)}) collective-permute-start(bf16[4,4,144,128]{3,2,1,0:T(8,128)(2,1)S(1)} %get-tuple-element.70), channel_id=1, source_target_pairs={{4,0},{8,4},{12,8},{16,12},{20,16},{24,20},{28,24},{5,1},{9,5},{13... | collective-permute-start | bytes 1769480 | tf_op jit(solution)/shard_map/ppermute | solution.py:308
  109.4 11.3 %copy-start = (f32[9,4,160,128]{3,2,1,0:T(8,128)}, f32[9,4,160,128]{3,2,1,0:T(8,128)S(1)}, u32[]{:S(2)}) copy-start(f32[9,4,160,128]{3,2,1,0:T(8,128)S(1)} %get-tuple-element.68.refs_5_.refs_1_.refs_0_) | copy-start | bytes 8847364
  109.4 23.8 %copy-start.26 = (bf16[9,4,80,128]{3,2,1,0:T(8,128)(2,1)}, bf16[9,4,80,128]{3,2,1,0:T(8,128)(2,1)S(1)}, u32[]{:S(2)}) copy-start(bf16[9,4,80,128]{3,2,1,0:T(8,128)(2,1)S(1)} %get-tuple-element.75) | copy-start | bytes 2211844
  109.4 20.8 %collective-permute-start.24 = (bf16[9,4,80,128]{3,2,1,0:T(8,128)(2,1)}, bf16[9,4,80,128]{3,2,1,0:T(8,128)(2,1)}, u32[]{:S(2)}, u32[]{:S(2)}) collective-permute-start(bf16[9,4,80,128]{3,2,1,0:T(8,128)(2,1)} %get-tuple-element.74), channel_id=1, source_target_pairs={{3,2},{2,1},{7,6},{6,5},{11,10},{10,9},{15,14},{14,13},{19,18},{18... | collective-permute-start | bytes 2211848 | tf_op jit(solution)/shard_map/ppermute | solution.py:412
  111.4 23.9 %collective-permute-start.16 = (bf16[9,4,80,128]{3,2,1,0:T(8,128)(2,1)S(1)}, bf16[9,4,80,128]{3,2,1,0:T(8,128)(2,1)}, u32[]{:S(2)}, u32[]{:S(2)}) collective-permute-start(bf16[9,4,80,128]{3,2,1,0:T(8,128)(2,1)S(1)} %get-tuple-element.75), channel_id=1, source_target_pairs={{0,1},{1,2},{4,5},{5,6},{8,9},{9,10},{12,13},{13,14},{16,17},{17,1... | collective-permute-start | bytes 2211848 | tf_op jit(solution)/shard_map/ppermute | solution.py:411
  120.7 1.6 copy-start.3
  124.2 14.5 %collective-permute-start.20 = (bf16[9,4,80,128]{3,2,1,0:T(8,128)(2,1)}, bf16[9,4,80,128]{3,2,1,0:T(8,128)(2,1)}, u32[]{:S(2)}, u32[]{:S(2)}) collective-permute-start(bf16[9,4,80,128]{3,2,1,0:T(8,128)(2,1)} %get-tuple-element.76), channel_id=1, source_target_pairs={{3,2},{2,1},{7,6},{6,5},{11,10},{10,9},{15,14},{14,13},{19,18},{18... | collective-permute-start | bytes 2211848 | tf_op jit(solution)/shard_map/ppermute | solution.py:412
  125.7 27.9 %collective-permute-start.22 = (bf16[2,4,4,144,128]{4,3,2,1,0:T(8,128)(2,1)}, bf16[2,4,4,144,128]{4,3,2,1,0:T(8,128)(2,1)}, u32[]{:S(2)}, u32[]{:S(2)}) collective-permute-start(bf16[2,4,4,144,128]{4,3,2,1,0:T(8,128)(2,1)} %get-tuple-element.78), channel_id=1, source_target_pairs={{0,4},{4,8},{8,12},{12,16},{16,20},{20,24},{24,28},{1,5},{5,9},{9,... | collective-permute-start | bytes 3538952 | tf_op jit(solution)/shard_map/ppermute | solution.py:308
  127.8 19.2 %copy-start.29 = (bf16[9,4,80,128]{3,2,1,0:T(8,128)(2,1)S(1)}, bf16[9,4,80,128]{3,2,1,0:T(8,128)(2,1)}, u32[]{:S(2)}) copy-start(bf16[9,4,80,128]{3,2,1,0:T(8,128)(2,1)} %copy-done.28) | copy-start | bytes 2211844
  127.8 30.5 %collective-permute-start.23 = (bf16[2,4,4,144,128]{4,3,2,1,0:T(8,128)(2,1)}, bf16[2,4,4,144,128]{4,3,2,1,0:T(8,128)(2,1)}, u32[]{:S(2)}, u32[]{:S(2)}) collective-permute-start(bf16[2,4,4,144,128]{4,3,2,1,0:T(8,128)(2,1)} %copy-done.35), channel_id=1, source_target_pairs={{4,0},{8,4},{12,8},{16,12},{20,16},{24,20},{28,24},{5,1},{9,5},{13... | collective-permute-start | bytes 3538952 | tf_op jit(solution)/shard_map/ppermute | solution.py:308
  130.2 19.1 %collective-permute-start.18 = (bf16[9,4,80,128]{3,2,1,0:T(8,128)(2,1)}, bf16[9,4,80,128]{3,2,1,0:T(8,128)(2,1)S(1)}, u32[]{:S(2)}, u32[]{:S(2)}) collective-permute-start(bf16[9,4,80,128]{3,2,1,0:T(8,128)(2,1)} %copy-done.28), channel_id=1, source_target_pairs={{0,1},{1,2},{4,5},{5,6},{8,9},{9,10},{12,13},{13,14},{16,17},{17,1... | collective-permute-start | bytes 2211848 | tf_op jit(solution)/shard_map/ppermute | solution.py:411
  135.3 23.0 %collective-permute-start.25 = (bf16[9,4,80,128]{3,2,1,0:T(8,128)(2,1)}, bf16[9,4,80,128]{3,2,1,0:T(8,128)(2,1)S(1)}, u32[]{:S(2)}, u32[]{:S(2)}) collective-permute-start(bf16[9,4,80,128]{3,2,1,0:T(8,128)(2,1)} %broadcast_select_fusion), channel_id=1, source_target_pairs={{2,1},{1,0},{3,2},{6,5},{5,4},{7,6},{10,9},{9,8},{11,10},{14,13},{... | collective-permute-start | bytes 2211848 | tf_op jit(solution)/shard_map/ppermute | solution.py:412
  138.7 26.5 %collective-permute-start.17 = (bf16[9,4,80,128]{3,2,1,0:T(8,128)(2,1)}, bf16[9,4,80,128]{3,2,1,0:T(8,128)(2,1)}, u32[]{:S(2)}, u32[]{:S(2)}) collective-permute-start(bf16[9,4,80,128]{3,2,1,0:T(8,128)(2,1)} %broadcast_select_fusion.3), channel_id=1, source_target_pairs={{1,2},{2,3},{0,1},{5,6},{6,7},{4,5},{9,10},{10,11},{8,9},{13,14},{... | collective-permute-start | bytes 2211848 | tf_op jit(solution)/shard_map/ppermute | solution.py:411
  149.4 37.7 %collective-permute-start.21 = (bf16[9,4,80,128]{3,2,1,0:T(8,128)(2,1)}, bf16[9,4,80,128]{3,2,1,0:T(8,128)(2,1)}, u32[]{:S(2)}, u32[]{:S(2)}) collective-permute-start(bf16[9,4,80,128]{3,2,1,0:T(8,128)(2,1)} %broadcast_select_fusion.1), channel_id=1, source_target_pairs={{2,1},{1,0},{3,2},{6,5},{5,4},{7,6},{10,9},{9,8},{11,10},{14,13},{... | collective-permute-start | bytes 2211848 | tf_op jit(solution)/shard_map/ppermute | solution.py:412
  153.6 33.5 %collective-permute-start.19 = (bf16[9,4,80,128]{3,2,1,0:T(8,128)(2,1)}, bf16[9,4,80,128]{3,2,1,0:T(8,128)(2,1)}, u32[]{:S(2)}, u32[]{:S(2)}) collective-permute-start(bf16[9,4,80,128]{3,2,1,0:T(8,128)(2,1)} %broadcast_select_fusion.2), channel_id=1, source_target_pairs={{1,2},{2,3},{0,1},{5,6},{6,7},{4,5},{9,10},{10,11},{8,9},{13,14},{... | collective-permute-start | bytes 2211848 | tf_op jit(solution)/shard_map/ppermute | solution.py:411
  158.3 16.5 %copy-start.33 = (bf16[9,4,80,128]{3,2,1,0:T(8,128)(2,1)}, bf16[9,4,80,128]{3,2,1,0:T(8,128)(2,1)S(1)}, u32[]{:S(2)}) copy-start(bf16[9,4,80,128]{3,2,1,0:T(8,128)(2,1)S(1)} %collective-permute-done.25.refs_7_) | copy-start | bytes 2211844
  165.2 1.8 copy-start.1
  167.0 1.8 copy-start.4
  168.8 8.3 %copy-start.5 = (f32[9,4,160,128]{3,2,1,0:T(8,128)S(1)}, f32[9,4,160,128]{3,2,1,0:T(8,128)}, u32[]{:S(2)}) copy-start(f32[9,4,160,128]{3,2,1,0:T(8,128)} %copy-done.3) | copy-start | bytes 8847364
  174.8 1.2 copy-start.13
  177.2 6.4 %copy-start.7 = (bf16[9,4,80,256]{3,2,1,0:T(8,128)(2,1)}, bf16[9,4,80,256]{3,2,1,0:T(8,128)(2,1)S(1)}, u32[]{:S(2)}) copy-start(bf16[9,4,80,256]{3,2,1,0:T(8,128)(2,1)S(1)} %get-tuple-element.80.refs_5_) | copy-start | bytes 4423684
  183.5 1.2 copy-start.9
  184.7 1.2 copy-start.16
  185.9 1.2 copy-start.22
  187.1 7.0 %copy-start.8 = (bf16[9,4,80,256]{3,2,1,0:T(8,128)(2,1)S(1)}, bf16[9,4,80,256]{3,2,1,0:T(8,128)(2,1)}, u32[]{:S(2)}) copy-start(bf16[9,4,80,256]{3,2,1,0:T(8,128)(2,1)} %copy-done.7) | copy-start | bytes 4423684
  187.1 7.0 %copy-start.10 = (bf16[9,4,80,256]{3,2,1,0:T(8,128)(2,1)S(1)}, bf16[9,4,80,256]{3,2,1,0:T(8,128)(2,1)}, u32[]{:S(2)}) copy-start(bf16[9,4,80,256]{3,2,1,0:T(8,128)(2,1)} %copy-done.9) | copy-start | bytes 4423684
  188.0 35.2 %collective-permute-start.27 = (bf16[9,4,80,128]{3,2,1,0:T(8,128)(2,1)}, bf16[9,4,80,128]{3,2,1,0:T(8,128)(2,1)}, u32[]{:S(2)}, u32[]{:S(2)}) collective-permute-start(bf16[9,4,80,128]{3,2,1,0:T(8,128)(2,1)} %get-tuple-element.82), channel_id=1, source_target_pairs={{2,3},{6,7},{10,11},{14,15},{18,19},{22,23},{26,27},{30,31}} | collective-permute-start | bytes 2211848 | tf_op jit(solution)/shard_map/ppermute | solution.py:411
  189.7 33.6 %collective-permute-start.29 = (bf16[9,4,80,128]{3,2,1,0:T(8,128)(2,1)}, bf16[9,4,80,128]{3,2,1,0:T(8,128)(2,1)}, u32[]{:S(2)}, u32[]{:S(2)}) collective-permute-start(bf16[9,4,80,128]{3,2,1,0:T(8,128)(2,1)} %get-tuple-element.83), channel_id=1, source_target_pairs={{1,0},{5,4},{9,8},{13,12},{17,16},{21,20},{25,24},{29,28}} | collective-permute-start | bytes 2211848 | tf_op jit(solution)/shard_map/ppermute | solution.py:412
  191.0 34.1 %collective-permute-start.28 = (bf16[9,4,80,128]{3,2,1,0:T(8,128)(2,1)}, bf16[9,4,80,128]{3,2,1,0:T(8,128)(2,1)}, u32[]{:S(2)}, u32[]{:S(2)}) collective-permute-start(bf16[9,4,80,128]{3,2,1,0:T(8,128)(2,1)} %copy-done.33), channel_id=1, source_target_pairs={{1,0},{5,4},{9,8},{13,12},{17,16},{21,20},{25,24},{29,28}} | collective-permute-start | bytes 2211848 | tf_op jit(solution)/shard_map/ppermute | solution.py:412
  192.3 32.8 %collective-permute-start.26 = (bf16[9,4,80,128]{3,2,1,0:T(8,128)(2,1)}, bf16[9,4,80,128]{3,2,1,0:T(8,128)(2,1)}, u32[]{:S(2)}, u32[]{:S(2)}) collective-permute-start(bf16[9,4,80,128]{3,2,1,0:T(8,128)(2,1)} %collective-permute-done.17.refs_6_), channel_id=1, source_target_pairs={{2,3},{6,7},{10,11},{14,15},{18,19},{22,23},{26,27},{30,31}} | collective-permute-start | bytes 2211848 | tf_op jit(solution)/shard_map/ppermute | solution.py:411
  194.1 1.4 copy-start.14
  195.4 1.4 copy-start.17
  196.8 1.4 copy-start.20
  198.2 1.4 copy-start.23
  204.0 7.5 %copy-start.15 = (bf16[9,4,80,256]{3,2,1,0:T(8,128)(2,1)S(1)}, bf16[9,4,80,256]{3,2,1,0:T(8,128)(2,1)}, u32[]{:S(2)}) copy-start(bf16[9,4,80,256]{3,2,1,0:T(8,128)(2,1)} %copy-done.13) | copy-start | bytes 4423684
  204.0 7.5 %copy-start.18 = (bf16[9,4,80,256]{3,2,1,0:T(8,128)(2,1)S(1)}, bf16[9,4,80,256]{3,2,1,0:T(8,128)(2,1)}, u32[]{:S(2)}) copy-start(bf16[9,4,80,256]{3,2,1,0:T(8,128)(2,1)} %copy-done.16) | copy-start | bytes 4423684
  204.0 7.5 %copy-start.21 = (bf16[9,4,80,256]{3,2,1,0:T(8,128)(2,1)S(1)}, bf16[9,4,80,256]{3,2,1,0:T(8,128)(2,1)}, u32[]{:S(2)}) copy-start(bf16[9,4,80,256]{3,2,1,0:T(8,128)(2,1)} %copy-done.19) | copy-start | bytes 4423684
  204.0 7.5 %copy-start.24 = (bf16[9,4,80,256]{3,2,1,0:T(8,128)(2,1)S(1)}, bf16[9,4,80,256]{3,2,1,0:T(8,128)(2,1)}, u32[]{:S(2)}) copy-start(bf16[9,4,80,256]{3,2,1,0:T(8,128)(2,1)} %copy-done.22) | copy-start | bytes 4423684
  204.0 7.5 %copy-start.34 = (bf16[9,4,80,128]{3,2,1,0:T(8,128)(2,1)S(1)}, bf16[9,4,80,128]{3,2,1,0:T(8,128)(2,1)}, u32[]{:S(2)}) copy-start(bf16[9,4,80,128]{3,2,1,0:T(8,128)(2,1)} %copy-done.33) | copy-start | bytes 2211844
  211.5 5.7 %copy-start.2 = (f32[9,4,160,128]{3,2,1,0:T(8,128)S(1)}, f32[9,4,160,128]{3,2,1,0:T(8,128)}, u32[]{:S(2)}) copy-start(f32[9,4,160,128]{3,2,1,0:T(8,128)} %copy-done) | copy-start | bytes 8847364
  211.5 5.7 %copy-start.6 = (f32[9,4,160,128]{3,2,1,0:T(8,128)S(1)}, f32[9,4,160,128]{3,2,1,0:T(8,128)}, u32[]{:S(2)}) copy-start(f32[9,4,160,128]{3,2,1,0:T(8,128)} %copy-done.3) | copy-start | bytes 8847364
  225.1 2.5 copy-start.12
  232.7 3.0 %collective-permute-start.30 = (f32[2,4,64,128]{3,2,1,0:T(8,128)S(1)}, f32[2,4,64,128]{3,2,1,0:T(8,128)S(1)}, u32[]{:S(2)}, u32[]{:S(2)}) collective-permute-start(f32[2,4,64,128]{3,2,1,0:T(8,128)S(1)} %dynamic-slice_bitcast_fusion), channel_id=1, source_target_pairs={{0,4},{4,0},{8,12},{12,8},{16,20},{20,16},{24,28},{28,24},{1,5},{5... | collective-permute-start | bytes 786440 | tf_op jit(solution)/shard_map/ppermute | solution.py:441
  235.8 4.8 %collective-permute-start.31 = (f32[2,2,64,128]{3,2,1,0:T(8,128)S(1)}, f32[2,2,64,128]{3,2,1,0:T(8,128)S(1)}, u32[]{:S(2)}, u32[]{:S(2)}) collective-permute-start(f32[2,2,64,128]{3,2,1,0:T(8,128)S(1)} %dynamic-slice_bitcast_fusion.1), channel_id=1, source_target_pairs={{0,8},{4,12},{8,0},{12,4},{16,24},{20,28},{24,16},{28,20},{1,9},{5... | collective-permute-start | bytes 393224 | tf_op jit(solution)/shard_map/ppermute | solution.py:441
  240.6 3.2 %collective-permute-start.32 = (f32[2,1,64,128]{3,2,1,0:T(8,128)S(1)}, f32[2,1,64,128]{3,2,1,0:T(8,128)S(1)}, u32[]{:S(2)}, u32[]{:S(2)}) collective-permute-start(f32[2,1,64,128]{3,2,1,0:T(8,128)S(1)} %constant_dynamic-slice_fusion), channel_id=1, source_target_pairs={{0,16},{4,20},{8,24},{12,28},{16,0},{20,4},{24,8},{28,12},{1,17},{... | collective-permute-start | bytes 196616 | tf_op jit(solution)/shard_map/ppermute | solution.py:441
  243.9 13.2 %collective-permute-start.33 = (f32[2,64,64]{2,1,0:T(8,128)S(1)}, f32[2,64,64]{2,1,0:T(8,128)S(1)}, u32[]{:S(2)}, u32[]{:S(2)}) collective-permute-start(f32[2,64,64]{2,1,0:T(8,128)S(1)} %get-tuple-element.94), channel_id=1, source_target_pairs={{0,0},{1,8},{2,16},{3,24},{4,4},{5,12},{6,20},{7,28},{8,1},{9,9},{... | collective-permute-start | bytes 98312 | tf_op jit(solution)/shard_map/ppermute | solution.py:461
  252.3 8.1 %collective-permute-start.34 = (f32[2,64,64]{2,1,0:T(8,128)S(1)}, f32[2,64,64]{2,1,0:T(8,128)S(1)}, u32[]{:S(2)}, u32[]{:S(2)}) collective-permute-start(f32[2,64,64]{2,1,0:T(8,128)S(1)} %get-tuple-element.93), channel_id=1, source_target_pairs={{0,4},{1,12},{2,20},{3,28},{4,0},{5,8},{6,16},{7,24},{8,5},{9,13},... | collective-permute-start | bytes 98312 | tf_op jit(solution)/shard_map/ppermute | solution.py:461
  (8 other events, 8.3 us)

commit v2 on v1

--- a/solution.py
+++ b/solution.py
@@ -15,7 +15,7 @@
 PART = 80
 FIRST_B = NZ - PART
 SMALL_LIMIT = 6 << 20
-GRAM_LIMIT = 10 << 20
+GRAM_LIMIT = 56 << 20
 
 coeffs = (-205.0 / 72.0, 8.0 / 5.0, -1.0 / 5.0, 8.0 / 315.0, -1.0 / 560.0)
 kinetic = -0.5 / 0.09
@@ -358,7 +358,7 @@
 
 def gram(blocks, kinds, plan, rights, sums, after=()):
     chunks = len(rights)
-    steps = 6
+    steps = 3
     flat = [block.reshape(-1, 128) for block in blocks]
     used = sorted({kind for choices in kinds for kind in choices})
     right = [three[kind].reshape(-1, 256) for three in rights for kind in used]
@@ -431,16 +431,17 @@
 def summed_over_domain(table):
     count = lax.axis_size("domain")
     me = lax.axis_index("domain")
-    bit = 1
-    table = table.reshape(2, count, table.shape[1] // count, table.shape[2])
-    while bit < count:
-        groups = table.reshape((2, table.shape[1] // 2, 2) + table.shape[2:])
-        mine = lax.rem(me // bit, 2)
-        keep = lax.dynamic_index_in_dim(groups, mine, axis=2, keepdims=False)
-        send = lax.dynamic_index_in_dim(groups, 1 - mine, axis=2, keepdims=False)
-        table = keep + lax.ppermute(send, "domain", [(i, i ^ bit) for i in range(count)])
-        bit *= 2
-    return table[:, 0]
+    table = table.reshape(2, count // 2, 2, table.shape[1] // count, table.shape[2])
+    mine = lax.rem(me, 2)
+    keep = lax.dynamic_index_in_dim(table, mine, axis=2, keepdims=False)
+    send = lax.dynamic_index_in_dim(table, 1 - mine, axis=2, keepdims=False)
+    table = keep + lax.ppermute(send, "domain", [(i, i ^ 1) for i in range(count)])
+    total = lax.dynamic_index_in_dim(table, me // 2, axis=1, keepdims=False)
+    for other in range(1, count // 2):
+        send = lax.dynamic_index_in_dim(table, (me // 2) ^ other, axis=1, keepdims=False)
+        pairs = [(i, i ^ (2 * other)) for i in range(count)]
+        total = total + lax.ppermute(send, "domain", pairs)
+    return total
 
 
 def other_triangle(table):

time: 264 us -> 257 us (0.973)
  local copies, waits for them, and re-layouts: 30.8 us -> 19.8 us
  Pallas kernels: 81 us -> 85.2 us
    unnamed x74 -> x48, local copies, waits for them, and re-layouts: 28.8 us -> 16.4 us
    ppermute x3 -> x4, waiting for transfers between devices: 8.74 us -> 2.87 us  [the longest x3 1.71 us: summed_over_domain(): total = total + lax.ppermute(send, 'domain', pairs)]
    pallas_call x3, Pallas kernels: 18.2 us -> 22.4 us  [gram(): pl.pallas_call(functools.partial(gram_kernel, kinds, used, chunks), grid=...]
    ppermute x6, waiting for transfers between devices: 1.84 us -> 6.05 us  [hop_move(): lax.ppermute(down, 'band', [(bands - b, bands - 1 - b) for b in pairs])]
    ppermute x2, starting transfers between devices: 10.4 us -> 6.54 us  [other_triangle(): lax.ppermute(block, ('domain', 'band'), pairs).transpose(0, 2, 1)]
  transfers between devices with their start and end apart: 35 -> 36, of which waited for: 15 -> 15; matrix products, arithmetic and copies ran while one was open for 3% -> 4% of each run, Pallas kernels for 28% -> 30%
where the time goes in v2:
time: 257 us; the launch traced here: 256 us
  Pallas kernels  85.2 us (33%)
  starting transfers between devices  84.2 us (33%)
  waiting for transfers between devices  54.7 us (21%)
  local copies, waits for them, and re-layouts  19.8 us (8%)
  other arithmetic  10.6 us (4%)
    pallas_call x10, Pallas kernels, apply_op(): pl.pallas_call(functools.partial(apply_kernel, mode, len(after), bool(ear...  49.2 us
    ppermute x9, waiting for transfers between devices, exchange(): lax.ppermute(below, 'domain', down)  29.3 us
    pallas_call x3, Pallas kernels, gram(): pl.pallas_call(functools.partial(gram_kernel, kinds, used, chunks), grid=...  22.4 us
    ppermute x9, starting transfers between devices, exchange(): lax.ppermute(above, 'domain', up)  21.9 us
    ppermute x6, starting transfers between devices, hop_move(): up = lax.ppermute(up, 'band', [(b - 1, b) for b in pairs])  21.8 us
    ppermute x9, starting transfers between devices, exchange(): lax.ppermute(below, 'domain', down)  20.7 us
    unnamed x48, local copies, waits for them, and re-layouts  16.4 us
    ppermute x6, starting transfers between devices, hop_move(): lax.ppermute(down, 'band', [(bands - b, bands - 1 - b) for b in pairs])  8.68 us
  transfers between devices with their start and end apart: 36, of which 15 were waited for; matrix products, arithmetic and copies ran while one was open for 4% of the time, Pallas kernels for 30%

profile of v2, /device:TPU:3, one launch (start us, length us, event | category | flops | bytes accessed | tf_op | source)
XLA Modules:
  0.0 255.7 jit_solution(6301218922089246802)
XLA Ops:
  0.6 2.5 copy-done.9
  3.1 2.8 %pack.2 = (f32[9,4,160,128]{3,2,1,0:T(8,128)S(1)}, bf16[4,4,144,128]{3,2,1,0:T(8,128)(2,1)S(1)}, bf16[4,4,144,128]{3,2,1,0:T(8,128)(2,1)S(1)}) custom-call(f32[9,128,1152]{2,1,0:T(8,128)S(1)} %bitcast.72), custom_call_target="tpu_custom_call" | custom-call | bytes 10616832 | tf_op jit(solution)/shard_map/pack/pallas_call | solution.py:97
  5.9 3.8 %collective-permute-start = (bf16[4,4,144,128]{3,2,1,0:T(8,128)(2,1)S(1)}, bf16[4,4,144,128]{3,2,1,0:T(8,128)(2,1)S(1)}, u32[]{:S(2)}, u32[]{:S(2)}) collective-permute-start(bf16[4,4,144,128]{3,2,1,0:T(8,128)(2,1)S(1)} %get-tuple-element.47), channel_id=1, source_target_pairs={{0,4},{4,8},{8,12},{12,16},{16,20},{20,24},{24,28},{1,5},{5,9},{9,... | collective-permute-start | bytes 1769480 | tf_op jit(solution)/shard_map/ppermute | solution.py:308
  9.8 1.9 collective-permute-start.1
  11.7 2.8 %pack.3 = (f32[9,4,160,128]{3,2,1,0:T(8,128)S(1)}, bf16[4,4,144,128]{3,2,1,0:T(8,128)(2,1)S(1)}, bf16[4,4,144,128]{3,2,1,0:T(8,128)(2,1)S(1)}) custom-call(f32[9,128,1152]{2,1,0:T(8,128)S(1)} %bitcast.73), custom_call_target="tpu_custom_call" | custom-call | bytes 10616832 | tf_op jit(solution)/shard_map/pack/pallas_call | solution.py:97
  14.5 4.5 %collective-permute-start.4 = (bf16[4,4,144,128]{3,2,1,0:T(8,128)(2,1)S(1)}, bf16[4,4,144,128]{3,2,1,0:T(8,128)(2,1)S(1)}, u32[]{:S(2)}, u32[]{:S(2)}) collective-permute-start(bf16[4,4,144,128]{3,2,1,0:T(8,128)(2,1)S(1)} %get-tuple-element.53), channel_id=1, source_target_pairs={{0,4},{4,8},{8,12},{12,16},{16,20},{20,24},{24,28},{1,5},{5,9},{9,... | collective-permute-start | bytes 1769480 | tf_op jit(solution)/shard_map/ppermute | solution.py:308
  19.1 1.9 collective-permute-start.5
  21.1 1.9 spread.1.refs_3_.refs_4_
  22.9 5.3 %collective-permute-done.1.refs_2_ = bf16[4,4,144,128]{3,2,1,0:T(8,128)(2,1)S(1)} collective-permute-done((bf16[4,4,144,128]{3,2,1,0:T(8,128)(2,1)S(1)}, bf16[4,4,144,128]{3,2,1,0:T(8,128)(2,1)S(1)}, u32[]{:S(2)}, u32[]{:S(2)}) %collective-permute-start.1) | collective-permute-done | bytes 589856 | tf_op jit(solution)/shard_map/ppermute | solution.py:308
  28.2 4.2 %apply_first.2 = (f32[9,4,160,128]{3,2,1,0:T(8,128)S(1)}, bf16[4,4,144,128]{3,2,1,0:T(8,128)(2,1)S(1)}, bf16[4,4,144,128]{3,2,1,0:T(8,128)(2,1)S(1)}) custom-call(f32[9,4,160,128]{3,2,1,0:T(8,128)S(1)} %get-tuple-element.46.refs_0_.refs_1_, bf16[4,4,144,128]{3,2,1,0:T(8,128)(2,1)S(1)} %collective-permute-done.refs_1_, ...), custom_call_target="tpu_custom_call" | custom-call | bytes 16220160 | tf_op jit(solution)/shard_map/apply_first/pallas_call | solution.py:292
  32.5 1.9 collective-permute-start.2
  34.4 2.4 collective-permute-start.3
  36.8 4.0 %collective-permute-done.5.refs_2_ = bf16[4,4,144,128]{3,2,1,0:T(8,128)(2,1)S(1)} collective-permute-done((bf16[4,4,144,128]{3,2,1,0:T(8,128)(2,1)S(1)}, bf16[4,4,144,128]{3,2,1,0:T(8,128)(2,1)S(1)}, u32[]{:S(2)}, u32[]{:S(2)}) %collective-permute-start.5) | collective-permute-done | bytes 589856 | tf_op jit(solution)/shard_map/ppermute | solution.py:308
  40.9 4.2 %apply_first.3 = (f32[9,4,160,128]{3,2,1,0:T(8,128)S(1)}, bf16[4,4,144,128]{3,2,1,0:T(8,128)(2,1)S(1)}, bf16[4,4,144,128]{3,2,1,0:T(8,128)(2,1)S(1)}) custom-call(f32[9,4,160,128]{3,2,1,0:T(8,128)S(1)} %get-tuple-element.49.refs_4_.refs_0_.refs_1_, bf16[4,4,144,128]{3,2,1,0:T(8,128)(2,1)S(1)} %collective-permute-done.4.refs_1_, ...), custom_call_target="tpu_custom_call" | custom-call | bytes 16220160 | tf_op jit(solution)/shard_map/apply_first/pallas_call | solution.py:292
  45.1 1.9 collective-permute-start.8
  47.1 2.4 collective-permute-start.9
  49.5 4.0 %collective-permute-done.3.refs_3_ = bf16[4,4,144,128]{3,2,1,0:T(8,128)(2,1)S(1)} collective-permute-done((bf16[4,4,144,128]{3,2,1,0:T(8,128)(2,1)S(1)}, bf16[4,4,144,128]{3,2,1,0:T(8,128)(2,1)S(1)}, u32[]{:S(2)}, u32[]{:S(2)}) %collective-permute-start.3) | collective-permute-done | bytes 589856 | tf_op jit(solution)/shard_map/ppermute | solution.py:308
  53.5 4.3 %apply_middle.4 = (f32[9,4,160,128]{3,2,1,0:T(8,128)S(1)}, bf16[4,4,144,128]{3,2,1,0:T(8,128)(2,1)S(1)}, bf16[4,4,144,128]{3,2,1,0:T(8,128)(2,1)S(1)}) custom-call(f32[9,4,160,128]{3,2,1,0:T(8,128)S(1)} %get-tuple-element.50.refs_4_.refs_0_.refs_1_, f32[9,4,160,128]{3,2,1,0:T(8,128)S(1)} %get-tuple-element.46.refs_0_.refs_1_, ...), custom_call_target="tpu_custom_call" | custom-call | bytes 16220160 | tf_op jit(solution)/shard_map/apply_middle/pallas_call | solution.py:292
  57.8 1.9 collective-permute-start.6
  59.8 2.4 collective-permute-start.7
  62.2 4.0 %collective-permute-done.9.refs_3_ = bf16[4,4,144,128]{3,2,1,0:T(8,128)(2,1)S(1)} collective-permute-done((bf16[4,4,144,128]{3,2,1,0:T(8,128)(2,1)S(1)}, bf16[4,4,144,128]{3,2,1,0:T(8,128)(2,1)S(1)}, u32[]{:S(2)}, u32[]{:S(2)}) %collective-permute-start.9) | collective-permute-done | bytes 589856 | tf_op jit(solution)/shard_map/ppermute | solution.py:308
  66.2 4.3 %apply_middle.5 = (f32[9,4,160,128]{3,2,1,0:T(8,128)S(1)}, bf16[4,4,144,128]{3,2,1,0:T(8,128)(2,1)S(1)}, bf16[4,4,144,128]{3,2,1,0:T(8,128)(2,1)S(1)}) custom-call(f32[9,4,160,128]{3,2,1,0:T(8,128)S(1)} %get-tuple-element.55.refs_5_.refs_0_.refs_1_, f32[9,4,160,128]{3,2,1,0:T(8,128)S(1)} %get-tuple-element.49.refs_4_.refs_0_.refs_1_, ...), custom_call_target="tpu_custom_call" | custom-call | bytes 16220160 | tf_op jit(solution)/shard_map/apply_middle/pallas_call | solution.py:292
  70.5 1.9 collective-permute-start.12
  72.4 2.4 collective-permute-start.13
  74.8 4.0 %collective-permute-done.7.refs_3_ = bf16[4,4,144,128]{3,2,1,0:T(8,128)(2,1)S(1)} collective-permute-done((bf16[4,4,144,128]{3,2,1,0:T(8,128)(2,1)S(1)}, bf16[4,4,144,128]{3,2,1,0:T(8,128)(2,1)S(1)}, u32[]{:S(2)}, u32[]{:S(2)}) %collective-permute-start.7) | collective-permute-done | bytes 589856 | tf_op jit(solution)/shard_map/ppermute | solution.py:308
  78.8 4.3 %apply_middle.6 = (f32[9,4,160,128]{3,2,1,0:T(8,128)S(1)}, bf16[4,4,144,128]{3,2,1,0:T(8,128)(2,1)S(1)}, bf16[4,4,144,128]{3,2,1,0:T(8,128)(2,1)S(1)}) custom-call(f32[9,4,160,128]{3,2,1,0:T(8,128)S(1)} %get-tuple-element.56.refs_5_.refs_0_.refs_1_, f32[9,4,160,128]{3,2,1,0:T(8,128)S(1)} %get-tuple-element.50.refs_4_.refs_0_.refs_1_, ...), custom_call_target="tpu_custom_call" | custom-call | bytes 16220160 | tf_op jit(solution)/shard_map/apply_middle/pallas_call | solution.py:292
  83.1 1.9 collective-permute-start.10
  85.0 2.4 collective-permute-start.11
  87.5 4.0 %collective-permute-done.13.refs_3_ = bf16[4,4,144,128]{3,2,1,0:T(8,128)(2,1)S(1)} collective-permute-done((bf16[4,4,144,128]{3,2,1,0:T(8,128)(2,1)S(1)}, bf16[4,4,144,128]{3,2,1,0:T(8,128)(2,1)S(1)}, u32[]{:S(2)}, u32[]{:S(2)}) %collective-permute-start.13) | collective-permute-done | bytes 589856 | tf_op jit(solution)/shard_map/ppermute | solution.py:308
  91.4 4.3 %apply_middle.7 = (f32[9,4,160,128]{3,2,1,0:T(8,128)S(1)}, bf16[4,4,144,128]{3,2,1,0:T(8,128)(2,1)S(1)}, bf16[4,4,144,128]{3,2,1,0:T(8,128)(2,1)S(1)}) custom-call(f32[9,4,160,128]{3,2,1,0:T(8,128)S(1)} %get-tuple-element.61.refs_5_.refs_0_.refs_1_, f32[9,4,160,128]{3,2,1,0:T(8,128)S(1)} %get-tuple-element.55.refs_5_.refs_0_.refs_1_, ...), custom_call_target="tpu_custom_call" | custom-call | bytes 16220160 | tf_op jit(solution)/shard_map/apply_middle/pallas_call | solution.py:292
  95.8 1.9 collective-permute-start.14
  97.7 2.4 collective-permute-start.15
  100.1 4.0 %collective-permute-done.11.refs_3_ = bf16[4,4,144,128]{3,2,1,0:T(8,128)(2,1)S(1)} collective-permute-done((bf16[4,4,144,128]{3,2,1,0:T(8,128)(2,1)S(1)}, bf16[4,4,144,128]{3,2,1,0:T(8,128)(2,1)S(1)}, u32[]{:S(2)}, u32[]{:S(2)}) %collective-permute-start.11) | collective-permute-done | bytes 589856 | tf_op jit(solution)/shard_map/ppermute | solution.py:308
  104.1 5.3 %apply_last.2 = (f32[9,4,160,128]{3,2,1,0:T(8,128)S(1)}, bf16[4,4,144,128]{3,2,1,0:T(8,128)(2,1)S(1)}, bf16[4,4,144,128]{3,2,1,0:T(8,128)(2,1)S(1)}, bf16[9,4,80...) custom-call(f32[9,4,160,128]{3,2,1,0:T(8,128)S(1)} %get-tuple-element.62.refs_5_.refs_0_, ...), custom_call_target="tpu_custom_call" | custom-call | bytes 16220160 | tf_op jit(solution)/shard_map/apply_last/pallas_call | solution.py:292
  109.4 2.0 collective-permute-start.24
  111.4 3.4 %collective-permute-start.16 = (bf16[9,4,80,128]{3,2,1,0:T(8,128)(2,1)S(1)}, bf16[9,4,80,128]{3,2,1,0:T(8,128)(2,1)}, u32[]{:S(2)}, u32[]{:S(2)}) collective-permute-start(bf16[9,4,80,128]{3,2,1,0:T(8,128)(2,1)S(1)} %get-tuple-element.75), channel_id=1, source_target_pairs={{0,1},{1,2},{4,5},{5,6},{8,9},{9,10},{12,13},{13,14},{16,17},{17,1... | collective-permute-start | bytes 2211848 | tf_op jit(solution)/shard_map/ppermute | solution.py:411
  114.8 5.9 %apply_last.3 = (f32[9,4,160,128]{3,2,1,0:T(8,128)S(1)}, bf16[2,4,4,144,128]{4,3,2,1,0:T(8,128)(2,1)S(1)}, bf16[2,4,4,144,128]{4,3,2,1,0:T(8,128)(2,1)}, bf16[9,...) custom-call(f32[9,4,160,128]{3,2,1,0:T(8,128)S(1)} %get-tuple-element.67.refs_5_.refs_0_, ...), custom_call_target="tpu_custom_call" | custom-call | bytes 16220160 | tf_op jit(solution)/shard_map/apply_last/pallas_call | solution.py:292
  120.7 1.6 copy-done.3
  124.2 1.5 collective-permute-start.20
  125.7 2.0 collective-permute-start.22
  127.7 2.4 collective-permute-start.23
  130.2 2.9 %collective-permute-start.18 = (bf16[9,4,80,128]{3,2,1,0:T(8,128)(2,1)}, bf16[9,4,80,128]{3,2,1,0:T(8,128)(2,1)S(1)}, u32[]{:S(2)}, u32[]{:S(2)}) collective-permute-start(bf16[9,4,80,128]{3,2,1,0:T(8,128)(2,1)} %copy-done.16), channel_id=1, source_target_pairs={{0,1},{1,2},{4,5},{5,6},{8,9},{9,10},{12,13},{13,14},{16,17},{17,1... | collective-permute-start | bytes 2211848 | tf_op jit(solution)/shard_map/ppermute | solution.py:411
  133.1 2.1 broadcast_select_fusion
  136.5 2.1 broadcast_select_fusion.3
  138.6 8.5 %collective-permute-start.17 = (bf16[9,4,80,128]{3,2,1,0:T(8,128)(2,1)}, bf16[9,4,80,128]{3,2,1,0:T(8,128)(2,1)}, u32[]{:S(2)}, u32[]{:S(2)}) collective-permute-start(bf16[9,4,80,128]{3,2,1,0:T(8,128)(2,1)} %broadcast_select_fusion.3), channel_id=1, source_target_pairs={{1,2},{2,3},{0,1},{5,6},{6,7},{4,5},{9,10},{10,11},{8,9},{13,14},{... | collective-permute-start | bytes 2211848 | tf_op jit(solution)/shard_map/ppermute | solution.py:411
  147.1 2.1 broadcast_select_fusion.1
  150.6 2.1 broadcast_select_fusion.2
  152.7 4.7 %collective-permute-start.19 = (bf16[9,4,80,128]{3,2,1,0:T(8,128)(2,1)}, bf16[9,4,80,128]{3,2,1,0:T(8,128)(2,1)}, u32[]{:S(2)}, u32[]{:S(2)}) collective-permute-start(bf16[9,4,80,128]{3,2,1,0:T(8,128)(2,1)} %broadcast_select_fusion.2), channel_id=1, source_target_pairs={{1,2},{2,3},{0,1},{5,6},{6,7},{4,5},{9,10},{10,11},{8,9},{13,14},{... | collective-permute-start | bytes 2211848 | tf_op jit(solution)/shard_map/ppermute | solution.py:411
  157.4 7.7 %collective-permute-done.17.refs_6_ = bf16[9,4,80,128]{3,2,1,0:T(8,128)(2,1)} collective-permute-done((bf16[9,4,80,128]{3,2,1,0:T(8,128)(2,1)}, bf16[9,4,80,128]{3,2,1,0:T(8,128)(2,1)}, u32[]{:S(2)}, u32[]{:S(2)}) %collective-permute-start.17) | collective-permute-done | bytes 737312 | tf_op jit(solution)/shard_map/ppermute | solution.py:411
  165.1 1.8 copy-done.1
  166.9 1.8 copy-done.4
  168.8 6.0 %apply_image.2 = (bf16[9,4,80,256]{3,2,1,0:T(8,128)(2,1)S(1)}, bf16[9,4,80,256]{3,2,1,0:T(8,128)(2,1)S(1)}, bf16[9,4,80,256]{3,2,1,0:T(8,128)(2,1)S(1)}) custom-call(s32[1]{0:T(128)} %bitcast.6.refs_0_, f32[9,4,160,128]{3,2,1,0:T(8,128)S(1)} %copy-done.1, bf16[2,4,4,144,128]{4,3,2,1,0:T(8,128)(2,1)} %collective-permute-done.22.refs_2_, ...), custom_call_target="tpu_custom_call" | custom-call | bytes 16220160 | tf_op jit(solution)/shard_map/apply_image/pallas_call | solution.py:292
  177.0 6.4 %apply_image.3 = (bf16[9,4,80,256]{3,2,1,0:T(8,128)(2,1)S(1)}, bf16[9,4,80,256]{3,2,1,0:T(8,128)(2,1)S(1)}, bf16[9,4,80,256]{3,2,1,0:T(8,128)(2,1)S(1)}) custom-call(s32[1]{0:T(128)} %bitcast.6.refs_0_, f32[9,4,160,128]{3,2,1,0:T(8,128)S(1)} %copy-done.5, bf16[2,4,4,144,128]{4,3,2,1,0:T(8,128)(2,1)} %collective-permute-done.22.refs_2_, ...), custom_call_target="tpu_custom_call" | custom-call | bytes 16220160 | tf_op jit(solution)/shard_map/apply_image/pallas_call | solution.py:292
  191.0 1.6 collective-permute-start.26
  194.4 8.3 %gram.3.refs_10_ = f32[2,4,2,64,128]{4,3,2,1,0:T(8,128)} custom-call(s32[8]{0:T(128)} %stack.71.plan, bf16[2880,128]{1,0:T(8,128)(2,1)} %bitcast.84, bf16[2880,128]{1,0:T(8,128)(2,1)} %bitcast.85, bf16[2880,128]{1,0:T(8,128)(2,1)} %bitcast.23.refs_2_, bf16[2880,128]{1,0:T(8,128)(2,1)} %bitcast.24.refs_3_, bf16[2880,128]{1,0:T(8,128)(2,1)} %bitcast.25.refs_4_, ...), custom_call_target="tpu_custom_call" | custom-call | bytes 23592960 | tf_op jit(solution)/shard_map/gram/pallas_call | solution.py:367
  202.8 7.9 %gram.4.refs_2_.refs_8_ = f32[2,4,2,64,128]{4,3,2,1,0:T(8,128)} custom-call(s32[4]{0:T(128)} %pad_add_fusion.plan, bf16[2880,128]{1,0:T(8,128)(2,1)} %bitcast.5.refs_0_, bf16[2880,128]{1,0:T(8,128)(2,1)} %bitcast.7.refs_1_, bf16[2880,128]{1,0:T(8,128)(2,1)} %bitcast.86, bf16[2880,128]{1,0:T(8,128)(2,1)} %bitcast.9.refs_3_, bf16[2880,256]{1,0:T(8,128)(2,1)} %bitcast.67, ...), custom_call_target="tpu_custom_call" | custom-call | bytes 11796480 | tf_op jit(solution)/shard_map/gram/pallas_call | solution.py:367
  211.7 6.1 %unpack.1.refs_9_ = f32[9,128,1152]{2,1,0:T(8,128)} custom-call(f32[9,4,160,128]{3,2,1,0:T(8,128)S(1)} %copy-done.2, f32[9,4,160,128]{3,2,1,0:T(8,128)S(1)} %copy-done.6, f32[2,4,2,64,128]{4,3,2,1,0:T(8,128)S(1)} %copy-done.14), custom_call_target="tpu_custom_call" | custom-call | bytes 21233664 | tf_op jit(solution)/shard_map/unpack/pallas_call | solution.py:133
  217.8 6.0 %collective-permute-done.28 = bf16[9,4,80,128]{3,2,1,0:T(8,128)(2,1)} collective-permute-done((bf16[9,4,80,128]{3,2,1,0:T(8,128)(2,1)S(1)}, bf16[9,4,80,128]{3,2,1,0:T(8,128)(2,1)}, u32[]{:S(2)}, u32[]{:S(2)}) %collective-permute-start.28) | collective-permute-done | bytes 737312 | tf_op jit(solution)/shard_map/ppermute | solution.py:412
  223.9 6.2 %gram.5 = f32[2,4,2,64,128]{4,3,2,1,0:T(8,128)} custom-call(s32[4]{0:T(128)} %pad_add_fusion.1.plan, bf16[2880,128]{1,0:T(8,128)(2,1)} %bitcast.34.refs_0_, bf16[2880,128]{1,0:T(8,128)(2,1)} %bitcast.89, bf16[2880,128]{1,0:T(8,128)(2,1)} %bitcast.36.refs_2_, bf16[2880,128]{1,0:T(8,128)(2,1)} %bitcast.90, bf16[2880,256]{1,0:T(8,128)(2,1)} %bitcast.68, ...), custom_call_target="tpu_custom_call" | custom-call | bytes 11796480 | tf_op jit(solution)/shard_map/gram/pallas_call | solution.py:367
  231.1 1.9 collective-permute-start.30
  235.4 2.4 collective-permute-start.33
  239.7 4.4 %collective-permute-start.34 = (f32[2,64,64]{2,1,0:T(8,128)S(1)}, f32[2,64,64]{2,1,0:T(8,128)S(1)}, u32[]{:S(2)}, u32[]{:S(2)}) collective-permute-start(f32[2,64,64]{2,1,0:T(8,128)S(1)} %get-tuple-element.97), channel_id=1, source_target_pairs={{0,0},{1,8},{2,16},{3,24},{4,4},{5,12},{6,20},{7,28},{8,1},{9,9},{... | collective-permute-start | bytes 98312 | tf_op jit(solution)/shard_map/ppermute | solution.py:462
  244.1 2.1 collective-permute-start.35
  246.2 8.6 %collective-permute-done.35 = f32[2,64,64]{2,1,0:T(8,128)S(1)} collective-permute-done((f32[2,64,64]{2,1,0:T(8,128)S(1)}, f32[2,64,64]{2,1,0:T(8,128)S(1)}, u32[]{:S(2)}, u32[]{:S(2)}) %collective-permute-start.35) | collective-permute-done | bytes 32800 | tf_op jit(solution)/shard_map/ppermute | solution.py:462
  (94 shorter events, 23.6 us)
Async XLA Ops:
  0.6 2.5 copy-start.9
  5.9 15.1 %copy-start.23 = (f32[9,1152]{1,0:T(8,128)S(1)}, f32[9,1152]{1,0:T(8,128)}, u32[]{:S(2)}) copy-start(f32[9,1152]{1,0:T(8,128)} %param.3) | copy-start | bytes 124420
  5.9 17.0 %collective-permute-start = (bf16[4,4,144,128]{3,2,1,0:T(8,128)(2,1)S(1)}, bf16[4,4,144,128]{3,2,1,0:T(8,128)(2,1)S(1)}, u32[]{:S(2)}, u32[]{:S(2)}) collective-permute-start(bf16[4,4,144,128]{3,2,1,0:T(8,128)(2,1)S(1)} %get-tuple-element.47), channel_id=1, source_target_pairs={{0,4},{4,8},{8,12},{12,16},{16,20},{20,24},{24,28},{1,5},{5,9},{9,... | collective-permute-start | bytes 1769480 | tf_op jit(solution)/shard_map/ppermute | solution.py:308
  9.8 18.5 %collective-permute-start.1 = (bf16[4,4,144,128]{3,2,1,0:T(8,128)(2,1)S(1)}, bf16[4,4,144,128]{3,2,1,0:T(8,128)(2,1)S(1)}, u32[]{:S(2)}, u32[]{:S(2)}) collective-permute-start(bf16[4,4,144,128]{3,2,1,0:T(8,128)(2,1)S(1)} %get-tuple-element.48), channel_id=1, source_target_pairs={{4,0},{8,4},{12,8},{16,12},{20,16},{24,20},{28,24},{5,1},{9,5},{13... | collective-permute-start | bytes 1769480 | tf_op jit(solution)/shard_map/ppermute | solution.py:308
  14.5 22.3 %collective-permute-start.4 = (bf16[4,4,144,128]{3,2,1,0:T(8,128)(2,1)S(1)}, bf16[4,4,144,128]{3,2,1,0:T(8,128)(2,1)S(1)}, u32[]{:S(2)}, u32[]{:S(2)}) collective-permute-start(bf16[4,4,144,128]{3,2,1,0:T(8,128)(2,1)S(1)} %get-tuple-element.53), channel_id=1, source_target_pairs={{0,4},{4,8},{8,12},{12,16},{16,20},{20,24},{24,28},{1,5},{5,9},{9,... | collective-permute-start | bytes 1769480 | tf_op jit(solution)/shard_map/ppermute | solution.py:308
  19.1 21.8 %collective-permute-start.5 = (bf16[4,4,144,128]{3,2,1,0:T(8,128)(2,1)S(1)}, bf16[4,4,144,128]{3,2,1,0:T(8,128)(2,1)S(1)}, u32[]{:S(2)}, u32[]{:S(2)}) collective-permute-start(bf16[4,4,144,128]{3,2,1,0:T(8,128)(2,1)S(1)} %get-tuple-element.54), channel_id=1, source_target_pairs={{4,0},{8,4},{12,8},{16,12},{20,16},{24,20},{28,24},{5,1},{9,5},{13... | collective-permute-start | bytes 1769480 | tf_op jit(solution)/shard_map/ppermute | solution.py:308
  32.5 17.0 %collective-permute-start.2 = (bf16[4,4,144,128]{3,2,1,0:T(8,128)(2,1)S(1)}, bf16[4,4,144,128]{3,2,1,0:T(8,128)(2,1)S(1)}, u32[]{:S(2)}, u32[]{:S(2)}) collective-permute-start(bf16[4,4,144,128]{3,2,1,0:T(8,128)(2,1)S(1)} %get-tuple-element.51), channel_id=1, source_target_pairs={{0,4},{4,8},{8,12},{12,16},{16,20},{20,24},{24,28},{1,5},{5,9},{9,... | collective-permute-start | bytes 1769480 | tf_op jit(solution)/shard_map/ppermute | solution.py:308
  34.4 19.1 %collective-permute-start.3 = (bf16[4,4,144,128]{3,2,1,0:T(8,128)(2,1)S(1)}, bf16[4,4,144,128]{3,2,1,0:T(8,128)(2,1)S(1)}, u32[]{:S(2)}, u32[]{:S(2)}) collective-permute-start(bf16[4,4,144,128]{3,2,1,0:T(8,128)(2,1)S(1)} %get-tuple-element.52), channel_id=1, source_target_pairs={{4,0},{8,4},{12,8},{16,12},{20,16},{24,20},{28,24},{5,1},{9,5},{13... | collective-permute-start | bytes 1769480 | tf_op jit(solution)/shard_map/ppermute | solution.py:308
  45.1 17.0 %collective-permute-start.8 = (bf16[4,4,144,128]{3,2,1,0:T(8,128)(2,1)S(1)}, bf16[4,4,144,128]{3,2,1,0:T(8,128)(2,1)S(1)}, u32[]{:S(2)}, u32[]{:S(2)}) collective-permute-start(bf16[4,4,144,128]{3,2,1,0:T(8,128)(2,1)S(1)} %get-tuple-element.59), channel_id=1, source_target_pairs={{0,4},{4,8},{8,12},{12,16},{16,20},{20,24},{24,28},{1,5},{5,9},{9,... | collective-permute-start | bytes 1769480 | tf_op jit(solution)/shard_map/ppermute | solution.py:308
  47.1 19.1 %collective-permute-start.9 = (bf16[4,4,144,128]{3,2,1,0:T(8,128)(2,1)S(1)}, bf16[4,4,144,128]{3,2,1,0:T(8,128)(2,1)S(1)}, u32[]{:S(2)}, u32[]{:S(2)}) collective-permute-start(bf16[4,4,144,128]{3,2,1,0:T(8,128)(2,1)S(1)} %get-tuple-element.60), channel_id=1, source_target_pairs={{4,0},{8,4},{12,8},{16,12},{20,16},{24,20},{28,24},{5,1},{9,5},{13... | collective-permute-start | bytes 1769480 | tf_op jit(solution)/shard_map/ppermute | solution.py:308
  57.8 17.0 %collective-permute-start.6 = (bf16[4,4,144,128]{3,2,1,0:T(8,128)(2,1)S(1)}, bf16[4,4,144,128]{3,2,1,0:T(8,128)(2,1)S(1)}, u32[]{:S(2)}, u32[]{:S(2)}) collective-permute-start(bf16[4,4,144,128]{3,2,1,0:T(8,128)(2,1)S(1)} %get-tuple-element.57), channel_id=1, source_target_pairs={{0,4},{4,8},{8,12},{12,16},{16,20},{20,24},{24,28},{1,5},{5,9},{9,... | collective-permute-start | bytes 1769480 | tf_op jit(solution)/shard_map/ppermute | solution.py:308
  59.8 19.0 %collective-permute-start.7 = (bf16[4,4,144,128]{3,2,1,0:T(8,128)(2,1)S(1)}, bf16[4,4,144,128]{3,2,1,0:T(8,128)(2,1)S(1)}, u32[]{:S(2)}, u32[]{:S(2)}) collective-permute-start(bf16[4,4,144,128]{3,2,1,0:T(8,128)(2,1)S(1)} %get-tuple-element.58), channel_id=1, source_target_pairs={{4,0},{8,4},{12,8},{16,12},{20,16},{24,20},{28,24},{5,1},{9,5},{13... | collective-permute-start | bytes 1769480 | tf_op jit(solution)/shard_map/ppermute | solution.py:308
  70.5 17.0 %collective-permute-start.12 = (bf16[4,4,144,128]{3,2,1,0:T(8,128)(2,1)S(1)}, bf16[4,4,144,128]{3,2,1,0:T(8,128)(2,1)S(1)}, u32[]{:S(2)}, u32[]{:S(2)}) collective-permute-start(bf16[4,4,144,128]{3,2,1,0:T(8,128)(2,1)S(1)} %get-tuple-element.65), channel_id=1, source_target_pairs={{0,4},{4,8},{8,12},{12,16},{16,20},{20,24},{24,28},{1,5},{5,9},{9,... | collective-permute-start | bytes 1769480 | tf_op jit(solution)/shard_map/ppermute | solution.py:308
  72.4 19.0 %collective-permute-start.13 = (bf16[4,4,144,128]{3,2,1,0:T(8,128)(2,1)S(1)}, bf16[4,4,144,128]{3,2,1,0:T(8,128)(2,1)S(1)}, u32[]{:S(2)}, u32[]{:S(2)}) collective-permute-start(bf16[4,4,144,128]{3,2,1,0:T(8,128)(2,1)S(1)} %get-tuple-element.66), channel_id=1, source_target_pairs={{4,0},{8,4},{12,8},{16,12},{20,16},{24,20},{28,24},{5,1},{9,5},{13... | collective-permute-start | bytes 1769480 | tf_op jit(solution)/shard_map/ppermute | solution.py:308
  83.1 17.0 %collective-permute-start.10 = (bf16[4,4,144,128]{3,2,1,0:T(8,128)(2,1)S(1)}, bf16[4,4,144,128]{3,2,1,0:T(8,128)(2,1)S(1)}, u32[]{:S(2)}, u32[]{:S(2)}) collective-permute-start(bf16[4,4,144,128]{3,2,1,0:T(8,128)(2,1)S(1)} %get-tuple-element.63), channel_id=1, source_target_pairs={{0,4},{4,8},{8,12},{12,16},{16,20},{20,24},{24,28},{1,5},{5,9},{9,... | collective-permute-start | bytes 1769480 | tf_op jit(solution)/shard_map/ppermute | solution.py:308
  85.0 19.0 %collective-permute-start.11 = (bf16[4,4,144,128]{3,2,1,0:T(8,128)(2,1)S(1)}, bf16[4,4,144,128]{3,2,1,0:T(8,128)(2,1)S(1)}, u32[]{:S(2)}, u32[]{:S(2)}) collective-permute-start(bf16[4,4,144,128]{3,2,1,0:T(8,128)(2,1)S(1)} %get-tuple-element.64), channel_id=1, source_target_pairs={{4,0},{8,4},{12,8},{16,12},{20,16},{24,20},{28,24},{5,1},{9,5},{13... | collective-permute-start | bytes 1769480 | tf_op jit(solution)/shard_map/ppermute | solution.py:308
  95.8 19.0 %collective-permute-start.14 = (bf16[4,4,144,128]{3,2,1,0:T(8,128)(2,1)S(1)}, bf16[4,4,144,128]{3,2,1,0:T(8,128)(2,1)S(1)}, u32[]{:S(2)}, u32[]{:S(2)}) collective-permute-start(bf16[4,4,144,128]{3,2,1,0:T(8,128)(2,1)S(1)} %get-tuple-element.69), channel_id=1, source_target_pairs={{0,4},{4,8},{8,12},{12,16},{16,20},{20,24},{24,28},{1,5},{5,9},{9,... | collective-permute-start | bytes 1769480 | tf_op jit(solution)/shard_map/ppermute | solution.py:308
  97.7 17.1 %collective-permute-start.15 = (bf16[4,4,144,128]{3,2,1,0:T(8,128)(2,1)S(1)}, bf16[4,4,144,128]{3,2,1,0:T(8,128)(2,1)S(1)}, u32[]{:S(2)}, u32[]{:S(2)}) collective-permute-start(bf16[4,4,144,128]{3,2,1,0:T(8,128)(2,1)S(1)} %get-tuple-element.70), channel_id=1, source_target_pairs={{4,0},{8,4},{12,8},{16,12},{20,16},{24,20},{28,24},{5,1},{9,5},{13... | collective-permute-start | bytes 1769480 | tf_op jit(solution)/shard_map/ppermute | solution.py:308
  109.4 11.3 %copy-start = (f32[9,4,160,128]{3,2,1,0:T(8,128)}, f32[9,4,160,128]{3,2,1,0:T(8,128)S(1)}, u32[]{:S(2)}) copy-start(f32[9,4,160,128]{3,2,1,0:T(8,128)S(1)} %get-tuple-element.68.refs_5_.refs_1_.refs_0_) | copy-start | bytes 8847364
  109.4 23.8 %copy-start.15 = (bf16[9,4,80,128]{3,2,1,0:T(8,128)(2,1)}, bf16[9,4,80,128]{3,2,1,0:T(8,128)(2,1)S(1)}, u32[]{:S(2)}) copy-start(bf16[9,4,80,128]{3,2,1,0:T(8,128)(2,1)S(1)} %get-tuple-element.75) | copy-start | bytes 2211844
  109.4 20.8 %collective-permute-start.24 = (bf16[9,4,80,128]{3,2,1,0:T(8,128)(2,1)}, bf16[9,4,80,128]{3,2,1,0:T(8,128)(2,1)}, u32[]{:S(2)}, u32[]{:S(2)}) collective-permute-start(bf16[9,4,80,128]{3,2,1,0:T(8,128)(2,1)} %get-tuple-element.74), channel_id=1, source_target_pairs={{3,2},{2,1},{7,6},{6,5},{11,10},{10,9},{15,14},{14,13},{19,18},{18... | collective-permute-start | bytes 2211848 | tf_op jit(solution)/shard_map/ppermute | solution.py:412
  111.4 23.8 %collective-permute-start.16 = (bf16[9,4,80,128]{3,2,1,0:T(8,128)(2,1)S(1)}, bf16[9,4,80,128]{3,2,1,0:T(8,128)(2,1)}, u32[]{:S(2)}, u32[]{:S(2)}) collective-permute-start(bf16[9,4,80,128]{3,2,1,0:T(8,128)(2,1)S(1)} %get-tuple-element.75), channel_id=1, source_target_pairs={{0,1},{1,2},{4,5},{5,6},{8,9},{9,10},{12,13},{13,14},{16,17},{17,1... | collective-permute-start | bytes 2211848 | tf_op jit(solution)/shard_map/ppermute | solution.py:411
  120.7 1.6 copy-start.3
  122.2 0.9 copy-start.16
  123.1 1.1 copy-start.19
  124.2 14.4 %collective-permute-start.20 = (bf16[9,4,80,128]{3,2,1,0:T(8,128)(2,1)}, bf16[9,4,80,128]{3,2,1,0:T(8,128)(2,1)}, u32[]{:S(2)}, u32[]{:S(2)}) collective-permute-start(bf16[9,4,80,128]{3,2,1,0:T(8,128)(2,1)} %get-tuple-element.76), channel_id=1, source_target_pairs={{3,2},{2,1},{7,6},{6,5},{11,10},{10,9},{15,14},{14,13},{19,18},{18... | collective-permute-start | bytes 2211848 | tf_op jit(solution)/shard_map/ppermute | solution.py:412
  125.7 27.0 %collective-permute-start.22 = (bf16[2,4,4,144,128]{4,3,2,1,0:T(8,128)(2,1)}, bf16[2,4,4,144,128]{4,3,2,1,0:T(8,128)(2,1)}, u32[]{:S(2)}, u32[]{:S(2)}) collective-permute-start(bf16[2,4,4,144,128]{4,3,2,1,0:T(8,128)(2,1)} %get-tuple-element.78), channel_id=1, source_target_pairs={{0,4},{4,8},{8,12},{12,16},{16,20},{20,24},{24,28},{1,5},{5,9},{9,... | collective-permute-start | bytes 3538952 | tf_op jit(solution)/shard_map/ppermute | solution.py:308
  127.7 19.4 %copy-start.17 = (bf16[9,4,80,128]{3,2,1,0:T(8,128)(2,1)S(1)}, bf16[9,4,80,128]{3,2,1,0:T(8,128)(2,1)}, u32[]{:S(2)}) copy-start(bf16[9,4,80,128]{3,2,1,0:T(8,128)(2,1)} %copy-done.16) | copy-start | bytes 2211844
  127.7 29.6 %collective-permute-start.23 = (bf16[2,4,4,144,128]{4,3,2,1,0:T(8,128)(2,1)}, bf16[2,4,4,144,128]{4,3,2,1,0:T(8,128)(2,1)}, u32[]{:S(2)}, u32[]{:S(2)}) collective-permute-start(bf16[2,4,4,144,128]{4,3,2,1,0:T(8,128)(2,1)} %copy-done.19), channel_id=1, source_target_pairs={{4,0},{8,4},{12,8},{16,12},{20,16},{24,20},{28,24},{5,1},{9,5},{13... | collective-permute-start | bytes 3538952 | tf_op jit(solution)/shard_map/ppermute | solution.py:308
  130.2 19.1 %collective-permute-start.18 = (bf16[9,4,80,128]{3,2,1,0:T(8,128)(2,1)}, bf16[9,4,80,128]{3,2,1,0:T(8,128)(2,1)S(1)}, u32[]{:S(2)}, u32[]{:S(2)}) collective-permute-start(bf16[9,4,80,128]{3,2,1,0:T(8,128)(2,1)} %copy-done.16), channel_id=1, source_target_pairs={{0,1},{1,2},{4,5},{5,6},{8,9},{9,10},{12,13},{13,14},{16,17},{17,1... | collective-permute-start | bytes 2211848 | tf_op jit(solution)/shard_map/ppermute | solution.py:411
  135.2 22.2 %collective-permute-start.25 = (bf16[9,4,80,128]{3,2,1,0:T(8,128)(2,1)}, bf16[9,4,80,128]{3,2,1,0:T(8,128)(2,1)S(1)}, u32[]{:S(2)}, u32[]{:S(2)}) collective-permute-start(bf16[9,4,80,128]{3,2,1,0:T(8,128)(2,1)} %broadcast_select_fusion), channel_id=1, source_target_pairs={{2,1},{1,0},{3,2},{6,5},{5,4},{7,6},{10,9},{9,8},{11,10},{14,13},{... | collective-permute-start | bytes 2211848 | tf_op jit(solution)/shard_map/ppermute | solution.py:412
  138.6 26.5 %collective-permute-start.17 = (bf16[9,4,80,128]{3,2,1,0:T(8,128)(2,1)}, bf16[9,4,80,128]{3,2,1,0:T(8,128)(2,1)}, u32[]{:S(2)}, u32[]{:S(2)}) collective-permute-start(bf16[9,4,80,128]{3,2,1,0:T(8,128)(2,1)} %broadcast_select_fusion.3), channel_id=1, source_target_pairs={{1,2},{2,3},{0,1},{5,6},{6,7},{4,5},{9,10},{10,11},{8,9},{13,14},{... | collective-permute-start | bytes 2211848 | tf_op jit(solution)/shard_map/ppermute | solution.py:411
  149.3 1.3 copy-start.20
  149.3 37.6 %collective-permute-start.21 = (bf16[9,4,80,128]{3,2,1,0:T(8,128)(2,1)}, bf16[9,4,80,128]{3,2,1,0:T(8,128)(2,1)}, u32[]{:S(2)}, u32[]{:S(2)}) collective-permute-start(bf16[9,4,80,128]{3,2,1,0:T(8,128)(2,1)} %broadcast_select_fusion.1), channel_id=1, source_target_pairs={{2,1},{1,0},{3,2},{6,5},{5,4},{7,6},{10,9},{9,8},{11,10},{14,13},{... | collective-permute-start | bytes 2211848 | tf_op jit(solution)/shard_map/ppermute | solution.py:412
  152.7 34.2 %collective-permute-start.19 = (bf16[9,4,80,128]{3,2,1,0:T(8,128)(2,1)}, bf16[9,4,80,128]{3,2,1,0:T(8,128)(2,1)}, u32[]{:S(2)}, u32[]{:S(2)}) collective-permute-start(bf16[9,4,80,128]{3,2,1,0:T(8,128)(2,1)} %broadcast_select_fusion.2), channel_id=1, source_target_pairs={{1,2},{2,3},{0,1},{5,6},{6,7},{4,5},{9,10},{10,11},{8,9},{13,14},{... | collective-permute-start | bytes 2211848 | tf_op jit(solution)/shard_map/ppermute | solution.py:411
  157.4 32.4 %copy-start.18 = (bf16[9,4,80,128]{3,2,1,0:T(8,128)(2,1)}, bf16[9,4,80,128]{3,2,1,0:T(8,128)(2,1)S(1)}, u32[]{:S(2)}) copy-start(bf16[9,4,80,128]{3,2,1,0:T(8,128)(2,1)S(1)} %collective-permute-done.25.refs_7_) | copy-start | bytes 2211844
  165.1 1.8 copy-start.1
  166.9 1.8 copy-start.4
  168.8 8.2 %copy-start.5 = (f32[9,4,160,128]{3,2,1,0:T(8,128)S(1)}, f32[9,4,160,128]{3,2,1,0:T(8,128)}, u32[]{:S(2)}) copy-start(f32[9,4,160,128]{3,2,1,0:T(8,128)} %copy-done.3) | copy-start | bytes 8847364
  174.8 1.1 copy-start.10
  175.9 1.1 copy-start.12
  177.0 6.4 %copy-start.7 = (bf16[9,4,80,256]{3,2,1,0:T(8,128)(2,1)}, bf16[9,4,80,256]{3,2,1,0:T(8,128)(2,1)S(1)}, u32[]{:S(2)}) copy-start(bf16[9,4,80,256]{3,2,1,0:T(8,128)(2,1)S(1)} %get-tuple-element.80.refs_5_) | copy-start | bytes 4423684
  183.4 1.2 copy-start.8
  184.6 1.2 copy-start.11
  185.7 1.2 copy-start.13
  187.7 30.1 %collective-permute-start.27 = (bf16[9,4,80,128]{3,2,1,0:T(8,128)(2,1)}, bf16[9,4,80,128]{3,2,1,0:T(8,128)(2,1)S(1)}, u32[]{:S(2)}, u32[]{:S(2)}) collective-permute-start(bf16[9,4,80,128]{3,2,1,0:T(8,128)(2,1)} %get-tuple-element.82), channel_id=1, source_target_pairs={{2,3},{6,7},{10,11},{14,15},{18,19},{22,23},{26,27},{30,31}} | collective-permute-start | bytes 2211848 | tf_op jit(solution)/shard_map/ppermute | solution.py:411
  188.4 29.4 %collective-permute-start.29 = (bf16[9,4,80,128]{3,2,1,0:T(8,128)(2,1)}, bf16[9,4,80,128]{3,2,1,0:T(8,128)(2,1)S(1)}, u32[]{:S(2)}, u32[]{:S(2)}) collective-permute-start(bf16[9,4,80,128]{3,2,1,0:T(8,128)(2,1)} %get-tuple-element.83), channel_id=1, source_target_pairs={{1,0},{5,4},{9,8},{13,12},{17,16},{21,20},{25,24},{29,28}} | collective-permute-start | bytes 2211848 | tf_op jit(solution)/shard_map/ppermute | solution.py:412
  189.7 34.1 %collective-permute-start.28 = (bf16[9,4,80,128]{3,2,1,0:T(8,128)(2,1)S(1)}, bf16[9,4,80,128]{3,2,1,0:T(8,128)(2,1)}, u32[]{:S(2)}, u32[]{:S(2)}) collective-permute-start(bf16[9,4,80,128]{3,2,1,0:T(8,128)(2,1)S(1)} %collective-permute-done.25.refs_7_), channel_id=1, source_target_pairs={{1,0},{5,4},{9,8},{13,12},{17,16},{21,20},{25,24},{29,28}} | collective-permute-start | bytes 2211848 | tf_op jit(solution)/shard_map/ppermute | solution.py:412
  191.0 32.8 %collective-permute-start.26 = (bf16[9,4,80,128]{3,2,1,0:T(8,128)(2,1)}, bf16[9,4,80,128]{3,2,1,0:T(8,128)(2,1)}, u32[]{:S(2)}, u32[]{:S(2)}) collective-permute-start(bf16[9,4,80,128]{3,2,1,0:T(8,128)(2,1)} %collective-permute-done.17.refs_6_), channel_id=1, source_target_pairs={{2,3},{6,7},{10,11},{14,15},{18,19},{22,23},{26,27},{30,31}} | collective-permute-start | bytes 2211848 | tf_op jit(solution)/shard_map/ppermute | solution.py:411
  202.8 7.9 %copy-start.2 = (f32[9,4,160,128]{3,2,1,0:T(8,128)S(1)}, f32[9,4,160,128]{3,2,1,0:T(8,128)}, u32[]{:S(2)}) copy-start(f32[9,4,160,128]{3,2,1,0:T(8,128)} %copy-done) | copy-start | bytes 8847364
  202.8 7.9 %copy-start.6 = (f32[9,4,160,128]{3,2,1,0:T(8,128)S(1)}, f32[9,4,160,128]{3,2,1,0:T(8,128)}, u32[]{:S(2)}) copy-start(f32[9,4,160,128]{3,2,1,0:T(8,128)} %copy-done.3) | copy-start | bytes 8847364
  210.7 1.0 copy-start.14
  217.8 6.1 %copy-start.21 = (bf16[9,4,80,128]{3,2,1,0:T(8,128)(2,1)}, bf16[9,4,80,128]{3,2,1,0:T(8,128)(2,1)S(1)}, u32[]{:S(2)}) copy-start(bf16[9,4,80,128]{3,2,1,0:T(8,128)(2,1)S(1)} %collective-permute-done.27) | copy-start | bytes 2211844
  217.8 6.1 %copy-start.22 = (bf16[9,4,80,128]{3,2,1,0:T(8,128)(2,1)}, bf16[9,4,80,128]{3,2,1,0:T(8,128)(2,1)S(1)}, u32[]{:S(2)}) copy-start(bf16[9,4,80,128]{3,2,1,0:T(8,128)(2,1)S(1)} %collective-permute-done.29) | copy-start | bytes 2211844
  231.1 3.0 %collective-permute-start.30 = (f32[2,4,64,128]{3,2,1,0:T(8,128)S(1)}, f32[2,4,64,128]{3,2,1,0:T(8,128)S(1)}, u32[]{:S(2)}, u32[]{:S(2)}) collective-permute-start(f32[2,4,64,128]{3,2,1,0:T(8,128)S(1)} %dynamic-slice_bitcast_fusion), channel_id=1, source_target_pairs={{0,4},{4,0},{8,12},{12,8},{16,20},{20,16},{24,28},{28,24},{1,5},{5... | collective-permute-start | bytes 786440 | tf_op jit(solution)/shard_map/ppermute | solution.py:438
  235.1 3.2 %collective-permute-start.31 = (f32[2,64,128]{2,1,0:T(8,128)S(1)}, f32[2,64,128]{2,1,0:T(8,128)S(1)}, u32[]{:S(2)}, u32[]{:S(2)}) collective-permute-start(f32[2,64,128]{2,1,0:T(8,128)S(1)} %get-tuple-element.89), channel_id=1, source_target_pairs={{0,8},{4,12},{8,0},{12,4},{16,24},{20,28},{24,16},{28,20},{1,9},{5... | collective-permute-start | bytes 196616 | tf_op jit(solution)/shard_map/ppermute | solution.py:443
  235.4 3.4 %collective-permute-start.32 = (f32[2,64,128]{2,1,0:T(8,128)S(1)}, f32[2,64,128]{2,1,0:T(8,128)S(1)}, u32[]{:S(2)}, u32[]{:S(2)}) collective-permute-start(f32[2,64,128]{2,1,0:T(8,128)S(1)} %get-tuple-element.91), channel_id=1, source_target_pairs={{0,16},{4,20},{8,24},{12,28},{16,0},{20,4},{24,8},{28,12},{1,17},{... | collective-permute-start | bytes 196616 | tf_op jit(solution)/shard_map/ppermute | solution.py:443
  235.4 4.1 %collective-permute-start.33 = (f32[2,64,128]{2,1,0:T(8,128)S(1)}, f32[2,64,128]{2,1,0:T(8,128)S(1)}, u32[]{:S(2)}, u32[]{:S(2)}) collective-permute-start(f32[2,64,128]{2,1,0:T(8,128)S(1)} %get-tuple-element.90), channel_id=1, source_target_pairs={{0,24},{4,28},{8,16},{12,20},{16,8},{20,12},{24,0},{28,4},{1,25},{... | collective-permute-start | bytes 196616 | tf_op jit(solution)/shard_map/ppermute | solution.py:443
  239.7 6.6 %collective-permute-start.34 = (f32[2,64,64]{2,1,0:T(8,128)S(1)}, f32[2,64,64]{2,1,0:T(8,128)S(1)}, u32[]{:S(2)}, u32[]{:S(2)}) collective-permute-start(f32[2,64,64]{2,1,0:T(8,128)S(1)} %get-tuple-element.97), channel_id=1, source_target_pairs={{0,0},{1,8},{2,16},{3,24},{4,4},{5,12},{6,20},{7,28},{8,1},{9,9},{... | collective-permute-start | bytes 98312 | tf_op jit(solution)/shard_map/ppermute | solution.py:462
  244.1 10.7 %collective-permute-start.35 = (f32[2,64,64]{2,1,0:T(8,128)S(1)}, f32[2,64,64]{2,1,0:T(8,128)S(1)}, u32[]{:S(2)}, u32[]{:S(2)}) collective-permute-start(f32[2,64,64]{2,1,0:T(8,128)S(1)} %get-tuple-element.96), channel_id=1, source_target_pairs={{0,4},{1,12},{2,20},{3,28},{4,0},{5,8},{6,16},{7,24},{8,5},{9,13},... | collective-permute-start | bytes 98312 | tf_op jit(solution)/shard_map/ppermute | solution.py:462

commit v3 on v2

--- a/solution.py
+++ b/solution.py
@@ -16,6 +16,7 @@
 FIRST_B = NZ - PART
 SMALL_LIMIT = 6 << 20
 GRAM_LIMIT = 56 << 20
+LAST_GRAM_LIMIT = 20 << 20
 
 coeffs = (-205.0 / 72.0, 8.0 / 5.0, -1.0 / 5.0, 8.0 / 315.0, -1.0 / 560.0)
 kinetic = -0.5 / 0.09
@@ -308,7 +309,7 @@
     return lax.ppermute(above, "domain", up), lax.ppermute(below, "domain", down)
 
 
-def gram_kernel(kinds, used, chunks, plan, *refs):
+def gram_kernel(kinds, used, chunks, base, plan, *refs):
     count = len(kinds)
     blocks, refs = refs[: count * chunks], refs[count * chunks :]
     rights, refs = refs[: len(used) * chunks], refs[len(used) * chunks :]
@@ -319,7 +320,7 @@
     for i, choices in enumerate(kinds):
         for kind in choices:
 
-            @pl.when(plan[2 * i] == kind)
+            @pl.when(plan[base + 2 * i] == kind)
             def _():
                 mine = blocks[chunks * i : chunks * (i + 1)]
                 turned = jnp.concatenate([block[...].T for block in mine], axis=0)
@@ -341,7 +342,7 @@
         out[...] = sums[...]
         for i in range(count):
 
-            @pl.when(plan[2 * i] < 3)
+            @pl.when(plan[base + 2 * i] < 3)
             def _():
                 for other in range(chunks):
                     top = slice(128 * other, 128 * other + GROUP)
@@ -353,10 +354,10 @@
                             lanes = slice(256 + 128 * m, 256 + 128 * (m + 1))
                             second = pltpu.roll(full[i, top, lanes], GROUP, 1)
                             value = jnp.where(left, value, second + full[i, low, lanes])
-                        out[m, plan[2 * i + 1], other] += value
-
-
-def gram(blocks, kinds, plan, rights, sums, after=()):
+                        out[m, plan[base + 2 * i + 1], other] += value
+
+
+def gram(blocks, kinds, plan, base, rights, sums, limit, after=()):
     chunks = len(rights)
     steps = 3
     flat = [block.reshape(-1, 128) for block in blocks]
@@ -365,7 +366,7 @@
     part = flat[0].shape[0] // steps
     whole = pl.BlockSpec(sums.shape, lambda s: (0,) * sums.ndim)
     return pl.pallas_call(
-        functools.partial(gram_kernel, kinds, used, chunks),
+        functools.partial(gram_kernel, kinds, used, chunks, base),
         grid=(steps,),
         in_specs=[IN_SMEM]
         + [pl.BlockSpec((part, 128), lambda s: (s, 0))] * len(flat)
@@ -375,7 +376,7 @@
         out_specs=whole,
         out_shape=jax.ShapeDtypeStruct(sums.shape, jnp.float32),
         scratch_shapes=[pltpu.VMEM((len(kinds), 128 * chunks, 256 * chunks), jnp.float32)],
-        compiler_params=pltpu.CompilerParams(vmem_limit_bytes=GRAM_LIMIT),
+        compiler_params=pltpu.CompilerParams(vmem_limit_bytes=limit),
         cost_estimate=cost(len(flat) * flat[0].size * 8),
         name="gram",
     )(plan, *flat, *right, sums, *after)
@@ -551,18 +552,22 @@
     late = [0 <= hop - bands // 2 < bands // 2 - 1 for hop in range(1, bands)]
     kinds = [((0, 1), (2, 0)) if behind else ((0,), (2,)) for behind in late]
 
+    plan = [jnp.int32(0), band, jnp.int32(1), band]
+    for one in plans:
+        plan = plan + one
+    plan = jnp.stack(plan).astype(jnp.int32)
+
     def add_products(sums, first, last, after=()):
-        blocks, plan, choice = [], [], []
+        blocks, choice = [], []
         if first == 0:
             blocks = [lows[c][part] for part in range(2) for c in range(chunks)]
             choice = [(0,), (1,)]
-            plan = [jnp.int32(0), band, jnp.int32(1), band]
         for i in range(max(first, 1) - 1, last):
             blocks += [ups[c][i] for c in range(chunks)] + [downs[c][i] for c in range(chunks)]
-            plan = plan + plans[i]
             choice += kinds[i]
-        rows = jnp.stack(plan).astype(jnp.int32)
-        return gram(blocks, tuple(choice), rows, rights, sums, after=after)
+        base = 4 * first
+        limit = LAST_GRAM_LIMIT if last == bands - 1 else GRAM_LIMIT
+        return gram(blocks, tuple(choice), plan, base, rights, sums, limit, after=after)
 
     done = max(bands - 2, 1)
     table = zeros

time: 257 us -> 255 us (level)
  Pallas kernels: 85.2 us -> 82.4 us
    pallas_call x3, Pallas kernels: 22.4 us -> 19.6 us  [gram(): pl.pallas_call(functools.partial(gram_kernel, kinds, used, chunks, base),...]
    unnamed x48 -> x58, local copies, waits for them, and re-layouts: 16.4 us -> 19 us
where the time goes in v3:
time: 255 us; the launch traced here: 253 us
  starting transfers between devices  84.1 us (33%)
  Pallas kernels  82.4 us (32%)
  waiting for transfers between devices  55.7 us (22%)
  local copies, waits for them, and re-layouts  21.5 us (8%)
  other arithmetic  8.48 us (3%)
    pallas_call x10, Pallas kernels, apply_op(): pl.pallas_call(functools.partial(apply_kernel, mode, len(after), bool(ear...  49.2 us
    ppermute x9, waiting for transfers between devices, exchange(): lax.ppermute(below, 'domain', down)  29.3 us
    ppermute x9, starting transfers between devices, exchange(): lax.ppermute(above, 'domain', up)  21.9 us
    ppermute x6, starting transfers between devices, hop_move(): up = lax.ppermute(up, 'band', [(b - 1, b) for b in pairs])  21.7 us
    ppermute x9, starting transfers between devices, exchange(): lax.ppermute(below, 'domain', down)  20.7 us
    pallas_call x3, Pallas kernels, gram(): pl.pallas_call(functools.partial(gram_kernel, kinds, used, chunks, base),...  19.6 us
    unnamed x58, local copies, waits for them, and re-layouts  19 us
    ppermute x6, starting transfers between devices, hop_move(): lax.ppermute(down, 'band', [(bands - b, bands - 1 - b) for b in pairs])  8.69 us
  transfers between devices with their start and end apart: 36, of which 15 were waited for; matrix products, arithmetic and copies ran while one was open for 4% of the time, Pallas kernels for 30%

profile of v3, /device:TPU:3, one launch (start us, length us, event | category | flops | bytes accessed | tf_op | source)
XLA Modules:
  0.0 253.4 jit_solution(11066441367193376383)
XLA Ops:
  0.6 2.5 copy-done.11
  3.1 2.8 %pack.2 = (f32[9,4,160,128]{3,2,1,0:T(8,128)S(1)}, bf16[4,4,144,128]{3,2,1,0:T(8,128)(2,1)S(1)}, bf16[4,4,144,128]{3,2,1,0:T(8,128)(2,1)S(1)}) custom-call(f32[9,128,1152]{2,1,0:T(8,128)S(1)} %bitcast.72), custom_call_target="tpu_custom_call" | custom-call | bytes 10616832 | tf_op jit(solution)/shard_map/pack/pallas_call | solution.py:98
  5.9 3.8 %collective-permute-start = (bf16[4,4,144,128]{3,2,1,0:T(8,128)(2,1)S(1)}, bf16[4,4,144,128]{3,2,1,0:T(8,128)(2,1)S(1)}, u32[]{:S(2)}, u32[]{:S(2)}) collective-permute-start(bf16[4,4,144,128]{3,2,1,0:T(8,128)(2,1)S(1)} %get-tuple-element.47), channel_id=1, source_target_pairs={{0,4},{4,8},{8,12},{12,16},{16,20},{20,24},{24,28},{1,5},{5,9},{9,... | collective-permute-start | bytes 1769480 | tf_op jit(solution)/shard_map/ppermute | solution.py:309
  9.8 1.9 collective-permute-start.1
  11.7 2.8 %pack.3 = (f32[9,4,160,128]{3,2,1,0:T(8,128)S(1)}, bf16[4,4,144,128]{3,2,1,0:T(8,128)(2,1)S(1)}, bf16[4,4,144,128]{3,2,1,0:T(8,128)(2,1)S(1)}) custom-call(f32[9,128,1152]{2,1,0:T(8,128)S(1)} %bitcast.73), custom_call_target="tpu_custom_call" | custom-call | bytes 10616832 | tf_op jit(solution)/shard_map/pack/pallas_call | solution.py:98
  14.5 4.5 %collective-permute-start.4 = (bf16[4,4,144,128]{3,2,1,0:T(8,128)(2,1)S(1)}, bf16[4,4,144,128]{3,2,1,0:T(8,128)(2,1)S(1)}, u32[]{:S(2)}, u32[]{:S(2)}) collective-permute-start(bf16[4,4,144,128]{3,2,1,0:T(8,128)(2,1)S(1)} %get-tuple-element.53), channel_id=1, source_target_pairs={{0,4},{4,8},{8,12},{12,16},{16,20},{20,24},{24,28},{1,5},{5,9},{9,... | collective-permute-start | bytes 1769480 | tf_op jit(solution)/shard_map/ppermute | solution.py:309
  19.1 1.9 collective-permute-start.5
  21.1 1.9 spread.1.refs_3_.refs_4_
  22.9 5.3 %collective-permute-done.1.refs_2_ = bf16[4,4,144,128]{3,2,1,0:T(8,128)(2,1)S(1)} collective-permute-done((bf16[4,4,144,128]{3,2,1,0:T(8,128)(2,1)S(1)}, bf16[4,4,144,128]{3,2,1,0:T(8,128)(2,1)S(1)}, u32[]{:S(2)}, u32[]{:S(2)}) %collective-permute-start.1) | collective-permute-done | bytes 589856 | tf_op jit(solution)/shard_map/ppermute | solution.py:309
  28.2 4.2 %apply_first.2 = (f32[9,4,160,128]{3,2,1,0:T(8,128)S(1)}, bf16[4,4,144,128]{3,2,1,0:T(8,128)(2,1)S(1)}, bf16[4,4,144,128]{3,2,1,0:T(8,128)(2,1)S(1)}) custom-call(f32[9,4,160,128]{3,2,1,0:T(8,128)S(1)} %get-tuple-element.46.refs_0_.refs_1_, bf16[4,4,144,128]{3,2,1,0:T(8,128)(2,1)S(1)} %collective-permute-done.refs_1_, ...), custom_call_target="tpu_custom_call" | custom-call | bytes 16220160 | tf_op jit(solution)/shard_map/apply_first/pallas_call | solution.py:293
  32.5 1.9 collective-permute-start.2
  34.4 2.4 collective-permute-start.3
  36.8 4.0 %collective-permute-done.5.refs_2_ = bf16[4,4,144,128]{3,2,1,0:T(8,128)(2,1)S(1)} collective-permute-done((bf16[4,4,144,128]{3,2,1,0:T(8,128)(2,1)S(1)}, bf16[4,4,144,128]{3,2,1,0:T(8,128)(2,1)S(1)}, u32[]{:S(2)}, u32[]{:S(2)}) %collective-permute-start.5) | collective-permute-done | bytes 589856 | tf_op jit(solution)/shard_map/ppermute | solution.py:309
  40.9 4.2 %apply_first.3 = (f32[9,4,160,128]{3,2,1,0:T(8,128)S(1)}, bf16[4,4,144,128]{3,2,1,0:T(8,128)(2,1)S(1)}, bf16[4,4,144,128]{3,2,1,0:T(8,128)(2,1)S(1)}) custom-call(f32[9,4,160,128]{3,2,1,0:T(8,128)S(1)} %get-tuple-element.49.refs_4_.refs_0_.refs_1_, bf16[4,4,144,128]{3,2,1,0:T(8,128)(2,1)S(1)} %collective-permute-done.4.refs_1_, ...), custom_call_target="tpu_custom_call" | custom-call | bytes 16220160 | tf_op jit(solution)/shard_map/apply_first/pallas_call | solution.py:293
  45.1 1.9 collective-permute-start.8
  47.1 2.4 collective-permute-start.9
  49.5 4.0 %collective-permute-done.3.refs_3_ = bf16[4,4,144,128]{3,2,1,0:T(8,128)(2,1)S(1)} collective-permute-done((bf16[4,4,144,128]{3,2,1,0:T(8,128)(2,1)S(1)}, bf16[4,4,144,128]{3,2,1,0:T(8,128)(2,1)S(1)}, u32[]{:S(2)}, u32[]{:S(2)}) %collective-permute-start.3) | collective-permute-done | bytes 589856 | tf_op jit(solution)/shard_map/ppermute | solution.py:309
  53.5 4.3 %apply_middle.4 = (f32[9,4,160,128]{3,2,1,0:T(8,128)S(1)}, bf16[4,4,144,128]{3,2,1,0:T(8,128)(2,1)S(1)}, bf16[4,4,144,128]{3,2,1,0:T(8,128)(2,1)S(1)}) custom-call(f32[9,4,160,128]{3,2,1,0:T(8,128)S(1)} %get-tuple-element.50.refs_4_.refs_0_.refs_1_, f32[9,4,160,128]{3,2,1,0:T(8,128)S(1)} %get-tuple-element.46.refs_0_.refs_1_, ...), custom_call_target="tpu_custom_call" | custom-call | bytes 16220160 | tf_op jit(solution)/shard_map/apply_middle/pallas_call | solution.py:293
  57.8 1.9 collective-permute-start.6
  59.8 2.4 collective-permute-start.7
  62.2 4.0 %collective-permute-done.9.refs_3_ = bf16[4,4,144,128]{3,2,1,0:T(8,128)(2,1)S(1)} collective-permute-done((bf16[4,4,144,128]{3,2,1,0:T(8,128)(2,1)S(1)}, bf16[4,4,144,128]{3,2,1,0:T(8,128)(2,1)S(1)}, u32[]{:S(2)}, u32[]{:S(2)}) %collective-permute-start.9) | collective-permute-done | bytes 589856 | tf_op jit(solution)/shard_map/ppermute | solution.py:309
  66.2 4.3 %apply_middle.5 = (f32[9,4,160,128]{3,2,1,0:T(8,128)S(1)}, bf16[4,4,144,128]{3,2,1,0:T(8,128)(2,1)S(1)}, bf16[4,4,144,128]{3,2,1,0:T(8,128)(2,1)S(1)}) custom-call(f32[9,4,160,128]{3,2,1,0:T(8,128)S(1)} %get-tuple-element.55.refs_5_.refs_0_.refs_1_, f32[9,4,160,128]{3,2,1,0:T(8,128)S(1)} %get-tuple-element.49.refs_4_.refs_0_.refs_1_, ...), custom_call_target="tpu_custom_call" | custom-call | bytes 16220160 | tf_op jit(solution)/shard_map/apply_middle/pallas_call | solution.py:293
  70.5 1.9 collective-permute-start.12
  72.4 2.4 collective-permute-start.13
  74.8 4.0 %collective-permute-done.7.refs_3_ = bf16[4,4,144,128]{3,2,1,0:T(8,128)(2,1)S(1)} collective-permute-done((bf16[4,4,144,128]{3,2,1,0:T(8,128)(2,1)S(1)}, bf16[4,4,144,128]{3,2,1,0:T(8,128)(2,1)S(1)}, u32[]{:S(2)}, u32[]{:S(2)}) %collective-permute-start.7) | collective-permute-done | bytes 589856 | tf_op jit(solution)/shard_map/ppermute | solution.py:309
  78.8 4.3 %apply_middle.6 = (f32[9,4,160,128]{3,2,1,0:T(8,128)S(1)}, bf16[4,4,144,128]{3,2,1,0:T(8,128)(2,1)S(1)}, bf16[4,4,144,128]{3,2,1,0:T(8,128)(2,1)S(1)}) custom-call(f32[9,4,160,128]{3,2,1,0:T(8,128)S(1)} %get-tuple-element.56.refs_5_.refs_0_.refs_1_, f32[9,4,160,128]{3,2,1,0:T(8,128)S(1)} %get-tuple-element.50.refs_4_.refs_0_.refs_1_, ...), custom_call_target="tpu_custom_call" | custom-call | bytes 16220160 | tf_op jit(solution)/shard_map/apply_middle/pallas_call | solution.py:293
  83.1 1.9 collective-permute-start.10
  85.0 2.4 collective-permute-start.11
  87.5 4.0 %collective-permute-done.13.refs_3_ = bf16[4,4,144,128]{3,2,1,0:T(8,128)(2,1)S(1)} collective-permute-done((bf16[4,4,144,128]{3,2,1,0:T(8,128)(2,1)S(1)}, bf16[4,4,144,128]{3,2,1,0:T(8,128)(2,1)S(1)}, u32[]{:S(2)}, u32[]{:S(2)}) %collective-permute-start.13) | collective-permute-done | bytes 589856 | tf_op jit(solution)/shard_map/ppermute | solution.py:309
  91.4 4.3 %apply_middle.7 = (f32[9,4,160,128]{3,2,1,0:T(8,128)S(1)}, bf16[4,4,144,128]{3,2,1,0:T(8,128)(2,1)S(1)}, bf16[4,4,144,128]{3,2,1,0:T(8,128)(2,1)S(1)}) custom-call(f32[9,4,160,128]{3,2,1,0:T(8,128)S(1)} %get-tuple-element.61.refs_5_.refs_0_.refs_1_, f32[9,4,160,128]{3,2,1,0:T(8,128)S(1)} %get-tuple-element.55.refs_5_.refs_0_.refs_1_, ...), custom_call_target="tpu_custom_call" | custom-call | bytes 16220160 | tf_op jit(solution)/shard_map/apply_middle/pallas_call | solution.py:293
  95.8 1.9 collective-permute-start.14
  97.7 2.4 collective-permute-start.15
  100.1 4.0 %collective-permute-done.11.refs_3_ = bf16[4,4,144,128]{3,2,1,0:T(8,128)(2,1)S(1)} collective-permute-done((bf16[4,4,144,128]{3,2,1,0:T(8,128)(2,1)S(1)}, bf16[4,4,144,128]{3,2,1,0:T(8,128)(2,1)S(1)}, u32[]{:S(2)}, u32[]{:S(2)}) %collective-permute-start.11) | collective-permute-done | bytes 589856 | tf_op jit(solution)/shard_map/ppermute | solution.py:309
  104.1 5.3 %apply_last.2 = (f32[9,4,160,128]{3,2,1,0:T(8,128)S(1)}, bf16[4,4,144,128]{3,2,1,0:T(8,128)(2,1)S(1)}, bf16[4,4,144,128]{3,2,1,0:T(8,128)(2,1)S(1)}, bf16[9,4,80...) custom-call(f32[9,4,160,128]{3,2,1,0:T(8,128)S(1)} %get-tuple-element.62.refs_5_.refs_0_, ...), custom_call_target="tpu_custom_call" | custom-call | bytes 16220160 | tf_op jit(solution)/shard_map/apply_last/pallas_call | solution.py:293
  109.4 2.0 collective-permute-start.24
  111.4 3.4 %collective-permute-start.16 = (bf16[9,4,80,128]{3,2,1,0:T(8,128)(2,1)S(1)}, bf16[9,4,80,128]{3,2,1,0:T(8,128)(2,1)}, u32[]{:S(2)}, u32[]{:S(2)}) collective-permute-start(bf16[9,4,80,128]{3,2,1,0:T(8,128)(2,1)S(1)} %get-tuple-element.75), channel_id=1, source_target_pairs={{0,1},{1,2},{4,5},{5,6},{8,9},{9,10},{12,13},{13,14},{16,17},{17,1... | collective-permute-start | bytes 2211848 | tf_op jit(solution)/shard_map/ppermute | solution.py:412
  114.8 5.9 %apply_last.3 = (f32[9,4,160,128]{3,2,1,0:T(8,128)S(1)}, bf16[2,4,4,144,128]{4,3,2,1,0:T(8,128)(2,1)S(1)}, bf16[2,4,4,144,128]{4,3,2,1,0:T(8,128)(2,1)}, bf16[9,...) custom-call(f32[9,4,160,128]{3,2,1,0:T(8,128)S(1)} %get-tuple-element.67.refs_5_.refs_0_, ...), custom_call_target="tpu_custom_call" | custom-call | bytes 16220160 | tf_op jit(solution)/shard_map/apply_last/pallas_call | solution.py:293
  120.7 1.5 copy-done.3
  125.7 2.0 collective-permute-start.22
  127.7 2.4 collective-permute-start.23
  130.2 2.9 %collective-permute-start.18 = (bf16[9,4,80,128]{3,2,1,0:T(8,128)(2,1)}, bf16[9,4,80,128]{3,2,1,0:T(8,128)(2,1)S(1)}, u32[]{:S(2)}, u32[]{:S(2)}) collective-permute-start(bf16[9,4,80,128]{3,2,1,0:T(8,128)(2,1)} %copy-done.22), channel_id=1, source_target_pairs={{0,1},{1,2},{4,5},{5,6},{8,9},{9,10},{12,13},{13,14},{16,17},{17,1... | collective-permute-start | bytes 2211848 | tf_op jit(solution)/shard_map/ppermute | solution.py:412
  133.2 2.1 broadcast_select_fusion
  136.5 2.1 broadcast_select_fusion.3
  138.6 8.5 %collective-permute-start.17 = (bf16[9,4,80,128]{3,2,1,0:T(8,128)(2,1)}, bf16[9,4,80,128]{3,2,1,0:T(8,128)(2,1)}, u32[]{:S(2)}, u32[]{:S(2)}) collective-permute-start(bf16[9,4,80,128]{3,2,1,0:T(8,128)(2,1)} %broadcast_select_fusion.3), channel_id=1, source_target_pairs={{1,2},{2,3},{0,1},{5,6},{6,7},{4,5},{9,10},{10,11},{8,9},{13,14},{... | collective-permute-start | bytes 2211848 | tf_op jit(solution)/shard_map/ppermute | solution.py:412
  147.1 2.1 broadcast_select_fusion.1
  150.6 2.1 broadcast_select_fusion.2
  152.7 4.7 %collective-permute-start.19 = (bf16[9,4,80,128]{3,2,1,0:T(8,128)(2,1)}, bf16[9,4,80,128]{3,2,1,0:T(8,128)(2,1)}, u32[]{:S(2)}, u32[]{:S(2)}) collective-permute-start(bf16[9,4,80,128]{3,2,1,0:T(8,128)(2,1)} %broadcast_select_fusion.2), channel_id=1, source_target_pairs={{1,2},{2,3},{0,1},{5,6},{6,7},{4,5},{9,10},{10,11},{8,9},{13,14},{... | collective-permute-start | bytes 2211848 | tf_op jit(solution)/shard_map/ppermute | solution.py:412
  157.4 7.7 %collective-permute-done.17.refs_6_ = bf16[9,4,80,128]{3,2,1,0:T(8,128)(2,1)} collective-permute-done((bf16[9,4,80,128]{3,2,1,0:T(8,128)(2,1)}, bf16[9,4,80,128]{3,2,1,0:T(8,128)(2,1)}, u32[]{:S(2)}, u32[]{:S(2)}) %collective-permute-start.17) | collective-permute-done | bytes 737312 | tf_op jit(solution)/shard_map/ppermute | solution.py:412
  165.1 1.8 copy-done.1
  166.9 1.8 copy-done.4
  168.8 6.0 %apply_image.2 = (bf16[9,4,80,256]{3,2,1,0:T(8,128)(2,1)S(1)}, bf16[9,4,80,256]{3,2,1,0:T(8,128)(2,1)S(1)}, bf16[9,4,80,256]{3,2,1,0:T(8,128)(2,1)S(1)}) custom-call(s32[1]{0:T(128)} %bitcast.15.refs_0_, f32[9,4,160,128]{3,2,1,0:T(8,128)S(1)} %copy-done.1, bf16[2,4,4,144,128]{4,3,2,1,0:T(8,128)(2,1)} %collective-permute-done.22.refs_2_, ...), custom_call_target="tpu_custom_call" | custom-call | bytes 16220160 | tf_op jit(solution)/shard_map/apply_image/pallas_call | solution.py:293
  177.0 6.4 %apply_image.3 = (bf16[9,4,80,256]{3,2,1,0:T(8,128)(2,1)S(1)}, bf16[9,4,80,256]{3,2,1,0:T(8,128)(2,1)S(1)}, bf16[9,4,80,256]{3,2,1,0:T(8,128)(2,1)S(1)}) custom-call(s32[1]{0:T(128)} %bitcast.15.refs_0_, f32[9,4,160,128]{3,2,1,0:T(8,128)S(1)} %copy-done.5, bf16[2,4,4,144,128]{4,3,2,1,0:T(8,128)(2,1)} %collective-permute-done.22.refs_2_, ...), custom_call_target="tpu_custom_call" | custom-call | bytes 16220160 | tf_op jit(solution)/shard_map/apply_image/pallas_call | solution.py:293
  191.1 1.5 collective-permute-start.26
  193.3 8.3 %gram.3.refs_10_ = f32[2,4,2,64,128]{4,3,2,1,0:T(8,128)} custom-call(s32[16]{0:T(128)} %stack.68.plan, bf16[2880,128]{1,0:T(8,128)(2,1)} %bitcast.85, bf16[2880,128]{1,0:T(8,128)(2,1)} %bitcast.86, bf16[2880,128]{1,0:T(8,128)(2,1)} %bitcast.27.refs_2_, bf16[2880,128]{1,0:T(8,128)(2,1)} %bitcast.28.refs_3_, bf16[2880,128]{1,0:T(8,128)(2,1)} %bitcast.29.refs_4_, ...), custom_call_target="tpu_custom_call" | custom-call | bytes 23592960 | tf_op jit(solution)/shard_map/gram/pallas_call | solution.py:368
  201.7 7.9 %gram.4.refs_2_.refs_8_ = f32[2,4,2,64,128]{4,3,2,1,0:T(8,128)} custom-call(s32[16]{0:T(128)} %stack.68.plan, bf16[2880,128]{1,0:T(8,128)(2,1)} %bitcast.14.refs_0_, bf16[2880,128]{1,0:T(8,128)(2,1)} %bitcast.16.refs_1_, bf16[2880,128]{1,0:T(8,128)(2,1)} %bitcast.87, bf16[2880,128]{1,0:T(8,128)(2,1)} %bitcast.18.refs_3_, bf16[2880,256]{1,0:T(8,128)(2,1)} %bitcast.67, ...), custom_call_target="tpu_custom_call" | custom-call | bytes 11796480 | tf_op jit(solution)/shard_map/gram/pallas_call | solution.py:368
  210.6 6.1 %unpack.1.refs_9_ = f32[9,128,1152]{2,1,0:T(8,128)} custom-call(f32[9,4,160,128]{3,2,1,0:T(8,128)S(1)} %copy-done.2, f32[9,4,160,128]{3,2,1,0:T(8,128)S(1)} %copy-done.6, f32[2,4,2,64,128]{4,3,2,1,0:T(8,128)S(1)} %copy-done.19), custom_call_target="tpu_custom_call" | custom-call | bytes 21233664 | tf_op jit(solution)/shard_map/unpack/pallas_call | solution.py:134
  216.7 7.1 %collective-permute-done.28 = bf16[9,4,80,128]{3,2,1,0:T(8,128)(2,1)} collective-permute-done((bf16[9,4,80,128]{3,2,1,0:T(8,128)(2,1)S(1)}, bf16[9,4,80,128]{3,2,1,0:T(8,128)(2,1)}, u32[]{:S(2)}, u32[]{:S(2)}) %collective-permute-start.28) | collective-permute-done | bytes 737312 | tf_op jit(solution)/shard_map/ppermute | solution.py:413
  224.0 2.5 copy-done.12
  226.5 3.4 %gram.5 = f32[2,4,2,64,128]{4,3,2,1,0:T(8,128)S(1)} custom-call(s32[16]{0:T(128)S(1)} %copy-done.25, bf16[2880,128]{1,0:T(8,128)(2,1)} %bitcast.34.refs_0_, bf16[2880,128]{1,0:T(8,128)(2,1)S(1)} %bitcast.88, bf16[2880,128]{1,0:T(8,128)(2,1)} %bitcast.36.refs_2_, bf16[2880,128]{1,0:T(8,128)(2,1)S(1)} %bitcast.89, bf16[2880,256]{1,0:T(8,128)(2,1)S(1)} %bitcast.68, ...), custom_call_target="tpu_custom_call" | custom-call | bytes 11796480 | tf_op jit(solution)/shard_map/gram/pallas_call | solution.py:368
  229.9 1.9 collective-permute-start.30
  233.2 2.5 collective-permute-start.33
  237.5 2.2 collective-permute-start.34
  239.8 4.3 %collective-permute-start.35 = (f32[2,64,64]{2,1,0:T(8,128)S(1)}, f32[2,64,64]{2,1,0:T(8,128)S(1)}, u32[]{:S(2)}, u32[]{:S(2)}) collective-permute-start(f32[2,64,64]{2,1,0:T(8,128)S(1)} %get-tuple-element.96), channel_id=1, source_target_pairs={{0,4},{1,12},{2,20},{3,28},{4,0},{5,8},{6,16},{7,24},{8,5},{9,13},... | collective-permute-start | bytes 98312 | tf_op jit(solution)/shard_map/ppermute | solution.py:463
  244.1 8.4 %collective-permute-done.35 = f32[2,64,64]{2,1,0:T(8,128)S(1)} collective-permute-done((f32[2,64,64]{2,1,0:T(8,128)S(1)}, f32[2,64,64]{2,1,0:T(8,128)S(1)}, u32[]{:S(2)}, u32[]{:S(2)}) %collective-permute-start.35) | collective-permute-done | bytes 32800 | tf_op jit(solution)/shard_map/ppermute | solution.py:463
  (102 shorter events, 22.2 us)
Async XLA Ops:
  0.6 2.5 copy-start.11
  5.9 15.1 %copy-start.28 = (f32[9,1152]{1,0:T(8,128)S(1)}, f32[9,1152]{1,0:T(8,128)}, u32[]{:S(2)}) copy-start(f32[9,1152]{1,0:T(8,128)} %param.3) | copy-start | bytes 124420
  5.9 17.0 %collective-permute-start = (bf16[4,4,144,128]{3,2,1,0:T(8,128)(2,1)S(1)}, bf16[4,4,144,128]{3,2,1,0:T(8,128)(2,1)S(1)}, u32[]{:S(2)}, u32[]{:S(2)}) collective-permute-start(bf16[4,4,144,128]{3,2,1,0:T(8,128)(2,1)S(1)} %get-tuple-element.47), channel_id=1, source_target_pairs={{0,4},{4,8},{8,12},{12,16},{16,20},{20,24},{24,28},{1,5},{5,9},{9,... | collective-permute-start | bytes 1769480 | tf_op jit(solution)/shard_map/ppermute | solution.py:309
  9.8 18.5 %collective-permute-start.1 = (bf16[4,4,144,128]{3,2,1,0:T(8,128)(2,1)S(1)}, bf16[4,4,144,128]{3,2,1,0:T(8,128)(2,1)S(1)}, u32[]{:S(2)}, u32[]{:S(2)}) collective-permute-start(bf16[4,4,144,128]{3,2,1,0:T(8,128)(2,1)S(1)} %get-tuple-element.48), channel_id=1, source_target_pairs={{4,0},{8,4},{12,8},{16,12},{20,16},{24,20},{28,24},{5,1},{9,5},{13... | collective-permute-start | bytes 1769480 | tf_op jit(solution)/shard_map/ppermute | solution.py:309
  14.5 22.3 %collective-permute-start.4 = (bf16[4,4,144,128]{3,2,1,0:T(8,128)(2,1)S(1)}, bf16[4,4,144,128]{3,2,1,0:T(8,128)(2,1)S(1)}, u32[]{:S(2)}, u32[]{:S(2)}) collective-permute-start(bf16[4,4,144,128]{3,2,1,0:T(8,128)(2,1)S(1)} %get-tuple-element.53), channel_id=1, source_target_pairs={{0,4},{4,8},{8,12},{12,16},{16,20},{20,24},{24,28},{1,5},{5,9},{9,... | collective-permute-start | bytes 1769480 | tf_op jit(solution)/shard_map/ppermute | solution.py:309
  19.1 21.8 %collective-permute-start.5 = (bf16[4,4,144,128]{3,2,1,0:T(8,128)(2,1)S(1)}, bf16[4,4,144,128]{3,2,1,0:T(8,128)(2,1)S(1)}, u32[]{:S(2)}, u32[]{:S(2)}) collective-permute-start(bf16[4,4,144,128]{3,2,1,0:T(8,128)(2,1)S(1)} %get-tuple-element.54), channel_id=1, source_target_pairs={{4,0},{8,4},{12,8},{16,12},{20,16},{24,20},{28,24},{5,1},{9,5},{13... | collective-permute-start | bytes 1769480 | tf_op jit(solution)/shard_map/ppermute | solution.py:309
  32.5 17.0 %collective-permute-start.2 = (bf16[4,4,144,128]{3,2,1,0:T(8,128)(2,1)S(1)}, bf16[4,4,144,128]{3,2,1,0:T(8,128)(2,1)S(1)}, u32[]{:S(2)}, u32[]{:S(2)}) collective-permute-start(bf16[4,4,144,128]{3,2,1,0:T(8,128)(2,1)S(1)} %get-tuple-element.51), channel_id=1, source_target_pairs={{0,4},{4,8},{8,12},{12,16},{16,20},{20,24},{24,28},{1,5},{5,9},{9,... | collective-permute-start | bytes 1769480 | tf_op jit(solution)/shard_map/ppermute | solution.py:309
  34.4 19.1 %collective-permute-start.3 = (bf16[4,4,144,128]{3,2,1,0:T(8,128)(2,1)S(1)}, bf16[4,4,144,128]{3,2,1,0:T(8,128)(2,1)S(1)}, u32[]{:S(2)}, u32[]{:S(2)}) collective-permute-start(bf16[4,4,144,128]{3,2,1,0:T(8,128)(2,1)S(1)} %get-tuple-element.52), channel_id=1, source_target_pairs={{4,0},{8,4},{12,8},{16,12},{20,16},{24,20},{28,24},{5,1},{9,5},{13... | collective-permute-start | bytes 1769480 | tf_op jit(solution)/shard_map/ppermute | solution.py:309
  45.1 17.0 %collective-permute-start.8 = (bf16[4,4,144,128]{3,2,1,0:T(8,128)(2,1)S(1)}, bf16[4,4,144,128]{3,2,1,0:T(8,128)(2,1)S(1)}, u32[]{:S(2)}, u32[]{:S(2)}) collective-permute-start(bf16[4,4,144,128]{3,2,1,0:T(8,128)(2,1)S(1)} %get-tuple-element.59), channel_id=1, source_target_pairs={{0,4},{4,8},{8,12},{12,16},{16,20},{20,24},{24,28},{1,5},{5,9},{9,... | collective-permute-start | bytes 1769480 | tf_op jit(solution)/shard_map/ppermute | solution.py:309
  47.1 19.1 %collective-permute-start.9 = (bf16[4,4,144,128]{3,2,1,0:T(8,128)(2,1)S(1)}, bf16[4,4,144,128]{3,2,1,0:T(8,128)(2,1)S(1)}, u32[]{:S(2)}, u32[]{:S(2)}) collective-permute-start(bf16[4,4,144,128]{3,2,1,0:T(8,128)(2,1)S(1)} %get-tuple-element.60), channel_id=1, source_target_pairs={{4,0},{8,4},{12,8},{16,12},{20,16},{24,20},{28,24},{5,1},{9,5},{13... | collective-permute-start | bytes 1769480 | tf_op jit(solution)/shard_map/ppermute | solution.py:309
  57.8 17.0 %collective-permute-start.6 = (bf16[4,4,144,128]{3,2,1,0:T(8,128)(2,1)S(1)}, bf16[4,4,144,128]{3,2,1,0:T(8,128)(2,1)S(1)}, u32[]{:S(2)}, u32[]{:S(2)}) collective-permute-start(bf16[4,4,144,128]{3,2,1,0:T(8,128)(2,1)S(1)} %get-tuple-element.57), channel_id=1, source_target_pairs={{0,4},{4,8},{8,12},{12,16},{16,20},{20,24},{24,28},{1,5},{5,9},{9,... | collective-permute-start | bytes 1769480 | tf_op jit(solution)/shard_map/ppermute | solution.py:309
  59.8 19.0 %collective-permute-start.7 = (bf16[4,4,144,128]{3,2,1,0:T(8,128)(2,1)S(1)}, bf16[4,4,144,128]{3,2,1,0:T(8,128)(2,1)S(1)}, u32[]{:S(2)}, u32[]{:S(2)}) collective-permute-start(bf16[4,4,144,128]{3,2,1,0:T(8,128)(2,1)S(1)} %get-tuple-element.58), channel_id=1, source_target_pairs={{4,0},{8,4},{12,8},{16,12},{20,16},{24,20},{28,24},{5,1},{9,5},{13... | collective-permute-start | bytes 1769480 | tf_op jit(solution)/shard_map/ppermute | solution.py:309
  70.5 17.0 %collective-permute-start.12 = (bf16[4,4,144,128]{3,2,1,0:T(8,128)(2,1)S(1)}, bf16[4,4,144,128]{3,2,1,0:T(8,128)(2,1)S(1)}, u32[]{:S(2)}, u32[]{:S(2)}) collective-permute-start(bf16[4,4,144,128]{3,2,1,0:T(8,128)(2,1)S(1)} %get-tuple-element.65), channel_id=1, source_target_pairs={{0,4},{4,8},{8,12},{12,16},{16,20},{20,24},{24,28},{1,5},{5,9},{9,... | collective-permute-start | bytes 1769480 | tf_op jit(solution)/shard_map/ppermute | solution.py:309
  72.4 19.0 %collective-permute-start.13 = (bf16[4,4,144,128]{3,2,1,0:T(8,128)(2,1)S(1)}, bf16[4,4,144,128]{3,2,1,0:T(8,128)(2,1)S(1)}, u32[]{:S(2)}, u32[]{:S(2)}) collective-permute-start(bf16[4,4,144,128]{3,2,1,0:T(8,128)(2,1)S(1)} %get-tuple-element.66), channel_id=1, source_target_pairs={{4,0},{8,4},{12,8},{16,12},{20,16},{24,20},{28,24},{5,1},{9,5},{13... | collective-permute-start | bytes 1769480 | tf_op jit(solution)/shard_map/ppermute | solution.py:309
  83.1 17.0 %collective-permute-start.10 = (bf16[4,4,144,128]{3,2,1,0:T(8,128)(2,1)S(1)}, bf16[4,4,144,128]{3,2,1,0:T(8,128)(2,1)S(1)}, u32[]{:S(2)}, u32[]{:S(2)}) collective-permute-start(bf16[4,4,144,128]{3,2,1,0:T(8,128)(2,1)S(1)} %get-tuple-element.63), channel_id=1, source_target_pairs={{0,4},{4,8},{8,12},{12,16},{16,20},{20,24},{24,28},{1,5},{5,9},{9,... | collective-permute-start | bytes 1769480 | tf_op jit(solution)/shard_map/ppermute | solution.py:309
  85.0 19.0 %collective-permute-start.11 = (bf16[4,4,144,128]{3,2,1,0:T(8,128)(2,1)S(1)}, bf16[4,4,144,128]{3,2,1,0:T(8,128)(2,1)S(1)}, u32[]{:S(2)}, u32[]{:S(2)}) collective-permute-start(bf16[4,4,144,128]{3,2,1,0:T(8,128)(2,1)S(1)} %get-tuple-element.64), channel_id=1, source_target_pairs={{4,0},{8,4},{12,8},{16,12},{20,16},{24,20},{28,24},{5,1},{9,5},{13... | collective-permute-start | bytes 1769480 | tf_op jit(solution)/shard_map/ppermute | solution.py:309
  95.8 19.0 %collective-permute-start.14 = (bf16[4,4,144,128]{3,2,1,0:T(8,128)(2,1)S(1)}, bf16[4,4,144,128]{3,2,1,0:T(8,128)(2,1)S(1)}, u32[]{:S(2)}, u32[]{:S(2)}) collective-permute-start(bf16[4,4,144,128]{3,2,1,0:T(8,128)(2,1)S(1)} %get-tuple-element.69), channel_id=1, source_target_pairs={{0,4},{4,8},{8,12},{12,16},{16,20},{20,24},{24,28},{1,5},{5,9},{9,... | collective-permute-start | bytes 1769480 | tf_op jit(solution)/shard_map/ppermute | solution.py:309
  97.7 17.1 %collective-permute-start.15 = (bf16[4,4,144,128]{3,2,1,0:T(8,128)(2,1)S(1)}, bf16[4,4,144,128]{3,2,1,0:T(8,128)(2,1)S(1)}, u32[]{:S(2)}, u32[]{:S(2)}) collective-permute-start(bf16[4,4,144,128]{3,2,1,0:T(8,128)(2,1)S(1)} %get-tuple-element.70), channel_id=1, source_target_pairs={{4,0},{8,4},{12,8},{16,12},{20,16},{24,20},{28,24},{5,1},{9,5},{13... | collective-permute-start | bytes 1769480 | tf_op jit(solution)/shard_map/ppermute | solution.py:309
  109.4 11.3 %copy-start = (f32[9,4,160,128]{3,2,1,0:T(8,128)}, f32[9,4,160,128]{3,2,1,0:T(8,128)S(1)}, u32[]{:S(2)}) copy-start(f32[9,4,160,128]{3,2,1,0:T(8,128)S(1)} %get-tuple-element.68.refs_5_.refs_1_.refs_0_) | copy-start | bytes 8847364
  109.4 23.8 %copy-start.21 = (bf16[9,4,80,128]{3,2,1,0:T(8,128)(2,1)}, bf16[9,4,80,128]{3,2,1,0:T(8,128)(2,1)S(1)}, u32[]{:S(2)}) copy-start(bf16[9,4,80,128]{3,2,1,0:T(8,128)(2,1)S(1)} %get-tuple-element.75) | copy-start | bytes 2211844
  109.4 20.8 %collective-permute-start.24 = (bf16[9,4,80,128]{3,2,1,0:T(8,128)(2,1)}, bf16[9,4,80,128]{3,2,1,0:T(8,128)(2,1)}, u32[]{:S(2)}, u32[]{:S(2)}) collective-permute-start(bf16[9,4,80,128]{3,2,1,0:T(8,128)(2,1)} %get-tuple-element.74), channel_id=1, source_target_pairs={{3,2},{2,1},{7,6},{6,5},{11,10},{10,9},{15,14},{14,13},{19,18},{18... | collective-permute-start | bytes 2211848 | tf_op jit(solution)/shard_map/ppermute | solution.py:413
  111.4 23.8 %collective-permute-start.16 = (bf16[9,4,80,128]{3,2,1,0:T(8,128)(2,1)S(1)}, bf16[9,4,80,128]{3,2,1,0:T(8,128)(2,1)}, u32[]{:S(2)}, u32[]{:S(2)}) collective-permute-start(bf16[9,4,80,128]{3,2,1,0:T(8,128)(2,1)S(1)} %get-tuple-element.75), channel_id=1, source_target_pairs={{0,1},{1,2},{4,5},{5,6},{8,9},{9,10},{12,13},{13,14},{16,17},{17,1... | collective-permute-start | bytes 2211848 | tf_op jit(solution)/shard_map/ppermute | solution.py:412
  120.7 1.6 copy-start.3
  123.1 1.1 copy-start.26
  124.2 14.4 %collective-permute-start.20 = (bf16[9,4,80,128]{3,2,1,0:T(8,128)(2,1)}, bf16[9,4,80,128]{3,2,1,0:T(8,128)(2,1)}, u32[]{:S(2)}, u32[]{:S(2)}) collective-permute-start(bf16[9,4,80,128]{3,2,1,0:T(8,128)(2,1)} %get-tuple-element.76), channel_id=1, source_target_pairs={{3,2},{2,1},{7,6},{6,5},{11,10},{10,9},{15,14},{14,13},{19,18},{18... | collective-permute-start | bytes 2211848 | tf_op jit(solution)/shard_map/ppermute | solution.py:413
  125.7 27.0 %collective-permute-start.22 = (bf16[2,4,4,144,128]{4,3,2,1,0:T(8,128)(2,1)}, bf16[2,4,4,144,128]{4,3,2,1,0:T(8,128)(2,1)}, u32[]{:S(2)}, u32[]{:S(2)}) collective-permute-start(bf16[2,4,4,144,128]{4,3,2,1,0:T(8,128)(2,1)} %get-tuple-element.78), channel_id=1, source_target_pairs={{0,4},{4,8},{8,12},{12,16},{16,20},{20,24},{24,28},{1,5},{5,9},{9,... | collective-permute-start | bytes 3538952 | tf_op jit(solution)/shard_map/ppermute | solution.py:309
  127.7 19.3 %copy-start.23 = (bf16[9,4,80,128]{3,2,1,0:T(8,128)(2,1)S(1)}, bf16[9,4,80,128]{3,2,1,0:T(8,128)(2,1)}, u32[]{:S(2)}) copy-start(bf16[9,4,80,128]{3,2,1,0:T(8,128)(2,1)} %copy-done.22) | copy-start | bytes 2211844
  127.7 29.6 %collective-permute-start.23 = (bf16[2,4,4,144,128]{4,3,2,1,0:T(8,128)(2,1)}, bf16[2,4,4,144,128]{4,3,2,1,0:T(8,128)(2,1)}, u32[]{:S(2)}, u32[]{:S(2)}) collective-permute-start(bf16[2,4,4,144,128]{4,3,2,1,0:T(8,128)(2,1)} %copy-done.26), channel_id=1, source_target_pairs={{4,0},{8,4},{12,8},{16,12},{20,16},{24,20},{28,24},{5,1},{9,5},{13... | collective-permute-start | bytes 3538952 | tf_op jit(solution)/shard_map/ppermute | solution.py:309
  130.2 19.1 %collective-permute-start.18 = (bf16[9,4,80,128]{3,2,1,0:T(8,128)(2,1)}, bf16[9,4,80,128]{3,2,1,0:T(8,128)(2,1)S(1)}, u32[]{:S(2)}, u32[]{:S(2)}) collective-permute-start(bf16[9,4,80,128]{3,2,1,0:T(8,128)(2,1)} %copy-done.22), channel_id=1, source_target_pairs={{0,1},{1,2},{4,5},{5,6},{8,9},{9,10},{12,13},{13,14},{16,17},{17,1... | collective-permute-start | bytes 2211848 | tf_op jit(solution)/shard_map/ppermute | solution.py:412
  135.2 22.1 %collective-permute-start.25 = (bf16[9,4,80,128]{3,2,1,0:T(8,128)(2,1)}, bf16[9,4,80,128]{3,2,1,0:T(8,128)(2,1)S(1)}, u32[]{:S(2)}, u32[]{:S(2)}) collective-permute-start(bf16[9,4,80,128]{3,2,1,0:T(8,128)(2,1)} %broadcast_select_fusion), channel_id=1, source_target_pairs={{2,1},{1,0},{3,2},{6,5},{5,4},{7,6},{10,9},{9,8},{11,10},{14,13},{... | collective-permute-start | bytes 2211848 | tf_op jit(solution)/shard_map/ppermute | solution.py:413
  138.6 26.5 %collective-permute-start.17 = (bf16[9,4,80,128]{3,2,1,0:T(8,128)(2,1)}, bf16[9,4,80,128]{3,2,1,0:T(8,128)(2,1)}, u32[]{:S(2)}, u32[]{:S(2)}) collective-permute-start(bf16[9,4,80,128]{3,2,1,0:T(8,128)(2,1)} %broadcast_select_fusion.3), channel_id=1, source_target_pairs={{1,2},{2,3},{0,1},{5,6},{6,7},{4,5},{9,10},{10,11},{8,9},{13,14},{... | collective-permute-start | bytes 2211848 | tf_op jit(solution)/shard_map/ppermute | solution.py:412
  149.3 1.3 copy-start.27
  149.3 37.6 %collective-permute-start.21 = (bf16[9,4,80,128]{3,2,1,0:T(8,128)(2,1)}, bf16[9,4,80,128]{3,2,1,0:T(8,128)(2,1)}, u32[]{:S(2)}, u32[]{:S(2)}) collective-permute-start(bf16[9,4,80,128]{3,2,1,0:T(8,128)(2,1)} %broadcast_select_fusion.1), channel_id=1, source_target_pairs={{2,1},{1,0},{3,2},{6,5},{5,4},{7,6},{10,9},{9,8},{11,10},{14,13},{... | collective-permute-start | bytes 2211848 | tf_op jit(solution)/shard_map/ppermute | solution.py:413
  152.7 34.2 %collective-permute-start.19 = (bf16[9,4,80,128]{3,2,1,0:T(8,128)(2,1)}, bf16[9,4,80,128]{3,2,1,0:T(8,128)(2,1)}, u32[]{:S(2)}, u32[]{:S(2)}) collective-permute-start(bf16[9,4,80,128]{3,2,1,0:T(8,128)(2,1)} %broadcast_select_fusion.2), channel_id=1, source_target_pairs={{1,2},{2,3},{0,1},{5,6},{6,7},{4,5},{9,10},{10,11},{8,9},{13,14},{... | collective-permute-start | bytes 2211848 | tf_op jit(solution)/shard_map/ppermute | solution.py:412
  157.4 32.4 %copy-start.24 = (bf16[9,4,80,128]{3,2,1,0:T(8,128)(2,1)}, bf16[9,4,80,128]{3,2,1,0:T(8,128)(2,1)S(1)}, u32[]{:S(2)}) copy-start(bf16[9,4,80,128]{3,2,1,0:T(8,128)(2,1)S(1)} %collective-permute-done.25.refs_7_) | copy-start | bytes 2211844
  165.1 1.8 copy-start.1
  166.9 1.8 copy-start.4
  168.8 8.3 %copy-start.5 = (f32[9,4,160,128]{3,2,1,0:T(8,128)S(1)}, f32[9,4,160,128]{3,2,1,0:T(8,128)}, u32[]{:S(2)}) copy-start(f32[9,4,160,128]{3,2,1,0:T(8,128)} %copy-done.3) | copy-start | bytes 8847364
  174.8 1.1 copy-start.13
  175.9 1.1 copy-start.17
  177.0 6.4 %copy-start.7 = (bf16[9,4,80,256]{3,2,1,0:T(8,128)(2,1)}, bf16[9,4,80,256]{3,2,1,0:T(8,128)(2,1)S(1)}, u32[]{:S(2)}) copy-start(bf16[9,4,80,256]{3,2,1,0:T(8,128)(2,1)S(1)} %get-tuple-element.80.refs_5_) | copy-start | bytes 4423684
  183.4 1.2 copy-start.9
  184.6 1.2 copy-start.15
  185.8 1.2 copy-start.18
  187.8 29.0 %collective-permute-start.27 = (bf16[9,4,80,128]{3,2,1,0:T(8,128)(2,1)}, bf16[9,4,80,128]{3,2,1,0:T(8,128)(2,1)S(1)}, u32[]{:S(2)}, u32[]{:S(2)}) collective-permute-start(bf16[9,4,80,128]{3,2,1,0:T(8,128)(2,1)} %get-tuple-element.82), channel_id=1, source_target_pairs={{2,3},{6,7},{10,11},{14,15},{18,19},{22,23},{26,27},{30,31}} | collective-permute-start | bytes 2211848 | tf_op jit(solution)/shard_map/ppermute | solution.py:412
  188.5 28.3 %collective-permute-start.29 = (bf16[9,4,80,128]{3,2,1,0:T(8,128)(2,1)}, bf16[9,4,80,128]{3,2,1,0:T(8,128)(2,1)S(1)}, u32[]{:S(2)}, u32[]{:S(2)}) collective-permute-start(bf16[9,4,80,128]{3,2,1,0:T(8,128)(2,1)} %get-tuple-element.83), channel_id=1, source_target_pairs={{1,0},{5,4},{9,8},{13,12},{17,16},{21,20},{25,24},{29,28}} | collective-permute-start | bytes 2211848 | tf_op jit(solution)/shard_map/ppermute | solution.py:413
  189.8 34.1 %collective-permute-start.28 = (bf16[9,4,80,128]{3,2,1,0:T(8,128)(2,1)S(1)}, bf16[9,4,80,128]{3,2,1,0:T(8,128)(2,1)}, u32[]{:S(2)}, u32[]{:S(2)}) collective-permute-start(bf16[9,4,80,128]{3,2,1,0:T(8,128)(2,1)S(1)} %collective-permute-done.25.refs_7_), channel_id=1, source_target_pairs={{1,0},{5,4},{9,8},{13,12},{17,16},{21,20},{25,24},{29,28}} | collective-permute-start | bytes 2211848 | tf_op jit(solution)/shard_map/ppermute | solution.py:413
  191.1 32.8 %collective-permute-start.26 = (bf16[9,4,80,128]{3,2,1,0:T(8,128)(2,1)}, bf16[9,4,80,128]{3,2,1,0:T(8,128)(2,1)}, u32[]{:S(2)}, u32[]{:S(2)}) collective-permute-start(bf16[9,4,80,128]{3,2,1,0:T(8,128)(2,1)} %collective-permute-done.17.refs_6_), channel_id=1, source_target_pairs={{2,3},{6,7},{10,11},{14,15},{18,19},{22,23},{26,27},{30,31}} | collective-permute-start | bytes 2211848 | tf_op jit(solution)/shard_map/ppermute | solution.py:412
  201.7 7.9 %copy-start.2 = (f32[9,4,160,128]{3,2,1,0:T(8,128)S(1)}, f32[9,4,160,128]{3,2,1,0:T(8,128)}, u32[]{:S(2)}) copy-start(f32[9,4,160,128]{3,2,1,0:T(8,128)} %copy-done) | copy-start | bytes 8847364
  201.7 7.9 %copy-start.6 = (f32[9,4,160,128]{3,2,1,0:T(8,128)S(1)}, f32[9,4,160,128]{3,2,1,0:T(8,128)}, u32[]{:S(2)}) copy-start(f32[9,4,160,128]{3,2,1,0:T(8,128)} %copy-done.3) | copy-start | bytes 8847364
  209.6 1.0 copy-start.19
  210.6 13.3 %copy-start.8 = (bf16[9,4,80,256]{3,2,1,0:T(8,128)(2,1)S(1)}, bf16[9,4,80,256]{3,2,1,0:T(8,128)(2,1)}, u32[]{:S(2)}) copy-start(bf16[9,4,80,256]{3,2,1,0:T(8,128)(2,1)} %copy-done.7) | copy-start | bytes 4423684
  210.6 13.3 %copy-start.10 = (bf16[9,4,80,256]{3,2,1,0:T(8,128)(2,1)S(1)}, bf16[9,4,80,256]{3,2,1,0:T(8,128)(2,1)}, u32[]{:S(2)}) copy-start(bf16[9,4,80,256]{3,2,1,0:T(8,128)(2,1)} %copy-done.9) | copy-start | bytes 4423684
  210.6 13.3 %copy-start.14 = (bf16[9,4,80,256]{3,2,1,0:T(8,128)(2,1)S(1)}, bf16[9,4,80,256]{3,2,1,0:T(8,128)(2,1)}, u32[]{:S(2)}) copy-start(bf16[9,4,80,256]{3,2,1,0:T(8,128)(2,1)} %copy-done.13) | copy-start | bytes 4423684
  210.6 13.3 %copy-start.16 = (bf16[9,4,80,256]{3,2,1,0:T(8,128)(2,1)S(1)}, bf16[9,4,80,256]{3,2,1,0:T(8,128)(2,1)}, u32[]{:S(2)}) copy-start(bf16[9,4,80,256]{3,2,1,0:T(8,128)(2,1)} %copy-done.15) | copy-start | bytes 4423684
  210.6 13.3 %copy-start.20 = (f32[2,4,2,64,128]{4,3,2,1,0:T(8,128)S(1)}, f32[2,4,2,64,128]{4,3,2,1,0:T(8,128)}, u32[]{:S(2)}) copy-start(f32[2,4,2,64,128]{4,3,2,1,0:T(8,128)} %gram.4.refs_2_.refs_8_) | copy-start | bytes 1572868
  210.6 13.3 %copy-start.25 = (s32[16]{0:T(128)S(1)}, s32[16]{0:T(128)}, u32[]{:S(2)}) copy-start(s32[16]{0:T(128)} %stack.68.plan) | copy-start | bytes 196
  223.9 2.5 copy-start.12
  229.9 3.0 %collective-permute-start.30 = (f32[2,4,64,128]{3,2,1,0:T(8,128)S(1)}, f32[2,4,64,128]{3,2,1,0:T(8,128)S(1)}, u32[]{:S(2)}, u32[]{:S(2)}) collective-permute-start(f32[2,4,64,128]{3,2,1,0:T(8,128)S(1)} %dynamic-slice_bitcast_fusion), channel_id=1, source_target_pairs={{0,4},{4,0},{8,12},{12,8},{16,20},{20,16},{24,28},{28,24},{1,5},{5... | collective-permute-start | bytes 786440 | tf_op jit(solution)/shard_map/ppermute | solution.py:439
  233.0 3.2 %collective-permute-start.31 = (f32[2,64,128]{2,1,0:T(8,128)S(1)}, f32[2,64,128]{2,1,0:T(8,128)S(1)}, u32[]{:S(2)}, u32[]{:S(2)}) collective-permute-start(f32[2,64,128]{2,1,0:T(8,128)S(1)} %get-tuple-element.89), channel_id=1, source_target_pairs={{0,8},{4,12},{8,0},{12,4},{16,24},{20,28},{24,16},{28,20},{1,9},{5... | collective-permute-start | bytes 196616 | tf_op jit(solution)/shard_map/ppermute | solution.py:444
  233.2 3.4 %collective-permute-start.32 = (f32[2,64,128]{2,1,0:T(8,128)S(1)}, f32[2,64,128]{2,1,0:T(8,128)S(1)}, u32[]{:S(2)}, u32[]{:S(2)}) collective-permute-start(f32[2,64,128]{2,1,0:T(8,128)S(1)} %get-tuple-element.91), channel_id=1, source_target_pairs={{0,16},{4,20},{8,24},{12,28},{16,0},{20,4},{24,8},{28,12},{1,17},{... | collective-permute-start | bytes 196616 | tf_op jit(solution)/shard_map/ppermute | solution.py:444
  233.2 4.2 %collective-permute-start.33 = (f32[2,64,128]{2,1,0:T(8,128)S(1)}, f32[2,64,128]{2,1,0:T(8,128)S(1)}, u32[]{:S(2)}, u32[]{:S(2)}) collective-permute-start(f32[2,64,128]{2,1,0:T(8,128)S(1)} %get-tuple-element.90), channel_id=1, source_target_pairs={{0,24},{4,28},{8,16},{12,20},{16,8},{20,12},{24,0},{28,4},{1,25},{... | collective-permute-start | bytes 196616 | tf_op jit(solution)/shard_map/ppermute | solution.py:444
  237.5 6.6 %collective-permute-start.34 = (f32[2,64,64]{2,1,0:T(8,128)S(1)}, f32[2,64,64]{2,1,0:T(8,128)S(1)}, u32[]{:S(2)}, u32[]{:S(2)}) collective-permute-start(f32[2,64,64]{2,1,0:T(8,128)S(1)} %get-tuple-element.97), channel_id=1, source_target_pairs={{0,0},{1,8},{2,16},{3,24},{4,4},{5,12},{6,20},{7,28},{8,1},{9,9},{... | collective-permute-start | bytes 98312 | tf_op jit(solution)/shard_map/ppermute | solution.py:463
  239.8 12.7 %collective-permute-start.35 = (f32[2,64,64]{2,1,0:T(8,128)S(1)}, f32[2,64,64]{2,1,0:T(8,128)S(1)}, u32[]{:S(2)}, u32[]{:S(2)}) collective-permute-start(f32[2,64,64]{2,1,0:T(8,128)S(1)} %get-tuple-element.96), channel_id=1, source_target_pairs={{0,4},{1,12},{2,20},{3,28},{4,0},{5,8},{6,16},{7,24},{8,5},{9,13},... | collective-permute-start | bytes 98312 | tf_op jit(solution)/shard_map/ppermute | solution.py:463
  (1 other events, 0.9 us)
